TPU v7x, 256 devices: a whole 4x4x8 slice. The times are simulated.
256 devices in a mesh: row: 8 (over y, core), goal: 32 (over x, z).
Axes of the slice: x: 4, y: 4, z: 8, core: 2. Of those that a mesh axis runs over, the one named last changes fastest.
Arguments:
- phi: bfloat16 [16384, 512], P(('row', 'goal')), may hold values from -100 to 100
- psi: bfloat16 [32768, 512], P(('row', 'goal')), may hold values from -10 to 10
- positives: int32 [16384], P(('row', 'goal')), may hold values from 0 to 32767, as said below
Outputs:
- grad_phi: float32 [16384, 512], P(('row', 'goal'))
- grad_psi: float32 [32768, 512], P(('row', 'goal'))
- loss: float32 [], replicated
Inputs may be any that keep to these rules, and one draw needn't show every extreme that they name: `positives`: goal index of each state-action row's positive pair.
All inputs are finite; a program needn't handle non-finite values.
Results may differ from a plain program's by a relative error of at most 0.0055.
Values may be sent and summed in bfloat16 or wider, within the bound.
No kernel may reach another device: no remote copies, remote signals or barrier semaphores. Data moves between devices by JAX's collectives and lax.ppermute only.
A program may use at most 64 MiB of HBM per device.

v0:
```python
import math

import jax
import jax.numpy as jnp
from jax import lax
from jax.sharding import PartitionSpec as P


def product_t(left, right):
    return lax.dot_general(
        left, right, (((1,), (1,)), ((), ())), preferred_element_type=jnp.float32
    )


def product_tn(left, right):
    return lax.dot_general(
        left, right, (((0,), (0,)), ((), ())), preferred_element_type=jnp.float32
    )


def shards(phi, psi, positives):
    rows_all, pos_all = (
        lax.all_gather(phi, "goal", axis=0, tiled=True),
        lax.all_gather(positives, "goal", axis=0, tiled=True),
    )
    goals = lax.all_gather(psi, "row", axis=0, tiled=True)
    nrow = rows_all.shape[0]
    ncol = goals.shape[0]
    width = phi.shape[1]
    shard_rows = phi.shape[0]
    shard_goals = psi.shape[0]
    scale = 1.0 / math.sqrt(width)
    ngoal = lax.axis_size("goal")
    goal_index = lax.axis_index("goal")
    local = jnp.arange(ncol, dtype=jnp.int32)
    colid = (local // shard_goals * ngoal + goal_index) * shard_goals + local % shard_goals
    block = min(256, nrow)
    nblock = nrow // block
    row_blocks = rows_all.reshape(nblock, block, width)
    pos_blocks = pos_all.reshape(nblock, block)

    def logits_of(rows):
        return product_t(rows, goals) * scale

    def hits_of(pos):
        return pos[:, None] == colid[None, :]

    def peak_step(carry, item):
        col_max, col_count = carry
        rows, pos = item
        logits = logits_of(rows)
        col_max = jnp.maximum(col_max, jnp.max(logits, axis=0))
        col_count = col_count + jnp.sum(hits_of(pos).astype(jnp.float32), axis=0)
        return ((col_max, col_count), jnp.max(logits, axis=1))

    start = (jnp.full((ncol,), -1e30, jnp.float32), jnp.zeros((ncol,), jnp.float32))
    (col_max, col_count), row_max = lax.scan(peak_step, start, (row_blocks, pos_blocks))
    row_max = lax.pmax(row_max.reshape(nrow), "goal")
    col_max = lax.pmax(col_max, "row")

    def total_step(col_sum, item):
        rows, peak = item
        logits = logits_of(rows)
        col_sum = col_sum + jnp.sum(jnp.exp(logits - col_max[None, :]), axis=0)
        return (col_sum, jnp.sum(jnp.exp(logits - peak[:, None]), axis=1))

    col_sum, row_sum = lax.scan(
        total_step, jnp.zeros((ncol,), jnp.float32), (row_blocks, row_max.reshape(nblock, block))
    )
    row_sum = lax.psum(row_sum.reshape(nrow), "goal")
    col_sum, counts = lax.psum((col_sum, col_count), "row")
    row_lse = row_max + jnp.log(row_sum)
    col_lse = col_max + jnp.log(col_sum)
    lse_blocks = row_lse.reshape(nblock, block)

    def weights_of(rows, pos, lse):
        logits = logits_of(rows)
        hit = hits_of(pos)
        prob = jnp.exp(logits - lse[:, None]) + counts[None, :] * jnp.exp(logits - col_lse[None, :])
        weights = ((prob - 2.0 * hit.astype(jnp.float32)) * scale).astype(jnp.bfloat16)
        part = jnp.sum(jnp.where(hit, col_lse[None, :] - 2.0 * logits, 0.0))
        return (weights, part)

    start = (jnp.zeros((ncol, width), jnp.float32), jnp.zeros((), jnp.float32))

    def both_step(carry, item):
        rows, pos, lse = item
        weights, part = weights_of(rows, pos, lse)
        grad_rows = jnp.dot(weights, goals, preferred_element_type=jnp.float32)
        return ((carry[0] + product_tn(weights, rows), carry[1] + part), grad_rows)

    (grad_goals, part), grad_rows = lax.scan(both_step, start, (row_blocks, pos_blocks, lse_blocks))
    grad_phi = lax.psum_scatter(
        grad_rows.reshape(nrow, width), "goal", scatter_dimension=0, tiled=True
    )
    grad_psi = lax.psum_scatter(grad_goals, "row", scatter_dimension=0, tiled=True)
    own_lse = lax.dynamic_slice_in_dim(row_lse, goal_index * shard_rows, shard_rows, 0)
    total = lax.psum(jnp.sum(own_lse) + part, ("row", "goal"))
    loss = total / (nrow * lax.axis_size("row"))
    return (grad_phi, grad_psi, loss)


def solution(mesh):
    return jax.shard_map(
        shards,
        mesh=mesh,
        in_specs=(P(("row", "goal"), None), P(("row", "goal"), None), P(("row", "goal"))),
        out_specs=(P(("row", "goal"), None), P(("row", "goal"), None), P()),
        check_vma=False,
    )
```

profile of v0, /device:TPU:8, one launch (start us, length us, event | category | flops | bytes accessed | tf_op | source)
XLA Modules:
  0.0 639.5 jit_solution(1696523186058808433)
XLA Ops:
  7.2 0.7 all-gather.5.cloned.1.call-update
  7.9 0.7 all-gather.3.cloned.1.call-update
  8.8 1.3 dynamic-slice
  10.7 0.9 dynamic-update-slice
  11.6 23.8 %all-reduce = s32[2048]{0:T(1024)S(1)} all-reduce(s32[2048]{0:T(1024)S(1)} %dynamic-update-slice), channel_id=1, replica_groups=mesh['row'=8,'goal'=32] {'goal'}, use_global_device_ids=true, to_apply=%add | all-reduce | flops 2048 | bytes 16384
  35.4 1.8 all-gather.5.cloned.1.call-done
  37.2 81.9 %all-gather.3.cloned.1.call-done = bf16[2048,512]{1,0:T(8,128)(2,1)} async-done(((bf16[64,512]{1,0:T(8,128)(2,1)}), bf16[2048,512]{1,0:T(8,128)(2,1)}) %all-gather.3.cloned.1.call-update) | async-done | bytes 2097168 | tf_op jit(solution)/shard_map/all_gather | solution.py:23
  119.1 17.2 %while.45 = (s32[]{:T(128)}, f32[1024]{0:T(1024)S(1)}, f32[1024]{0:T(1024)S(1)}, f32[8,256]{1,0:T(8,128)S(1)}, bf16[8,256,512]{2,1,0:T(8,128)(2,1)}, /*index=5*/...) while((s32[]{:T(128)}, f32[1024]{0:T(1024)S(1)}, ...), condition=%wide.region_4.5_spmd.clone, body=%wide.region_0.4_spmd.clone.sunk | while | flops 270026496 | bytes 1357959 | solution.py:57
  119.1 0.2 convert_reduce_fusion.2
  119.3 1.9 fusion.65
  121.3 0.2 convert_reduce_fusion.2
  121.4 1.9 fusion.65
  123.4 0.2 convert_reduce_fusion.2
  123.6 1.9 fusion.65
  125.6 0.2 convert_reduce_fusion.2
  125.7 1.9 fusion.65
  127.7 0.2 convert_reduce_fusion.2
  127.9 1.9 fusion.65
  130.1 1.9 fusion.65
  132.2 1.9 fusion.65
  134.4 1.9 fusion.65
  136.3 73.1 %pmax.14 = f32[2048]{0:T(1024)S(1)} all-reduce(f32[2048]{0:T(1024)S(1)} %bitcast.78), channel_id=1, replica_groups=mesh['row'=8,'goal'=32] {'goal'}, use_global_device_ids=true, to_apply=%region_5.6 | all-reduce | flops 2048 | bytes 16384 | tf_op jit(solution)/shard_map/pmax | solution.py:58
  209.5 10.0 %pmax.15 = f32[1024]{0:T(1024)S(1)} all-reduce(f32[1024]{0:T(1024)S(1)} %get-tuple-element.225), channel_id=1, replica_groups=mesh['row'=8,'goal'=32] {'row'}, use_global_device_ids=true, to_apply=%region_6.7 | all-reduce | flops 1024 | bytes 8192 | tf_op jit(solution)/shard_map/pmax | solution.py:59
  219.5 16.7 %while.46 = (s32[]{:T(128)}, f32[1024]{0:T(1024)S(1)}, f32[8,256]{1,0:T(8,128)S(1)}, bf16[8,256,512]{2,1,0:T(8,128)(2,1)}, bf16[1024,512]{1,0:T(8,128)(2,1)}, /*...) while((s32[]{:T(128)}, f32[1024]{0:T(1024)S(1)}, ...), condition=%wide.region_10.11_spmd.clone, body=%wide.region_7.10_spmd.clone.sunk | while | flops 269746944 | bytes 1337467 | solution.py:67
  219.6 2.0 exponential_reduce_fusion.3
  221.6 2.0 exponential_reduce_fusion.3
  223.7 2.0 exponential_reduce_fusion.3
  225.8 2.0 exponential_reduce_fusion.3
  227.9 2.0 exponential_reduce_fusion.3
  230.0 2.0 exponential_reduce_fusion.3
  232.1 2.0 exponential_reduce_fusion.3
  234.1 2.0 exponential_reduce_fusion.3
  236.2 70.6 %psum.28 = f32[2048]{0:T(1024)S(1)} all-reduce(f32[2048]{0:T(1024)S(1)} %bitcast.79), channel_id=1, replica_groups=mesh['row'=8,'goal'=32] {'goal'}, use_global_device_ids=true, to_apply=%region_11.12 | all-reduce | flops 2048 | bytes 16384 | tf_op jit(solution)/shard_map/psum | solution.py:70
  306.9 12.0 %all-reduce.1 = (f32[1024]{0:T(1024)S(1)}, f32[1024]{0:T(1024)S(1)}) all-reduce(f32[1024]{0:T(1024)S(1)} %get-tuple-element.227, f32[1024]{0:T(1024)S(1)} %get-tuple-element.228), channel_id=1, replica_groups=mesh['row'=8,'goal'=32] {'row'}, use_global_device_ids=true, to_apply=%region_12.13 | all-reduce | flops 2048 | bytes 16384 | tf_op jit(solution)/shard_map/psum | solution.py:71
  318.9 55.2 %while.47 = (s32[]{:T(128)}, f32[1024,512]{1,0:T(8,128)S(1)}, f32[]{:T(128)}, f32[8,256,512]{2,1,0:T(8,128)}, bf16[8,256,512]{2,1,0:T(8,128)(2,1)}, /*index=5*/b...) while((s32[]{:T(128)}, f32[1024,512]{1,0:T(8,128)S(1)}, ...), condition=%wide.region_16.17_spmd.clone, body=%wide.region_14.16_spmd.clone.sunk | while | flops 812924928 | bytes 14726355 | solution.py:92
  319.0 2.5 fusion.73
  322.1 2.2 select_add_fusion.8
  324.3 1.5 fusion.74
  325.9 2.5 fusion.73
  329.0 2.2 select_add_fusion.8
  331.2 1.6 fusion.74
  332.8 2.5 fusion.73
  335.9 2.2 select_add_fusion.8
  338.1 1.6 fusion.74
  339.7 2.5 fusion.73
  342.8 2.2 select_add_fusion.8
  345.0 1.6 fusion.74
  346.6 2.5 fusion.73
  349.7 2.2 select_add_fusion.8
  351.9 1.5 fusion.74
  353.4 2.5 fusion.73
  356.6 2.2 select_add_fusion.8
  358.7 1.6 fusion.74
  360.3 2.5 fusion.73
  363.5 2.2 select_add_fusion.8
  365.6 1.5 fusion.74
  367.2 2.5 fusion.73
  370.4 2.2 select_add_fusion.8
  372.5 1.6 fusion.74
  374.1 1.3 copy-done
  375.5 0.5 reduce-scatter.3.cloned.1.call-update
  376.0 0.7 dynamic-slice_reduce_fusion
  377.4 75.5 %psum.31 = f32[]{:T(128)} all-reduce(f32[]{:T(128)S(6)} %add.83), channel_id=1, replica_groups=mesh['row'=8,'goal'=32] {'row','goal'}, use_global_device_ids=true, to_apply=%region_20.21 | all-reduce | flops 1 | bytes 8 | tf_op jit(solution)/shard_map/psum | solution.py:98
  453.5 178.3 %reduce-scatter.3.cloned.1.call-done = f32[64,512]{1,0:T(8,128)} async-done(((f32[2048,512]{1,0:T(8,128)}), f32[64,512]{1,0:T(8,128)}) %reduce-scatter.3.cloned.1.call-update) | async-done | bytes 131088 | tf_op jit(solution)/shard_map/reduce_scatter | solution.py:93
  (121 shorter events, 1.9 us)
Async XLA Ops:
  7.2 30.0 %all-gather.5.cloned.1.call-start = ((), (), s32[]{:S(2)}) async-start(), calls=%async_computation.3 | async-start | bytes 1179648 | tf_op jit(solution)/shard_map/all_gather | solution.py:26
  7.9 111.2 %all-gather.3.cloned.1.call-start = ((), (), s32[]{:S(2)}) async-start(), calls=%async_computation.2 | async-start | bytes 2162688 | tf_op jit(solution)/shard_map/all_gather | solution.py:23
  8.6 444.9 %reduce-scatter.5.cloned.1.call-start = ((), (), s32[]{:S(2)}) async-start(), calls=%async_computation.5 | async-start | bytes 2359296 | tf_op jit(solution)/shard_map/reduce_scatter | solution.py:96
  322.1 2.2 copy-start.1
  329.0 2.2 copy-start.1
  335.9 2.2 copy-start.1
  342.8 2.2 copy-start.1
  349.7 2.2 copy-start.1
  356.6 2.2 copy-start.1
  363.5 2.2 copy-start.1
  370.3 2.2 copy-start.1
  374.1 1.3 copy-start
  375.4 256.4 %reduce-scatter.3.cloned.1.call-start = ((), (), s32[]{:S(2)}) async-start(), calls=%async_computation.4 | async-start | bytes 4325376 | tf_op jit(solution)/shard_map/reduce_scatter | solution.py:93
Sparse Core Ops, SparseCore 0:
  9.9 27.2 all-gather.4
  39.7 79.2 all-gather.2
  375.6 29.0 reduce-scatter.4
  408.9 222.8 reduce-scatter.2
where the time goes:
time: 641 us; the launch traced here: 639 us
  blocking collectives  265 us (41%)
  waiting for transfers between devices  264 us (41%)
  matrix products  80.4 us (13%)
  between operations  17 us (3%)
    reduce_scatter x1, waiting for transfers between devices, shards(): lax.psum_scatter(grad_rows.reshape(nrow, width), 'goal', scatter_dimensio...  178 us
    all_gather x1, waiting for transfers between devices, shards(): lax.all_gather(phi, 'goal', axis=0, tiled=True)  81.9 us
    psum x1, blocking collectives, shards(): total = lax.psum(jnp.sum(own_lse) + part, ('row', 'goal'))  75.5 us
    pmax x1, blocking collectives, shards(): row_max = lax.pmax(row_max.reshape(nrow), 'goal')  73.1 us
    psum x1, blocking collectives, shards(): row_sum = lax.psum(row_sum.reshape(nrow), 'goal')  70.6 us
    dot_general x24, matrix products, product_t(): lax.dot_general(left, right, (((1,), (1,)), ((), ())), preferred_element_...  50.7 us
    unnamed x1, blocking collectives  23.8 us
    dot_general x8, matrix products, product_tn(): lax.dot_general(left, right, (((0,), (0,)), ((), ())), preferred_element_...  17.2 us
  transfers between devices with their start and end apart: 4, of which 3 were waited for; matrix products, arithmetic and copies ran while one was open for 0% of the time, Pallas kernels for 0%

commit v1 on v0

v1 whole, which is shorter than its diff:
```python
import functools
import math

import jax
import jax.numpy as jnp
from jax import lax
from jax.experimental import pallas as pl
from jax.experimental.pallas import tpu as pltpu
from jax.sharding import Mesh, PartitionSpec as P

ALL = ("y", "core", "x", "z")
PEERS = ("y", "core", "x")
EXTRA = 8
CHUNK = 256
LANES = 128
LOG2E = math.log2(math.e)
SHIFTS = (4, 3, 5, 2, 6, 1, 7)
VMEM_LIMIT = 32 * 1024 * 1024


def nt(left, right):
    return lax.dot_general(
        left, right, (((1,), (1,)), ((), ())), preferred_element_type=jnp.float32
    )


def tn(left, right):
    return lax.dot_general(
        left, right, (((0,), (0,)), ((), ())), preferred_element_type=jnp.float32
    )


def nn(left, right):
    return lax.dot_general(
        left, right, (((1,), (0,)), ((), ())), preferred_element_type=jnp.float32
    )


def to_rows(lanes):
    return jnp.transpose(jnp.broadcast_to(lanes, (LANES, LANES)))


def to_lanes(column):
    return jnp.transpose(jnp.broadcast_to(column, (LANES, LANES)))[0:1]


def place_shards(place_ref, pieces, psi_ref):
    own = place_ref[0]
    shard = pieces[0].shape[0]
    nz = len(pieces)
    for piece, shift in zip(pieces, (0,) + SHIFTS):
        slot = lax.rem(own + nz - shift, nz)
        psi_ref[pl.ds(pl.multiple_of(slot * shard, shard), shard), :] = piece[...]


def row_places(phi_ref, first, shards, shard):
    out = []
    for k in range(shards):
        block = phi_ref[first + k]
        code = to_rows(block[shard : shard + 1, :LANES].astype(jnp.float32))
        out.append(code[:shard] * 256.0 + code[shard : 2 * shard])
    return jnp.concatenate(out, axis=0)


def hit_mask(places, base, ncol):
    rel = places - base
    lane = lax.broadcasted_iota(jnp.int32, rel.shape, 1).astype(jnp.float32)
    off = rel - lane
    return jnp.concatenate(
        [off == float(t * LANES) for t in range(ncol // LANES)], axis=1
    )


def stats_kernel(scale2, shard, place_ref, phi_ref, *refs):
    nz = 1 + len(SHIFTS)
    pieces = refs[:nz]
    row_ref, col_ref, psi_ref = refs[nz:]
    place_shards(place_ref, pieces, psi_ref)
    ncol = psi_ref.shape[0]
    npeer = phi_ref.shape[0]
    per = CHUNK // shard
    base = place_ref[1].astype(jnp.float32)
    psi = psi_ref[...]
    col_max = jnp.full((1, ncol), -1e30, jnp.float32)
    col_sum = jnp.zeros((1, ncol), jnp.float32)
    count = jnp.zeros((1, ncol), jnp.float32)
    hit_sum = jnp.zeros((1, ncol), jnp.float32)
    for c in range(npeer // per):
        rows = phi_ref[c * per : (c + 1) * per, :shard, :].reshape(CHUNK, -1)
        logits = nt(rows, psi) * scale2
        peak = jnp.max(logits, axis=1, keepdims=True)
        total = jnp.sum(jnp.exp2(logits - peak), axis=1, keepdims=True)
        lse = peak + jnp.log2(total)
        for t in range(CHUNK // LANES):
            line = to_lanes(lse[t * LANES : (t + 1) * LANES])
            at = c * (CHUNK // LANES) + t
            row_ref[:, at : at + 1, :] = jnp.broadcast_to(line[None], (npeer, 1, LANES))
        new_max = jnp.maximum(col_max, jnp.max(logits, axis=0, keepdims=True))
        part = jnp.sum(jnp.exp2(logits - new_max), axis=0, keepdims=True)
        col_sum = col_sum * jnp.exp2(col_max - new_max) + part
        col_max = new_max
        hit = hit_mask(row_places(phi_ref, c * per, per, shard), base, ncol)
        count = count + jnp.sum(jnp.where(hit, 1.0, 0.0), axis=0, keepdims=True)
        hit_sum = hit_sum + jnp.sum(jnp.where(hit, logits, 0.0), axis=0, keepdims=True)
    col_lse = col_max + jnp.log2(col_sum)
    nline = ncol // LANES
    hits = jnp.zeros((1, LANES), jnp.float32)
    for t in range(nline):
        cut = slice(t * LANES, (t + 1) * LANES)
        col_ref[t : t + 1, :] = col_lse[:, cut]
        col_ref[nline + t : nline + t + 1, :] = count[:, cut]
        hits = hits + hit_sum[:, cut]
    lines = npeer * shard // LANES
    row_ref[:, lines : lines + 1, :] = jnp.broadcast_to(hits[None], (npeer, 1, LANES))
    row_ref[:, lines + 1 :, :] = jnp.zeros(
        (npeer, row_ref.shape[1] - lines - 1, LANES), jnp.float32
    )


def split3(value):
    first = value.astype(jnp.bfloat16)
    rest = value - first.astype(jnp.float32)
    second = rest.astype(jnp.bfloat16)
    third = (rest - second.astype(jnp.float32)).astype(jnp.bfloat16)
    return jnp.concatenate([first, second, third], axis=0)


def tail_rows(value, width):
    terms = jnp.broadcast_to(value, (1, width))
    first = terms.astype(jnp.bfloat16).astype(jnp.float32)
    second = (terms - first).astype(jnp.bfloat16).astype(jnp.float32)
    third = terms - first - second
    row = lax.broadcasted_iota(jnp.int32, (EXTRA, width), 0)
    full = jnp.where(
        row == 0, first, jnp.where(row == 1, second, jnp.where(row == 2, third, 0.0))
    )
    return full.astype(jnp.bfloat16)


def grads_kernel(scale, scale2, shard, place_ref, phi_ref, rows_ref, *refs):
    nz = 1 + len(SHIFTS)
    pieces = refs[:nz]
    col_parts = refs[nz : 2 * nz]
    gphi_ref = refs[2 * nz]
    gpsi_refs = refs[2 * nz + 1 : 3 * nz + 1]
    psi_ref, acc_ref = refs[3 * nz + 1 :]
    place_shards(place_ref, pieces, psi_ref)
    ncol, width = psi_ref.shape
    npeer = phi_ref.shape[0]
    per = CHUNK // shard
    nline = ncol // LANES
    lines = npeer * shard // LANES
    base = place_ref[1].astype(jnp.float32)
    shift2 = math.log2(scale)

    row_parts = rows_ref[:, :lines, :]
    row_peak = jnp.max(row_parts, axis=0)
    row_lse = row_peak + jnp.log2(jnp.sum(jnp.exp2(row_parts - row_peak[None]), axis=0))
    hits = jnp.sum(rows_ref[:, lines : lines + 1, :], axis=0)
    row_total = jnp.sum(row_lse, keepdims=True) - 2.0 * jnp.sum(hits, keepdims=True)

    cols = [part[...] for part in col_parts]
    col_peak = functools.reduce(jnp.maximum, [part[:nline] for part in cols])
    col_sum = functools.reduce(
        jnp.add, [jnp.exp2(part[:nline] - col_peak) for part in cols]
    )
    counts = functools.reduce(jnp.add, [part[nline:] for part in cols])
    col_lse = col_peak + jnp.log2(col_sum)
    col_total = jnp.sum(counts * col_lse, keepdims=True)
    col_shift = col_lse - jnp.log2(counts) - shift2
    col_line = jnp.concatenate([col_shift[t : t + 1] for t in range(nline)], axis=1)
    row_shift = row_lse - shift2

    psi = psi_ref[...]
    for c in range(npeer // per):
        rows = phi_ref[c * per : (c + 1) * per, :shard, :].reshape(CHUNK, width)
        logits = nt(rows, psi) * scale2
        first = c * (CHUNK // LANES)
        lse = jnp.concatenate(
            [to_rows(row_shift[first + t : first + t + 1]) for t in range(CHUNK // LANES)],
            axis=0,
        )
        lse = jnp.concatenate([lse] * nline, axis=1)
        hit = hit_mask(row_places(phi_ref, c * per, per, shard), base, ncol)
        weights = jnp.exp2(logits - lse) + jnp.exp2(logits - col_line)
        weights = (weights - jnp.where(hit, 2.0 * scale, 0.0)).astype(jnp.bfloat16)
        part = nn(weights, psi).astype(jnp.bfloat16)
        gphi_ref[c * per : (c + 1) * per, :shard, :] = part.reshape(per, shard, width)
        back = tn(weights, rows)
        if c == 0:
            acc_ref[...] = back
        else:
            acc_ref[...] += back
    tail = tail_rows(col_total, width)
    gphi_ref[:, shard:, :] = jnp.broadcast_to(tail[None], (npeer, EXTRA, width))
    tail = tail_rows(row_total, width)
    own = place_ref[0]
    piece = pieces[0].shape[0]
    for out, shift in zip(gpsi_refs, (0,) + SHIFTS):
        slot = lax.rem(own + shift, nz)
        part = acc_ref[pl.ds(pl.multiple_of(slot * piece, piece), piece), :]
        out[:piece, :] = part.astype(jnp.bfloat16)
        out[piece:, :] = tail


def total_kernel(nrow, phi_parts_ref, *refs):
    nz = 1 + len(SHIFTS)
    parts = refs[:nz]
    gphi_ref, gpsi_ref, loss_ref = refs[nz:]
    shard = gphi_ref.shape[0]
    piece = gpsi_ref.shape[0]
    total = phi_parts_ref[0].astype(jnp.float32)
    for k in range(1, phi_parts_ref.shape[0]):
        total = total + phi_parts_ref[k].astype(jnp.float32)
    gphi_ref[...] = total[:shard]
    loss = total[shard : shard + 1, :LANES]
    for r in range(1, 3):
        loss = loss + total[shard + r : shard + r + 1, :LANES]
    total = parts[0][...].astype(jnp.float32)
    for part in parts[1:]:
        total = total + part[...].astype(jnp.float32)
    gpsi_ref[...] = total[:piece]
    for r in range(3):
        loss = loss + total[piece + r : piece + r + 1, :LANES]
    loss_ref[...] = jnp.broadcast_to(loss * (math.log(2.0) / nrow), loss_ref.shape)


def shards(phi, psi, positives):
    shard, width = phi.shape
    piece = psi.shape[0]
    npeer = lax.axis_size(PEERS)
    nz = lax.axis_size("z")
    nrow = npeer * shard
    ncol = nz * piece
    scale = 1.0 / math.sqrt(width)
    scale2 = scale * LOG2E
    peer = lax.axis_index(PEERS)
    place = jnp.stack([lax.axis_index("z"), peer * ncol]).astype(jnp.int32)

    def spread(array):
        return lax.all_to_all(array, PEERS, 0, 0, tiled=True)

    def move(array, shift):
        return lax.ppermute(array, "z", [(i, (i + shift) % nz) for i in range(nz)])

    smem = pl.BlockSpec(memory_space=pltpu.SMEM)
    vmem = pl.BlockSpec(memory_space=pltpu.VMEM)
    params = pltpu.CompilerParams(vmem_limit_bytes=VMEM_LIMIT)

    code = jnp.concatenate([positives // 256, positives % 256]).astype(jnp.bfloat16)
    code = jnp.pad(code[None, :], ((0, EXTRA - 1), (0, width - 2 * shard)))
    block = jnp.concatenate([phi, code], axis=0)
    rows = spread(jnp.broadcast_to(block[None], (npeer,) + block.shape))
    goals = [psi] + [move(psi, s) for s in SHIFTS]

    lines = nrow // LANES + 8
    row_stats, col_stats = pl.pallas_call(
        functools.partial(stats_kernel, scale2, shard),
        out_shape=(
            jax.ShapeDtypeStruct((npeer, lines, LANES), jnp.float32),
            jax.ShapeDtypeStruct((2 * ncol // LANES, LANES), jnp.float32),
        ),
        in_specs=[smem] + [vmem] * (1 + nz),
        out_specs=(vmem, vmem),
        scratch_shapes=[pltpu.VMEM((ncol, width), jnp.bfloat16)],
        compiler_params=params,
        name="stats",
    )(place, rows, *goals)

    row_parts = spread(row_stats)
    col_parts = [col_stats] + [move(col_stats, s) for s in SHIFTS]

    outs = pl.pallas_call(
        functools.partial(grads_kernel, scale, scale2, shard),
        out_shape=(jax.ShapeDtypeStruct((npeer, shard + EXTRA, width), jnp.bfloat16),)
        + (jax.ShapeDtypeStruct((piece + EXTRA, width), jnp.bfloat16),) * nz,
        in_specs=[smem] + [vmem] * (2 + 2 * nz),
        out_specs=(vmem,) * (1 + nz),
        scratch_shapes=[
            pltpu.VMEM((ncol, width), jnp.bfloat16),
            pltpu.VMEM((ncol, width), jnp.float32),
        ],
        compiler_params=params,
        name="grads",
    )(place, rows, row_parts, *goals, *col_parts)

    phi_parts = spread(outs[0])
    psi_parts = [outs[1]] + [move(part, s) for part, s in zip(outs[2:], SHIFTS)]

    grad_phi, grad_psi, loss = pl.pallas_call(
        functools.partial(total_kernel, nrow * nz),
        out_shape=(
            jax.ShapeDtypeStruct((shard, width), jnp.float32),
            jax.ShapeDtypeStruct((piece, width), jnp.float32),
            jax.ShapeDtypeStruct((8, LANES), jnp.float32),
        ),
        in_specs=[vmem] * (1 + nz),
        out_specs=(vmem,) * 3,
        compiler_params=params,
        name="totals",
    )(phi_parts, *psi_parts)
    return (grad_phi, grad_psi, loss[0, 0])


def solution(mesh):
    nrow, ngoal = mesh.shape["row"], mesh.shape["goal"]
    fine = Mesh(mesh.devices.reshape(nrow // 2, 2, ngoal // 8, 8), ALL)
    return jax.shard_map(
        shards,
        mesh=fine,
        in_specs=(P(ALL, None), P(ALL, None), P(ALL)),
        out_specs=(P(ALL, None), P(ALL, None), P()),
        check_vma=False,
    )
```

time: 641 us -> 140 us (0.22)
  blocking collectives: 265 us -> 0 us
  waiting for transfers between devices: 264 us -> 32 us
  matrix products: 80.4 us -> 0 us
  starting transfers between devices: 0.16 us -> 68.3 us
  Pallas kernels: 0 us -> 17.5 us
  between operations: 17 us -> 0.74 us
  local copies, waits for them, and re-layouts: 4.45 us -> 18.6 us
    reduce_scatter x2 -> x0, waiting for transfers between devices: 178 us -> none  [the longest x1 178 us: shards(): lax.psum_scatter(grad_rows.reshape(nrow, width), 'goal', scatter_dimensio...]
    psum x3 -> x0, blocking collectives: 158 us -> none  [the longest x1 75.5 us: shards(): total = lax.psum(jnp.sum(own_lse) + part, ('row', 'goal'))]
    all_gather x2 -> x0, waiting for transfers between devices: 83.7 us -> none  [the longest x1 81.9 us: shards(): lax.all_gather(phi, 'goal', axis=0, tiled=True)]
    pmax x2 -> x0, blocking collectives: 83.2 us -> none  [the longest x1 73.1 us: shards(): row_max = lax.pmax(row_max.reshape(nrow), 'goal')]
    dot_general x40 -> x0, matrix products: 80.4 us -> none  [the longest x24 50.7 us: product_t(): lax.dot_general(left, right, (((1,), (1,)), ((), ())), preferred_element_...]
    ppermute x0 -> x21, starting transfers between devices: none -> 45.8 us  [move(): return lax.ppermute(array, 'z', [(i, (i + shift) % nz) for i in range(nz)])]
    ppermute x0 -> x21, waiting for transfers between devices: none -> 32 us  [move(): return lax.ppermute(array, 'z', [(i, (i + shift) % nz) for i in range(nz)])]
    unnamed x1 -> x0, blocking collectives: 23.8 us -> none
  transfers between devices with their start and end apart: 4 -> 24, of which waited for: 3 -> 9; matrix products, arithmetic and copies ran while one was open for 0% -> 0% of each run, Pallas kernels for 0% -> 0%
where the time goes in v1:
time: 140 us; the launch traced here: 139 us
  starting transfers between devices  68.3 us (49%)
  waiting for transfers between devices  32 us (23%)
  local copies, waits for them, and re-layouts  18.6 us (13%)
  Pallas kernels  17.5 us (12%)
  other arithmetic  1.67 us (1%)
    ppermute x21, starting transfers between devices, move(): return lax.ppermute(array, 'z', [(i, (i + shift) % nz) for i in range(nz)])  45.8 us
    ppermute x21, waiting for transfers between devices, move(): return lax.ppermute(array, 'z', [(i, (i + shift) % nz) for i in range(nz)])  32 us
    all_to_all x3, starting transfers between devices, spread(): return lax.all_to_all(array, PEERS, 0, 0, tiled=True)  22.5 us
    unnamed x58, local copies, waits for them, and re-layouts  16.5 us
    pallas_call x1, Pallas kernels, shards(): pl.pallas_call(functools.partial(grads_kernel, scale, scale2, shard), out...  9.35 us
    pallas_call x1, Pallas kernels, shards(): pl.pallas_call(functools.partial(stats_kernel, scale2, shard), out_shape=...  6.98 us
  transfers between devices with their start and end apart: 24, of which 9 were waited for; matrix products, arithmetic and copies ran while one was open for 0% of the time, Pallas kernels for 0%

profile of v1, /device:TPU:8, one launch (start us, length us, event | category | flops | bytes accessed | tf_op | source)
XLA Modules:
  0.0 138.7 jit_solution(801730304136450915)
XLA Ops:
  0.6 0.7 convert_bitcast_fusion
  1.3 0.1 fusion.5
  1.4 0.8 pad_maximum_fusion
  2.2 1.5 %broadcast_in_dim.2 = bf16[32,72,512]{2,1,0:T(8,128)(2,1)} broadcast(bf16[72,512]{1,0:T(8,128)(2,1)S(1)} %pad_maximum_fusion), dimensions={1,2} | broadcast | bytes 2433024 | tf_op jit(solution)/shard_map/broadcast_in_dim | solution.py:253
  3.8 7.7 %all-to-all-start = ((bf16[32,72,512]{2,1,0:T(8,128)(2,1)}), bf16[32,72,512]{2,1,0:T(8,128)(2,1)S(1)}, u32[]{:S(2)}, u32[]{:S(2)}) async-start(bf16[32,72,512]{2,1,0:T(8,128)(2,1)} %broadcast_in_dim.2), calls=%async_computation | async-start | bytes 4718592 | tf_op jit(solution)/shard_map/all_to_all | solution.py:241
  11.5 5.9 %collective-permute-start.6 = (bf16[128,512]{1,0:T(8,128)(2,1)S(1)}, bf16[128,512]{1,0:T(8,128)(2,1)S(1)}, u32[]{:S(2)}, u32[]{:S(2)}) collective-permute-start(bf16[128,512]{1,0:T(8,128)(2,1)S(1)} %copy-done.1), channel_id=1, source_target_pairs={{0,7},{1,0},{2,1},{3,2},{4,3},{5,4},{6,5},{7,6},{8,15},{9,8},{10,9... | collective-permute-start | bytes 393224 | tf_op jit(solution)/shard_map/ppermute | solution.py:244
  17.4 0.0 collective-permute-start.5
  17.4 2.5 %collective-permute-start.4 = (bf16[128,512]{1,0:T(8,128)(2,1)S(1)}, bf16[128,512]{1,0:T(8,128)(2,1)S(1)}, u32[]{:S(2)}, u32[]{:S(2)}) collective-permute-start(bf16[128,512]{1,0:T(8,128)(2,1)S(1)} %copy-done.1), channel_id=1, source_target_pairs={{0,6},{1,7},{2,0},{3,1},{4,2},{5,3},{6,4},{7,5},{8,14},{9,15},{10,... | collective-permute-start | bytes 393224 | tf_op jit(solution)/shard_map/ppermute | solution.py:244
  19.9 0.5 collective-permute-start.3
  20.3 2.9 %collective-permute-start.2 = (bf16[128,512]{1,0:T(8,128)(2,1)S(1)}, bf16[128,512]{1,0:T(8,128)(2,1)S(1)}, u32[]{:S(2)}, u32[]{:S(2)}) collective-permute-start(bf16[128,512]{1,0:T(8,128)(2,1)S(1)} %copy-done.1), channel_id=1, source_target_pairs={{0,5},{1,6},{2,7},{3,0},{4,1},{5,2},{6,3},{7,4},{8,13},{9,14},{10,... | collective-permute-start | bytes 393224 | tf_op jit(solution)/shard_map/ppermute | solution.py:244
  23.2 0.9 collective-permute-start.1
  24.1 4.6 %collective-permute-start = (bf16[128,512]{1,0:T(8,128)(2,1)S(1)}, bf16[128,512]{1,0:T(8,128)(2,1)S(1)}, u32[]{:S(2)}, u32[]{:S(2)}) collective-permute-start(bf16[128,512]{1,0:T(8,128)(2,1)S(1)} %copy-done.1), channel_id=1, source_target_pairs={{0,4},{1,5},{2,6},{3,7},{4,0},{5,1},{6,2},{7,3},{8,12},{9,13},{10,... | collective-permute-start | bytes 393224 | tf_op jit(solution)/shard_map/ppermute | solution.py:244
  28.7 0.1 pad_add_fusion.place_ref
  28.8 0.0 collective-permute-done.3.refs_4_
  28.8 1.1 collective-permute-done.2.refs_3_
  29.9 10.0 %collective-permute-done.1.refs_2_ = bf16[128,512]{1,0:T(8,128)(2,1)S(1)} collective-permute-done((bf16[128,512]{1,0:T(8,128)(2,1)S(1)}, bf16[128,512]{1,0:T(8,128)(2,1)S(1)}, u32[]{:S(2)}, u32[]{:S(2)}) %collective-permute-start.1) | collective-permute-done | bytes 131104 | tf_op jit(solution)/shard_map/ppermute | solution.py:244
  39.9 2.2 %collective-permute-done.refs_1_ = bf16[128,512]{1,0:T(8,128)(2,1)S(1)} collective-permute-done((bf16[128,512]{1,0:T(8,128)(2,1)S(1)}, bf16[128,512]{1,0:T(8,128)(2,1)S(1)}, u32[]{:S(2)}, u32[]{:S(2)}) %collective-permute-start) | collective-permute-done | bytes 131104 | tf_op jit(solution)/shard_map/ppermute | solution.py:244
  42.1 0.0 all-to-all-done.phi_ref
  42.1 7.0 %stats.1 = (f32[32,24,128]{2,1,0:T(8,128)S(1)}, f32[16,128]{1,0:T(8,128)S(1)}) custom-call(s32[2]{0:T(128)S(1)} %pad_add_fusion.place_ref, bf16[32,72,512]{2,1,0:T(8,128)(2,1)S(1)} %all-to-all-done.phi_ref, bf16[128,512]{1,0:T(8,128)(2,1)S(1)} %copy-done.1, bf16[128,512]{1,0:T(8,128)(2,1)S(1)} %collective-permute-done.refs_1_, ...), custom_call_target="tpu_custom_call" | custom-call | tf_op jit(solution)/shard_map/stats/pallas_call | solution.py:257
  49.1 0.7 copy-done.6
  49.8 7.4 %all-to-all-start.1 = ((f32[32,24,128]{2,1,0:T(8,128)}), f32[32,24,128]{2,1,0:T(8,128)S(1)}, u32[]{:S(2)}, u32[]{:S(2)}) async-start(f32[32,24,128]{2,1,0:T(8,128)} %copy-done.6), calls=%async_computation.1 | async-start | bytes 786432 | tf_op jit(solution)/shard_map/all_to_all | solution.py:241
  57.2 3.1 %collective-permute-start.13 = (f32[16,128]{1,0:T(8,128)S(1)}, f32[16,128]{1,0:T(8,128)S(1)}, u32[]{:S(2)}, u32[]{:S(2)}) collective-permute-start(f32[16,128]{1,0:T(8,128)S(1)} %get-tuple-element.18.refs_8_), channel_id=1, source_target_pairs={{0,7},{1,0},{2,1},{3,2},{4,3},{5,4},{6,5},{7,6},{8,15},{9,8},{10,9... | collective-permute-start | bytes 24584 | tf_op jit(solution)/shard_map/ppermute | solution.py:244
  60.3 3.3 %collective-permute-start.11 = (f32[16,128]{1,0:T(8,128)S(1)}, f32[16,128]{1,0:T(8,128)S(1)}, u32[]{:S(2)}, u32[]{:S(2)}) collective-permute-start(f32[16,128]{1,0:T(8,128)S(1)} %get-tuple-element.18.refs_8_), channel_id=1, source_target_pairs={{0,6},{1,7},{2,0},{3,1},{4,2},{5,3},{6,4},{7,5},{8,14},{9,15},{10,... | collective-permute-start | bytes 24584 | tf_op jit(solution)/shard_map/ppermute | solution.py:244
  63.6 2.9 %collective-permute-start.9 = (f32[16,128]{1,0:T(8,128)S(1)}, f32[16,128]{1,0:T(8,128)S(1)}, u32[]{:S(2)}, u32[]{:S(2)}) collective-permute-start(f32[16,128]{1,0:T(8,128)S(1)} %get-tuple-element.18.refs_8_), channel_id=1, source_target_pairs={{0,5},{1,6},{2,7},{3,0},{4,1},{5,2},{6,3},{7,4},{8,13},{9,14},{10,... | collective-permute-start | bytes 24584 | tf_op jit(solution)/shard_map/ppermute | solution.py:244
  66.4 1.0 collective-permute-start.8
  67.4 0.6 copy-done.11
  68.0 3.5 %collective-permute-start.7 = (f32[16,128]{1,0:T(8,128)S(1)}, f32[16,128]{1,0:T(8,128)S(1)}, u32[]{:S(2)}, u32[]{:S(2)}) collective-permute-start(f32[16,128]{1,0:T(8,128)S(1)} %get-tuple-element.18.refs_8_), channel_id=1, source_target_pairs={{0,4},{1,5},{2,6},{3,7},{4,0},{5,1},{6,2},{7,3},{8,12},{9,13},{10,... | collective-permute-start | bytes 24584 | tf_op jit(solution)/shard_map/ppermute | solution.py:244
  71.5 0.6 copy-done.13
  72.1 0.6 copy-done.15
  72.7 0.6 copy-done.17
  73.3 0.6 copy-done.19
  73.9 1.7 %collective-permute-done.7.refs_9_ = f32[16,128]{1,0:T(8,128)S(1)} collective-permute-done((f32[16,128]{1,0:T(8,128)S(1)}, f32[16,128]{1,0:T(8,128)S(1)}, u32[]{:S(2)}, u32[]{:S(2)}) %collective-permute-start.7) | collective-permute-done | bytes 8224 | tf_op jit(solution)/shard_map/ppermute | solution.py:244
  75.5 0.6 copy-done.21
  76.1 0.9 copy-done.3
  77.0 0.9 copy-done.5
  77.9 0.7 copy-done.12
  78.6 0.7 copy-done.14
  79.3 0.7 copy-done.16
  80.0 0.7 copy-done.18
  80.7 0.7 copy-done.20
  81.4 0.7 copy-done.22
  82.1 0.7 copy-done.24
  82.8 9.3 %grads.1 = (bf16[32,72,512]{2,1,0:T(8,128)(2,1)S(1)}, bf16[136,512]{1,0:T(8,128)(2,1)S(1)}, bf16[136,512]{1,0:T(8,128)(2,1)S(1)}, bf16[136,512]{1,0:T(8,128)(2,1...) custom-call(s32[2]{0:T(128)S(1)} %copy-done.24, ...), custom_call_target="tpu_custom_call" | custom-call | tf_op jit(solution)/shard_map/grads/pallas_call | solution.py:273
  92.1 1.4 %copy-done = bf16[32,72,512]{2,1,0:T(8,128)(2,1)} copy-done((bf16[32,72,512]{2,1,0:T(8,128)(2,1)}, bf16[32,72,512]{2,1,0:T(8,128)(2,1)S(1)}, u32[]{:S(2)}) %copy-start) | copy-done | bytes 2359320
  93.5 0.6 copy-done.7
  94.2 0.6 copy-done.25
  94.8 0.7 copy-done.26
  95.5 0.6 copy-done.27
  96.1 7.5 %all-to-all-start.2 = ((bf16[32,72,512]{2,1,0:T(8,128)(2,1)}), bf16[32,72,512]{2,1,0:T(8,128)(2,1)S(1)}, u32[]{:S(2)}, u32[]{:S(2)}) async-start(bf16[32,72,512]{2,1,0:T(8,128)(2,1)} %copy-done), calls=%async_computation.2 | async-start | bytes 4718592 | tf_op jit(solution)/shard_map/all_to_all | solution.py:241
  103.6 3.6 %collective-permute-start.14 = (bf16[136,512]{1,0:T(8,128)(2,1)S(1)}, bf16[136,512]{1,0:T(8,128)(2,1)S(1)}, u32[]{:S(2)}, u32[]{:S(2)}) collective-permute-start(bf16[136,512]{1,0:T(8,128)(2,1)S(1)} %copy-done.28), channel_id=1, source_target_pairs={{0,4},{1,5},{2,6},{3,7},{4,0},{5,1},{6,2},{7,3},{8,12},{9,13},{10,... | collective-permute-start | bytes 417800 | tf_op jit(solution)/shard_map/ppermute | solution.py:244
  107.3 5.0 %collective-permute-start.15 = (bf16[136,512]{1,0:T(8,128)(2,1)}, bf16[136,512]{1,0:T(8,128)(2,1)S(1)}, u32[]{:S(2)}, u32[]{:S(2)}) collective-permute-start(bf16[136,512]{1,0:T(8,128)(2,1)} %get-tuple-element.22), channel_id=1, source_target_pairs={{0,3},{1,4},{2,5},{3,6},{4,7},{5,0},{6,1},{7,2},{8,11},{9,12},{10,... | collective-permute-start | bytes 417800 | tf_op jit(solution)/shard_map/ppermute | solution.py:244
  112.3 0.0 collective-permute-start.16
  112.3 4.2 %collective-permute-start.17 = (bf16[136,512]{1,0:T(8,128)(2,1)}, bf16[136,512]{1,0:T(8,128)(2,1)S(1)}, u32[]{:S(2)}, u32[]{:S(2)}) collective-permute-start(bf16[136,512]{1,0:T(8,128)(2,1)} %get-tuple-element.24), channel_id=1, source_target_pairs={{0,2},{1,3},{2,4},{3,5},{4,6},{5,7},{6,0},{7,1},{8,10},{9,11},{10,... | collective-permute-start | bytes 417800 | tf_op jit(solution)/shard_map/ppermute | solution.py:244
  116.5 1.1 collective-permute-start.18
  117.6 0.9 collective-permute-start.19
  118.4 8.7 %collective-permute-done.15.refs_2_ = bf16[136,512]{1,0:T(8,128)(2,1)S(1)} collective-permute-done((bf16[136,512]{1,0:T(8,128)(2,1)}, bf16[136,512]{1,0:T(8,128)(2,1)S(1)}, u32[]{:S(2)}, u32[]{:S(2)}) %collective-permute-start.15) | collective-permute-done | bytes 139296 | tf_op jit(solution)/shard_map/ppermute | solution.py:244
  127.2 1.5 %collective-permute-done.16.refs_3_ = bf16[136,512]{1,0:T(8,128)(2,1)S(1)} collective-permute-done((bf16[136,512]{1,0:T(8,128)(2,1)}, bf16[136,512]{1,0:T(8,128)(2,1)S(1)}, u32[]{:S(2)}, u32[]{:S(2)}) %collective-permute-start.16) | collective-permute-done | bytes 139296 | tf_op jit(solution)/shard_map/ppermute | solution.py:244
  128.6 2.8 %collective-permute-done.17.refs_4_ = bf16[136,512]{1,0:T(8,128)(2,1)S(1)} collective-permute-done((bf16[136,512]{1,0:T(8,128)(2,1)}, bf16[136,512]{1,0:T(8,128)(2,1)S(1)}, u32[]{:S(2)}, u32[]{:S(2)}) %collective-permute-start.17) | collective-permute-done | bytes 139296 | tf_op jit(solution)/shard_map/ppermute | solution.py:244
  131.4 2.9 %collective-permute-done.18.refs_5_ = bf16[136,512]{1,0:T(8,128)(2,1)S(1)} collective-permute-done((bf16[136,512]{1,0:T(8,128)(2,1)}, bf16[136,512]{1,0:T(8,128)(2,1)S(1)}, u32[]{:S(2)}, u32[]{:S(2)}) %collective-permute-start.18) | collective-permute-done | bytes 139296 | tf_op jit(solution)/shard_map/ppermute | solution.py:244
  134.3 1.2 collective-permute-done.20.refs_7_
  135.5 0.7 copy-done.9
  136.2 0.9 copy-done.10
  137.1 1.1 totals.1
  138.2 0.5 slice.3
  (51 shorter events, 0.1 us)
Async XLA Ops:
  3.8 7.7 %copy-start.1 = (bf16[128,512]{1,0:T(8,128)(2,1)S(1)}, bf16[128,512]{1,0:T(8,128)(2,1)}, u32[]{:S(2)}) copy-start(bf16[128,512]{1,0:T(8,128)(2,1)} %refs_0_.3) | copy-start | bytes 393220
  3.8 38.3 %all-to-all-start = ((bf16[32,72,512]{2,1,0:T(8,128)(2,1)}), bf16[32,72,512]{2,1,0:T(8,128)(2,1)S(1)}, u32[]{:S(2)}, u32[]{:S(2)}) async-start(bf16[32,72,512]{2,1,0:T(8,128)(2,1)} %broadcast_in_dim.2), calls=%async_computation | async-start | bytes 4718592 | tf_op jit(solution)/shard_map/all_to_all | solution.py:241
  11.5 11.8 %collective-permute-start.6 = (bf16[128,512]{1,0:T(8,128)(2,1)S(1)}, bf16[128,512]{1,0:T(8,128)(2,1)S(1)}, u32[]{:S(2)}, u32[]{:S(2)}) collective-permute-start(bf16[128,512]{1,0:T(8,128)(2,1)S(1)} %copy-done.1), channel_id=1, source_target_pairs={{0,7},{1,0},{2,1},{3,2},{4,3},{5,4},{6,5},{7,6},{8,15},{9,8},{10,9... | collective-permute-start | bytes 393224 | tf_op jit(solution)/shard_map/ppermute | solution.py:244
  17.4 6.8 %collective-permute-start.5 = (bf16[128,512]{1,0:T(8,128)(2,1)S(1)}, bf16[128,512]{1,0:T(8,128)(2,1)S(1)}, u32[]{:S(2)}, u32[]{:S(2)}) collective-permute-start(bf16[128,512]{1,0:T(8,128)(2,1)S(1)} %copy-done.1), channel_id=1, source_target_pairs={{0,1},{1,2},{2,3},{3,4},{4,5},{5,6},{6,7},{7,0},{8,9},{9,10},{10,1... | collective-permute-start | bytes 393224 | tf_op jit(solution)/shard_map/ppermute | solution.py:244
  17.4 11.4 %collective-permute-start.4 = (bf16[128,512]{1,0:T(8,128)(2,1)S(1)}, bf16[128,512]{1,0:T(8,128)(2,1)S(1)}, u32[]{:S(2)}, u32[]{:S(2)}) collective-permute-start(bf16[128,512]{1,0:T(8,128)(2,1)S(1)} %copy-done.1), channel_id=1, source_target_pairs={{0,6},{1,7},{2,0},{3,1},{4,2},{5,3},{6,4},{7,5},{8,14},{9,15},{10,... | collective-permute-start | bytes 393224 | tf_op jit(solution)/shard_map/ppermute | solution.py:244
  19.9 9.0 %collective-permute-start.3 = (bf16[128,512]{1,0:T(8,128)(2,1)S(1)}, bf16[128,512]{1,0:T(8,128)(2,1)S(1)}, u32[]{:S(2)}, u32[]{:S(2)}) collective-permute-start(bf16[128,512]{1,0:T(8,128)(2,1)S(1)} %copy-done.1), channel_id=1, source_target_pairs={{0,2},{1,3},{2,4},{3,5},{4,6},{5,7},{6,0},{7,1},{8,10},{9,11},{10,... | collective-permute-start | bytes 393224 | tf_op jit(solution)/shard_map/ppermute | solution.py:244
  20.3 9.6 %collective-permute-start.2 = (bf16[128,512]{1,0:T(8,128)(2,1)S(1)}, bf16[128,512]{1,0:T(8,128)(2,1)S(1)}, u32[]{:S(2)}, u32[]{:S(2)}) collective-permute-start(bf16[128,512]{1,0:T(8,128)(2,1)S(1)} %copy-done.1), channel_id=1, source_target_pairs={{0,5},{1,6},{2,7},{3,0},{4,1},{5,2},{6,3},{7,4},{8,13},{9,14},{10,... | collective-permute-start | bytes 393224 | tf_op jit(solution)/shard_map/ppermute | solution.py:244
  23.2 16.7 %collective-permute-start.1 = (bf16[128,512]{1,0:T(8,128)(2,1)S(1)}, bf16[128,512]{1,0:T(8,128)(2,1)S(1)}, u32[]{:S(2)}, u32[]{:S(2)}) collective-permute-start(bf16[128,512]{1,0:T(8,128)(2,1)S(1)} %copy-done.1), channel_id=1, source_target_pairs={{0,3},{1,4},{2,5},{3,6},{4,7},{5,0},{6,1},{7,2},{8,11},{9,12},{10,... | collective-permute-start | bytes 393224 | tf_op jit(solution)/shard_map/ppermute | solution.py:244
  24.1 17.9 %collective-permute-start = (bf16[128,512]{1,0:T(8,128)(2,1)S(1)}, bf16[128,512]{1,0:T(8,128)(2,1)S(1)}, u32[]{:S(2)}, u32[]{:S(2)}) collective-permute-start(bf16[128,512]{1,0:T(8,128)(2,1)S(1)} %copy-done.1), channel_id=1, source_target_pairs={{0,4},{1,5},{2,6},{3,7},{4,0},{5,1},{6,2},{7,3},{8,12},{9,13},{10,... | collective-permute-start | bytes 393224 | tf_op jit(solution)/shard_map/ppermute | solution.py:244
  28.8 21.0 %copy-start.23 = (s32[2]{0:T(128)}, s32[2]{0:T(128)S(1)}, u32[]{:S(2)}) copy-start(s32[2]{0:T(128)S(1)} %pad_add_fusion.place_ref) | copy-start | bytes 28
  39.9 9.9 %copy-start.2 = (bf16[128,512]{1,0:T(8,128)(2,1)}, bf16[128,512]{1,0:T(8,128)(2,1)S(1)}, u32[]{:S(2)}) copy-start(bf16[128,512]{1,0:T(8,128)(2,1)S(1)} %collective-permute-done.1.refs_2_) | copy-start | bytes 393220
  42.1 7.8 %copy-start.4 = (bf16[128,512]{1,0:T(8,128)(2,1)}, bf16[128,512]{1,0:T(8,128)(2,1)S(1)}, u32[]{:S(2)}) copy-start(bf16[128,512]{1,0:T(8,128)(2,1)S(1)} %collective-permute-done.refs_1_) | copy-start | bytes 393220
  49.0 0.8 copy-start.6
  49.8 26.3 %all-to-all-start.1 = ((f32[32,24,128]{2,1,0:T(8,128)}), f32[32,24,128]{2,1,0:T(8,128)S(1)}, u32[]{:S(2)}, u32[]{:S(2)}) async-start(f32[32,24,128]{2,1,0:T(8,128)} %copy-done.6), calls=%async_computation.1 | async-start | bytes 786432 | tf_op jit(solution)/shard_map/all_to_all | solution.py:241
  57.2 9.2 %collective-permute-start.13 = (f32[16,128]{1,0:T(8,128)S(1)}, f32[16,128]{1,0:T(8,128)S(1)}, u32[]{:S(2)}, u32[]{:S(2)}) collective-permute-start(f32[16,128]{1,0:T(8,128)S(1)} %get-tuple-element.18.refs_8_), channel_id=1, source_target_pairs={{0,7},{1,0},{2,1},{3,2},{4,3},{5,4},{6,5},{7,6},{8,15},{9,8},{10,9... | collective-permute-start | bytes 24584 | tf_op jit(solution)/shard_map/ppermute | solution.py:244
  60.3 7.1 %collective-permute-start.12 = (f32[16,128]{1,0:T(8,128)S(1)}, f32[16,128]{1,0:T(8,128)S(1)}, u32[]{:S(2)}, u32[]{:S(2)}) collective-permute-start(f32[16,128]{1,0:T(8,128)S(1)} %get-tuple-element.18.refs_8_), channel_id=1, source_target_pairs={{0,1},{1,2},{2,3},{3,4},{4,5},{5,6},{6,7},{7,0},{8,9},{9,10},{10,1... | collective-permute-start | bytes 24584 | tf_op jit(solution)/shard_map/ppermute | solution.py:244
  60.3 11.2 %collective-permute-start.11 = (f32[16,128]{1,0:T(8,128)S(1)}, f32[16,128]{1,0:T(8,128)S(1)}, u32[]{:S(2)}, u32[]{:S(2)}) collective-permute-start(f32[16,128]{1,0:T(8,128)S(1)} %get-tuple-element.18.refs_8_), channel_id=1, source_target_pairs={{0,6},{1,7},{2,0},{3,1},{4,2},{5,3},{6,4},{7,5},{8,14},{9,15},{10,... | collective-permute-start | bytes 24584 | tf_op jit(solution)/shard_map/ppermute | solution.py:244
  63.6 8.5 %collective-permute-start.10 = (f32[16,128]{1,0:T(8,128)S(1)}, f32[16,128]{1,0:T(8,128)S(1)}, u32[]{:S(2)}, u32[]{:S(2)}) collective-permute-start(f32[16,128]{1,0:T(8,128)S(1)} %get-tuple-element.18.refs_8_), channel_id=1, source_target_pairs={{0,2},{1,3},{2,4},{3,5},{4,6},{5,7},{6,0},{7,1},{8,10},{9,11},{10,... | collective-permute-start | bytes 24584 | tf_op jit(solution)/shard_map/ppermute | solution.py:244
  63.6 9.1 %collective-permute-start.9 = (f32[16,128]{1,0:T(8,128)S(1)}, f32[16,128]{1,0:T(8,128)S(1)}, u32[]{:S(2)}, u32[]{:S(2)}) collective-permute-start(f32[16,128]{1,0:T(8,128)S(1)} %get-tuple-element.18.refs_8_), channel_id=1, source_target_pairs={{0,5},{1,6},{2,7},{3,0},{4,1},{5,2},{6,3},{7,4},{8,13},{9,14},{10,... | collective-permute-start | bytes 24584 | tf_op jit(solution)/shard_map/ppermute | solution.py:244
  66.4 6.9 %collective-permute-start.8 = (f32[16,128]{1,0:T(8,128)S(1)}, f32[16,128]{1,0:T(8,128)S(1)}, u32[]{:S(2)}, u32[]{:S(2)}) collective-permute-start(f32[16,128]{1,0:T(8,128)S(1)} %get-tuple-element.18.refs_8_), channel_id=1, source_target_pairs={{0,3},{1,4},{2,5},{3,6},{4,7},{5,0},{6,1},{7,2},{8,11},{9,12},{10,... | collective-permute-start | bytes 24584 | tf_op jit(solution)/shard_map/ppermute | solution.py:244
  67.4 0.6 copy-start.11
  68.0 7.6 %collective-permute-start.7 = (f32[16,128]{1,0:T(8,128)S(1)}, f32[16,128]{1,0:T(8,128)S(1)}, u32[]{:S(2)}, u32[]{:S(2)}) collective-permute-start(f32[16,128]{1,0:T(8,128)S(1)} %get-tuple-element.18.refs_8_), channel_id=1, source_target_pairs={{0,4},{1,5},{2,6},{3,7},{4,0},{5,1},{6,2},{7,3},{8,12},{9,13},{10,... | collective-permute-start | bytes 24584 | tf_op jit(solution)/shard_map/ppermute | solution.py:244
  71.5 0.6 copy-start.13
  72.1 0.6 copy-start.15
  72.7 0.6 copy-start.17
  73.3 0.6 copy-start.19
  75.5 0.6 copy-start.21
  76.1 0.9 copy-start.3
  77.0 0.9 copy-start.5
  77.9 0.7 copy-start.12
  78.6 0.7 copy-start.14
  79.3 0.7 copy-start.16
  80.0 0.7 copy-start.18
  80.7 0.7 copy-start.20
  81.4 0.7 copy-start.22
  82.1 0.7 copy-start.24
  92.1 1.4 %copy-start = (bf16[32,72,512]{2,1,0:T(8,128)(2,1)}, bf16[32,72,512]{2,1,0:T(8,128)(2,1)S(1)}, u32[]{:S(2)}) copy-start(bf16[32,72,512]{2,1,0:T(8,128)(2,1)S(1)} %get-tuple-element.19) | copy-start | bytes 7077892
  93.5 0.6 copy-start.7
  94.2 0.6 copy-start.25
  94.8 0.7 copy-start.26
  95.5 0.6 copy-start.27
  96.1 7.5 %copy-start.28 = (bf16[136,512]{1,0:T(8,128)(2,1)S(1)}, bf16[136,512]{1,0:T(8,128)(2,1)}, u32[]{:S(2)}) copy-start(bf16[136,512]{1,0:T(8,128)(2,1)} %copy-done.27) | copy-start | bytes 417796
  96.1 40.0 %copy-start.8 = (bf16[136,512]{1,0:T(8,128)(2,1)S(1)}, bf16[136,512]{1,0:T(8,128)(2,1)}, u32[]{:S(2)}) copy-start(bf16[136,512]{1,0:T(8,128)(2,1)} %copy-done.7) | copy-start | bytes 417796
  96.1 40.0 %all-to-all-start.2 = ((bf16[32,72,512]{2,1,0:T(8,128)(2,1)}), bf16[32,72,512]{2,1,0:T(8,128)(2,1)S(1)}, u32[]{:S(2)}, u32[]{:S(2)}) async-start(bf16[32,72,512]{2,1,0:T(8,128)(2,1)} %copy-done), calls=%async_computation.2 | async-start | bytes 4718592 | tf_op jit(solution)/shard_map/all_to_all | solution.py:241
  103.6 13.9 %collective-permute-start.14 = (bf16[136,512]{1,0:T(8,128)(2,1)S(1)}, bf16[136,512]{1,0:T(8,128)(2,1)S(1)}, u32[]{:S(2)}, u32[]{:S(2)}) collective-permute-start(bf16[136,512]{1,0:T(8,128)(2,1)S(1)} %copy-done.28), channel_id=1, source_target_pairs={{0,4},{1,5},{2,6},{3,7},{4,0},{5,1},{6,2},{7,3},{8,12},{9,13},{10,... | collective-permute-start | bytes 417800 | tf_op jit(solution)/shard_map/ppermute | solution.py:244
  107.3 19.9 %collective-permute-start.15 = (bf16[136,512]{1,0:T(8,128)(2,1)}, bf16[136,512]{1,0:T(8,128)(2,1)S(1)}, u32[]{:S(2)}, u32[]{:S(2)}) collective-permute-start(bf16[136,512]{1,0:T(8,128)(2,1)} %get-tuple-element.22), channel_id=1, source_target_pairs={{0,3},{1,4},{2,5},{3,6},{4,7},{5,0},{6,1},{7,2},{8,11},{9,12},{10,... | collective-permute-start | bytes 417800 | tf_op jit(solution)/shard_map/ppermute | solution.py:244
  112.3 16.4 %collective-permute-start.16 = (bf16[136,512]{1,0:T(8,128)(2,1)}, bf16[136,512]{1,0:T(8,128)(2,1)S(1)}, u32[]{:S(2)}, u32[]{:S(2)}) collective-permute-start(bf16[136,512]{1,0:T(8,128)(2,1)} %get-tuple-element.23), channel_id=1, source_target_pairs={{0,5},{1,6},{2,7},{3,0},{4,1},{5,2},{6,3},{7,4},{8,13},{9,14},{10,... | collective-permute-start | bytes 417800 | tf_op jit(solution)/shard_map/ppermute | solution.py:244
  112.3 19.1 %collective-permute-start.17 = (bf16[136,512]{1,0:T(8,128)(2,1)}, bf16[136,512]{1,0:T(8,128)(2,1)S(1)}, u32[]{:S(2)}, u32[]{:S(2)}) collective-permute-start(bf16[136,512]{1,0:T(8,128)(2,1)} %get-tuple-element.24), channel_id=1, source_target_pairs={{0,2},{1,3},{2,4},{3,5},{4,6},{5,7},{6,0},{7,1},{8,10},{9,11},{10,... | collective-permute-start | bytes 417800 | tf_op jit(solution)/shard_map/ppermute | solution.py:244
  116.5 17.8 %collective-permute-start.18 = (bf16[136,512]{1,0:T(8,128)(2,1)}, bf16[136,512]{1,0:T(8,128)(2,1)S(1)}, u32[]{:S(2)}, u32[]{:S(2)}) collective-permute-start(bf16[136,512]{1,0:T(8,128)(2,1)} %get-tuple-element.25), channel_id=1, source_target_pairs={{0,6},{1,7},{2,0},{3,1},{4,2},{5,3},{6,4},{7,5},{8,14},{9,15},{10,... | collective-permute-start | bytes 417800 | tf_op jit(solution)/shard_map/ppermute | solution.py:244
  117.6 16.7 %collective-permute-start.19 = (bf16[136,512]{1,0:T(8,128)(2,1)}, bf16[136,512]{1,0:T(8,128)(2,1)S(1)}, u32[]{:S(2)}, u32[]{:S(2)}) collective-permute-start(bf16[136,512]{1,0:T(8,128)(2,1)} %copy-done.26), channel_id=1, source_target_pairs={{0,1},{1,2},{2,3},{3,4},{4,5},{5,6},{6,7},{7,0},{8,9},{9,10},{10,1... | collective-permute-start | bytes 417800 | tf_op jit(solution)/shard_map/ppermute | solution.py:244
  127.2 8.3 %collective-permute-start.20 = (bf16[136,512]{1,0:T(8,128)(2,1)}, bf16[136,512]{1,0:T(8,128)(2,1)S(1)}, u32[]{:S(2)}, u32[]{:S(2)}) collective-permute-start(bf16[136,512]{1,0:T(8,128)(2,1)} %copy-done.25), channel_id=1, source_target_pairs={{0,7},{1,0},{2,1},{3,2},{4,3},{5,4},{6,5},{7,6},{8,15},{9,8},{10,9... | collective-permute-start | bytes 417800 | tf_op jit(solution)/shard_map/ppermute | solution.py:244
  135.5 0.7 copy-start.9
  136.2 0.9 copy-start.10

commit v2 on v1

v2 whole, which is shorter than its diff:
```python
import functools
import math

import jax
import jax.numpy as jnp
from jax import lax
from jax.experimental import pallas as pl
from jax.experimental.pallas import tpu as pltpu
from jax.sharding import Mesh, PartitionSpec as P

ALL = ("y", "core", "x", "z")
PEERS = ("y", "core", "x")
PLANE = ("y", "x")
EXTRA = 8
CHUNK = 256
LANES = 128
LOG2E = math.log2(math.e)
SHIFTS = (1, 2, 3, 4, 5, 6, 7)
VMEM_LIMIT = 24 * 1024 * 1024


def nt(left, right):
    return lax.dot_general(
        left, right, (((1,), (1,)), ((), ())), preferred_element_type=jnp.float32
    )


def tn(left, right):
    return lax.dot_general(
        left, right, (((0,), (0,)), ((), ())), preferred_element_type=jnp.float32
    )


def nn(left, right):
    return lax.dot_general(
        left, right, (((1,), (0,)), ((), ())), preferred_element_type=jnp.float32
    )


def to_rows(lanes):
    return jnp.transpose(jnp.broadcast_to(lanes, (LANES, LANES)))


def to_lanes(column):
    return jnp.transpose(jnp.broadcast_to(column, (LANES, LANES)))[0:1]


def place_shards(place_ref, pieces, psi_ref):
    own = place_ref[0]
    shard = pieces[0].shape[0]
    nz = len(pieces)
    for piece, shift in zip(pieces, (0,) + SHIFTS):
        slot = lax.rem(own + nz - shift, nz)
        psi_ref[pl.ds(pl.multiple_of(slot * shard, shard), shard), :] = piece[...]


def row_places(phi_ref, first, shards, shard):
    out = []
    for k in range(shards):
        block = phi_ref[first + k]
        code = to_rows(block[shard : shard + 1, :LANES].astype(jnp.float32))
        out.append(code[:shard] * 256.0 + code[shard : 2 * shard])
    return jnp.concatenate(out, axis=0)


def hit_mask(places, base, ncol):
    rel = places - base
    lane = lax.broadcasted_iota(jnp.int32, rel.shape, 1).astype(jnp.float32)
    off = rel - lane
    return jnp.concatenate(
        [off == float(t * LANES) for t in range(ncol // LANES)], axis=1
    )


def pack_kernel(phi_ref, pos_ref, out_ref, block_ref, sem):
    shard, width = phi_ref.shape
    block_ref[:shard, :] = phi_ref[...]
    places = pos_ref[...]
    high = lax.shift_right_logical(places, 8)
    code = jnp.concatenate([high, places - high * 256], axis=1).astype(jnp.float32)
    code = jnp.concatenate([code, jnp.zeros((1, width - 2 * shard), jnp.float32)], axis=1)
    block_ref[shard:, :] = jnp.broadcast_to(code, (EXTRA, width)).astype(jnp.bfloat16)
    copies = [
        pltpu.make_async_copy(block_ref, out_ref.at[k], sem.at[k])
        for k in range(out_ref.shape[0])
    ]
    for copy in copies:
        copy.start()
    for copy in copies:
        copy.wait()


def chunks_of(refs, shard):
    per = CHUNK // shard
    out = []
    for half, ref in enumerate(refs):
        for first in range(0, ref.shape[0], per):
            out.append((len(out), half, first, ref))
    return out


def line_of(place_ref, number, half, count):
    lines = CHUNK // LANES
    core = place_ref[2]
    whose = core if half == 0 else 1 - core
    return whose * (count // 2 * lines) + (number % (count // 2)) * lines


def row_lines(scale2, shard, phi_ref, psi):
    per = CHUNK // shard
    out = []
    for _, _, first, ref in chunks_of((phi_ref,), shard):
        rows = ref[first : first + per, :shard, :].reshape(CHUNK, -1)
        logits = nt(rows, psi) * scale2
        peak = jnp.max(logits, axis=1, keepdims=True)
        total = jnp.sum(jnp.exp2(logits - peak), axis=1, keepdims=True)
        lse = peak + jnp.log2(total)
        for t in range(CHUNK // LANES):
            out.append(to_lanes(lse[t * LANES : (t + 1) * LANES]))
    return jnp.concatenate(out, axis=0)


def own_rows_kernel(scale2, shard, place_ref, phi_ref, *refs):
    pieces = refs[:-4]
    line_ref, psi_out, psi_ref, sem = refs[-4:]
    place_shards(place_ref, pieces, psi_ref)
    copy = pltpu.make_async_copy(psi_ref, psi_out, sem)
    copy.start()
    line_ref[...] = row_lines(scale2, shard, phi_ref, psi_ref[...])
    copy.wait()


def all_rows_kernel(
    scale2, shard, place_ref, phi_ref, line_ref, psi_in, row_ref, psi_ref, sem
):
    copy = pltpu.make_async_copy(psi_in, psi_ref, sem)
    copy.start()
    count = line_ref.shape[0]
    npeer = row_ref.shape[0]
    core = place_ref[2]
    copy.wait()
    lines = row_lines(scale2, shard, phi_ref, psi_ref[...])
    for whose, part in ((core, line_ref[...]), (1 - core, lines)):
        at = pl.multiple_of(whose * count, count)
        row_ref[:, pl.ds(at, count), :] = jnp.broadcast_to(part[None], (npeer, count, LANES))


def block_copies(pairs, sems):
    out = []
    for k, (src, dst) in enumerate(pairs):
        cuts = [pl.ds(r, CHUNK) for r in range(0, src.shape[0], CHUNK)]
        out.append(
            [
                pltpu.make_async_copy(src.at[cut], dst.at[cut], sems.at[k, i])
                for i, cut in enumerate(cuts)
            ]
        )
    return out


def cols_kernel(
    scale2, shard, place_ref, own_ref, other_ref, psi_in, col_ref, peak_ref, exp_out, *refs
):
    psi_ref, exp_ref, sem, sems = refs
    copy = pltpu.make_async_copy(psi_in, psi_ref, sem)
    copy.start()
    nz = col_ref.shape[0]
    ncol = psi_ref.shape[0]
    nline = ncol // LANES
    per = CHUNK // shard
    base = place_ref[1].astype(jnp.float32)
    copy.wait()
    psi = psi_ref[...]
    (stores,) = block_copies([(exp_ref, exp_out)], sems)
    col_max = jnp.full((1, ncol), -1e30, jnp.float32)
    col_sum = jnp.zeros((1, ncol), jnp.float32)
    count = jnp.zeros((1, ncol), jnp.float32)
    hit_sum = jnp.zeros((1, ncol), jnp.float32)
    for number, _, first, phi_ref in chunks_of((own_ref, other_ref), shard):
        rows = phi_ref[first : first + per, :shard, :].reshape(CHUNK, -1)
        logits = nt(rows, psi) * scale2
        new_max = jnp.maximum(col_max, jnp.max(logits, axis=0, keepdims=True))
        part = jnp.exp2(logits - new_max)
        exp_ref[number * CHUNK : (number + 1) * CHUNK, :] = part.astype(jnp.bfloat16)
        stores[number].start()
        part = jnp.sum(part, axis=0, keepdims=True)
        col_sum = col_sum * jnp.exp2(col_max - new_max) + part
        col_max = new_max
        for t in range(nline):
            at = number * nline + t
            peak_ref[at : at + 1, :] = new_max[:, t * LANES : (t + 1) * LANES]
        hit = hit_mask(row_places(phi_ref, first, per, shard), base, ncol)
        count = count + jnp.sum(jnp.where(hit, 1.0, 0.0), axis=0, keepdims=True)
        hit_sum = hit_sum + jnp.sum(jnp.where(hit, logits, 0.0), axis=0, keepdims=True)
    col_lse = col_max + jnp.log2(col_sum)
    for k, line in enumerate((col_lse, count, hit_sum)):
        for t in range(nline):
            cut = line[:, t * LANES : (t + 1) * LANES]
            at = k * nline + t
            col_ref[:, at : at + 1, :] = jnp.broadcast_to(cut[None], (nz, 1, LANES))
    for store in stores:
        store.wait()


def tail_rows(value, width):
    terms = jnp.broadcast_to(value, (1, width))
    first = terms.astype(jnp.bfloat16).astype(jnp.float32)
    second = (terms - first).astype(jnp.bfloat16).astype(jnp.float32)
    third = terms - first - second
    row = lax.broadcasted_iota(jnp.int32, (EXTRA, width), 0)
    full = jnp.where(
        row == 0, first, jnp.where(row == 1, second, jnp.where(row == 2, third, 0.0))
    )
    return full.astype(jnp.bfloat16)


def probs_kernel(
    scale, scale2, shard, place_ref, own_ref, other_ref, psi_in, rows_ref, *refs
):
    prob_out, tail_ref, shift_ref, psi_ref, prob_ref, sem, sems = refs
    copy = pltpu.make_async_copy(psi_in, psi_ref, sem)
    copy.start()
    ncol, width = psi_ref.shape
    per = CHUNK // shard
    base = place_ref[1].astype(jnp.float32)
    row_parts = rows_ref[...]
    row_peak = jnp.max(row_parts, axis=0)
    row_lse = row_peak + jnp.log2(jnp.sum(jnp.exp2(row_parts - row_peak[None]), axis=0))
    tail_ref[...] = tail_rows(jnp.sum(row_lse, keepdims=True), width)
    shift_ref[...] = row_lse - math.log2(scale)
    copy.wait()
    psi = psi_ref[...]
    (stores,) = block_copies([(prob_ref, prob_out)], sems)
    chunks = chunks_of((own_ref, other_ref), shard)
    for number, half, first, phi_ref in chunks:
        rows = phi_ref[first : first + per, :shard, :].reshape(CHUNK, width)
        logits = nt(rows, psi) * scale2
        at = line_of(place_ref, number, half, len(chunks))
        lse = jnp.concatenate(
            [to_rows(shift_ref[pl.ds(at + t, 1), :]) for t in range(CHUNK // LANES)],
            axis=0,
        )
        lse = jnp.concatenate([lse] * (ncol // LANES), axis=1)
        hit = hit_mask(row_places(phi_ref, first, per, shard), base, ncol)
        prob = jnp.exp2(logits - lse) - jnp.where(hit, 2.0 * scale, 0.0)
        prob_ref[number * CHUNK : (number + 1) * CHUNK, :] = prob.astype(jnp.bfloat16)
        stores[number].start()
    for store in stores:
        store.wait()


def weights_kernel(scale, shard, cols_ref, peak_ref, psi_in, prob_in, exp_in, *refs):
    gown_ref, gother_ref, w_ref, psi_ref, prob_ref, exp_ref, sem, sems = refs
    copy = pltpu.make_async_copy(psi_in, psi_ref, sem)
    loads = block_copies([(prob_in, prob_ref), (exp_in, exp_ref)], sems)
    loads[0][0].start()
    loads[1][0].start()
    copy.start()
    for pair in zip(loads[0][1:], loads[1][1:]):
        for load in pair:
            load.start()
    ncol, width = psi_ref.shape
    per = CHUNK // shard
    nline = ncol // LANES
    col_parts = cols_ref[:, :nline, :]
    col_peak = jnp.max(col_parts, axis=0)
    col_lse = col_peak + jnp.log2(jnp.sum(jnp.exp2(col_parts - col_peak[None]), axis=0))
    counts = jnp.sum(cols_ref[:, nline : 2 * nline, :], axis=0)
    hits = jnp.sum(cols_ref[:, 2 * nline :, :], axis=0)
    col_total = jnp.sum(counts * col_lse - 2.0 * hits, keepdims=True)
    tail = jnp.broadcast_to(tail_rows(col_total, width)[None], (per, EXTRA, width))
    copy.wait()
    psi = psi_ref[...]
    plane = gown_ref.shape[0]
    for number in range(len(loads[0])):
        cut = slice(number * CHUNK, (number + 1) * CHUNK)
        peak = peak_ref[number * nline : (number + 1) * nline, :]
        factor = counts * scale * jnp.exp2(peak - col_lse)
        factor = jnp.concatenate([factor[t : t + 1] for t in range(nline)], axis=1)
        loads[0][number].wait()
        loads[1][number].wait()
        weights = exp_ref[cut, :].astype(jnp.float32) * factor
        weights = (prob_ref[cut, :].astype(jnp.float32) + weights).astype(jnp.bfloat16)
        w_ref[cut, :] = weights
        part = nn(weights, psi).astype(jnp.bfloat16)
        half, first = divmod(number * per, plane)
        out_ref = gother_ref if half else gown_ref
        out_ref[first : first + per, :shard, :] = part.reshape(per, shard, width)
        out_ref[first : first + per, shard:, :] = tail


def join_kernel(shard, own_ref, other_ref, out_ref):
    npeer, _, width = own_ref.shape
    for k in range(npeer):
        total = own_ref[k].astype(jnp.float32) + other_ref[k].astype(jnp.float32)
        out_ref[k, :shard, :] = total[:shard].astype(jnp.bfloat16)
        if k == 0:
            loss = jnp.zeros((1, LANES), jnp.float32)
            for r in range(3):
                loss = loss + total[shard + r : shard + r + 1, :LANES]
            tail = tail_rows(loss[:, :1], width)
        out_ref[k, shard:, :] = tail


def goals_kernel(shard, place_ref, w_ref, own_ref, other_ref, tail_ref, *refs):
    nz = 1 + len(SHIFTS)
    gpsi_refs = refs[:nz]
    (acc_ref,) = refs[nz:]
    nrow, ncol = w_ref.shape
    own = own_ref[:, :shard, :].reshape(nrow // 2, -1)
    other = other_ref[:, :shard, :].reshape(nrow // 2, -1)
    rows = jnp.concatenate([own, other], axis=0)
    for c in range(ncol // CHUNK):
        cut = slice(c * CHUNK, (c + 1) * CHUNK)
        acc_ref[cut, :] = tn(w_ref[:, cut], rows).astype(jnp.bfloat16)
    own = place_ref[0]
    piece = ncol // nz
    for out, shift in zip(gpsi_refs, (0,) + SHIFTS):
        slot = lax.rem(own + shift, nz)
        out[:piece, :] = acc_ref[pl.ds(pl.multiple_of(slot * piece, piece), piece), :]
        out[piece:, :] = tail_ref[...]


def relay_kernel(*refs):
    out = refs[-1]
    piece = out.shape[0] - EXTRA
    width = out.shape[1]
    total = refs[0][...].astype(jnp.float32)
    for ref in refs[1:-1]:
        total = total + ref[...].astype(jnp.float32)
    out[:piece, :] = total[:piece].astype(jnp.bfloat16)
    loss = jnp.zeros((1, LANES), jnp.float32)
    for r in range(3):
        loss = loss + total[piece + r : piece + r + 1, :LANES]
    out[piece:, :] = tail_rows(loss[:, :1], width)


def total_kernel(nrow, phi_parts_ref, *refs):
    parts = refs[:-3]
    gphi_ref, gpsi_ref, loss_ref = refs[-3:]
    shard = gphi_ref.shape[0]
    piece = gpsi_ref.shape[0]
    total = phi_parts_ref[0].astype(jnp.float32)
    for k in range(1, phi_parts_ref.shape[0]):
        total = total + phi_parts_ref[k].astype(jnp.float32)
    gphi_ref[...] = total[:shard]
    loss = total[shard : shard + 1, :LANES]
    for r in range(1, 3):
        loss = loss + total[shard + r : shard + r + 1, :LANES]
    total = parts[0][...].astype(jnp.float32)
    for part in parts[1:]:
        total = total + part[...].astype(jnp.float32)
    gpsi_ref[...] = total[:piece]
    for r in range(3):
        loss = loss + total[piece + r : piece + r + 1, :LANES]
    loss_ref[...] = loss[:, :1] * (math.log(2.0) / nrow)


def shards(phi, psi, positives):
    shard, width = phi.shape
    piece = psi.shape[0]
    npeer = lax.axis_size(PEERS)
    nz = lax.axis_size("z")
    nrow = npeer * shard
    ncol = nz * piece
    scale = 1.0 / math.sqrt(width)
    scale2 = scale * LOG2E
    peer = lax.axis_index(PEERS)
    place = jnp.stack(
        [lax.axis_index("z"), peer * ncol, lax.axis_index("core")]
    ).astype(jnp.int32)

    def spread(array, axes):
        return lax.all_to_all(array, axes, 0, 0, tiled=True)

    def swap(array):
        return lax.ppermute(array, "core", [(0, 1), (1, 0)])

    def move(array, shift):
        return lax.ppermute(array, "z", [(i, (i + shift) % nz) for i in range(nz)])

    smem = pl.BlockSpec(memory_space=pltpu.SMEM)
    vmem = pl.BlockSpec(memory_space=pltpu.VMEM)
    params = pltpu.CompilerParams(vmem_limit_bytes=VMEM_LIMIT)

    nplane = npeer // 2
    packed = pl.pallas_call(
        pack_kernel,
        out_shape=jax.ShapeDtypeStruct((nplane, shard + EXTRA, width), jnp.bfloat16),
        in_specs=[vmem] * 2,
        out_specs=pl.BlockSpec(memory_space=pl.ANY),
        scratch_shapes=[
            pltpu.VMEM((shard + EXTRA, width), jnp.bfloat16),
            pltpu.SemaphoreType.DMA((nplane,)),
        ],
        compiler_params=params,
        name="pack",
    )(phi, positives.reshape(1, shard))
    own = spread(packed, PLANE)
    near = {0: psi, 2: move(psi, 2), 6: move(psi, 6), 1: move(psi, 1), 7: move(psi, 7)}
    near[3] = move(near[2], 1)
    near[5] = move(near[6], 7)
    near[4] = move(near[2], 2)
    tied = lax.optimization_barrier((own, *[near[k] for k in range(nz)]))
    own = tied[0]
    near = dict(enumerate(tied[1:]))
    other = swap(own)
    goals = [near[k] for k in range(nz)]
    flops = 2 * nrow * ncol * width

    def cost(products):
        return pl.CostEstimate(
            flops=int(products * flops), bytes_accessed=4 << 20, transcendentals=int(products * nrow * ncol)
        )

    anywhere = pl.BlockSpec(memory_space=pl.ANY)
    hbm = pl.BlockSpec(memory_space=pltpu.HBM)
    dma = pltpu.SemaphoreType.DMA
    nchunk = nrow // CHUNK
    psi_scratch = pltpu.VMEM((ncol, width), jnp.bfloat16)
    tile = jax.ShapeDtypeStruct((nrow, ncol), jnp.bfloat16)
    tile_hbm = pltpu.HBM((nrow, ncol), jnp.bfloat16)
    tile_scratch = pltpu.VMEM((nrow, ncol), jnp.bfloat16)
    own_lines, psi_all = pl.pallas_call(
        functools.partial(own_rows_kernel, scale2, shard),
        out_shape=(
            jax.ShapeDtypeStruct((nrow // LANES // 2, LANES), jnp.float32),
            jax.ShapeDtypeStruct((ncol, width), jnp.bfloat16),
        ),
        in_specs=[smem] + [vmem] * (1 + nz),
        out_specs=(vmem, anywhere),
        scratch_shapes=[psi_scratch, dma],
        compiler_params=params,
        cost_estimate=cost(0.5),
        name="own_rows",
    )(place, own, *goals)
    row_stats = pl.pallas_call(
        functools.partial(all_rows_kernel, scale2, shard),
        out_shape=jax.ShapeDtypeStruct((npeer, nrow // LANES, LANES), jnp.float32),
        in_specs=[smem] + [vmem] * 2 + [anywhere],
        out_specs=vmem,
        scratch_shapes=[psi_scratch, dma],
        compiler_params=params,
        cost_estimate=cost(0.5),
        name="all_rows",
    )(place, other, own_lines, psi_all)
    row_parts = spread(row_stats, PEERS)

    col_stats, peaks, exps = pl.pallas_call(
        functools.partial(cols_kernel, scale2, shard),
        out_shape=(
            jax.ShapeDtypeStruct((nz, 3 * ncol // LANES, LANES), jnp.float32),
            jax.ShapeDtypeStruct((nchunk * ncol // LANES, LANES), jnp.float32),
            tile_hbm,
        ),
        in_specs=[smem] + [vmem] * 2 + [anywhere],
        out_specs=(vmem, vmem, hbm),
        scratch_shapes=[psi_scratch, tile_scratch, dma, dma((1, nchunk))],
        compiler_params=params,
        cost_estimate=cost(1),
        name="cols",
    )(place, own, other, psi_all)
    row_parts, col_stats = lax.optimization_barrier((row_parts, col_stats))
    col_parts = spread(col_stats, "z")

    probs, tail = pl.pallas_call(
        functools.partial(probs_kernel, scale, scale2, shard),
        out_shape=(tile_hbm, jax.ShapeDtypeStruct((EXTRA, width), jnp.bfloat16)),
        in_specs=[smem] + [vmem] * 2 + [anywhere, vmem],
        out_specs=(hbm, vmem),
        scratch_shapes=[
            pltpu.VMEM((nrow // LANES, LANES), jnp.float32),
            psi_scratch,
            tile_scratch,
            dma,
            dma((1, nchunk)),
        ],
        compiler_params=params,
        cost_estimate=cost(1),
        name="probs",
    )(place, own, other, psi_all, row_parts)

    half = jax.ShapeDtypeStruct((nplane, shard + EXTRA, width), jnp.bfloat16)
    gown, gother, weights = pl.pallas_call(
        functools.partial(weights_kernel, scale, shard),
        out_shape=(half, half, tile),
        in_specs=[vmem] * 2 + [anywhere, hbm, hbm],
        out_specs=(vmem,) * 3,
        scratch_shapes=[psi_scratch, tile_scratch, tile_scratch, dma, dma((2, nchunk))],
        compiler_params=params,
        cost_estimate=cost(1),
        name="weights",
    )(
        col_parts,
        peaks,
        psi_all,
        pltpu.with_memory_space_constraint(probs, pltpu.HBM),
        pltpu.with_memory_space_constraint(exps, pltpu.HBM),
    )
    part = jax.ShapeDtypeStruct((piece + EXTRA, width), jnp.bfloat16)
    gpsi = pl.pallas_call(
        functools.partial(goals_kernel, shard),
        out_shape=(part,) * nz,
        in_specs=[smem] + [vmem] * 4,
        out_specs=(vmem,) * nz,
        scratch_shapes=[pltpu.VMEM((ncol, width), jnp.bfloat16)],
        compiler_params=params,
        cost_estimate=cost(1),
        name="goals",
    )(place, weights, own, other, tail)

    other_part, *gpsi = lax.optimization_barrier((swap(gother), *gpsi))
    joined = pl.pallas_call(
        functools.partial(join_kernel, shard),
        out_shape=half,
        in_specs=[vmem] * 2,
        out_specs=vmem,
        compiler_params=params,
        name="join",
    )(gown, other_part)
    phi_parts = spread(joined, PLANE)

    def relay(*parts):
        return pl.pallas_call(
            relay_kernel,
            out_shape=part,
            in_specs=[vmem] * len(parts),
            out_specs=vmem,
            compiler_params=params,
            name="relay",
        )(*parts)

    over3, over4, over5 = move(gpsi[3], 1), move(gpsi[4], 2), move(gpsi[5], 7)
    psi_parts = [gpsi[0], move(gpsi[1], 1), move(gpsi[7], 7)]
    psi_parts.append(move(relay(gpsi[2], over3, over4), 2))
    psi_parts.append(move(relay(gpsi[6], over5), 6))

    grad_phi, grad_psi, loss = pl.pallas_call(
        functools.partial(total_kernel, nrow * nz),
        out_shape=(
            jax.ShapeDtypeStruct((shard, width), jnp.float32),
            jax.ShapeDtypeStruct((piece, width), jnp.float32),
            jax.ShapeDtypeStruct((1, 1), jnp.float32),
        ),
        in_specs=[vmem] * (1 + len(psi_parts)),
        out_specs=(vmem,) * 3,
        compiler_params=params,
        name="totals",
    )(phi_parts, *psi_parts)
    return (grad_phi, grad_psi, loss.reshape(()))


def solution(mesh):
    nrow, ngoal = mesh.shape["row"], mesh.shape["goal"]
    fine = Mesh(mesh.devices.reshape(nrow // 2, 2, ngoal // 8, 8), ALL)
    return jax.shard_map(
        shards,
        mesh=fine,
        in_specs=(P(ALL, None), P(ALL, None), P(ALL)),
        out_specs=(P(ALL, None), P(ALL, None), P()),
        check_vma=False,
    )
```

time: 140 us -> 113 us (0.81)
  starting transfers between devices: 68.3 us -> 50 us
  local copies, waits for them, and re-layouts: 18.6 us -> 1.49 us
  Pallas kernels: 17.5 us -> 31.1 us
  waiting for transfers between devices: 32 us -> 28.1 us
  other arithmetic: 1.67 us -> 0.08 us
    ppermute x21 -> x14, starting transfers between devices: 45.8 us -> 24.4 us  [move(): return lax.ppermute(array, 'z', [(i, (i + shift) % nz) for i in range(nz)])]
    unnamed x58 -> x6, local copies, waits for them, and re-layouts: 16.5 us -> 1.49 us
    pallas_call x2 -> x10, Pallas kernels: 16.3 us -> 30.2 us  [the longest x1 7.54 us: shards(): pl.pallas_call(functools.partial(cols_kernel, scale2, shard), out_shape=(...]
    ppermute x21 -> x14, waiting for transfers between devices: 32 us -> 23.5 us  [move(): return lax.ppermute(array, 'z', [(i, (i + shift) % nz) for i in range(nz)])]
    all_to_all x3 -> x4, waiting for transfers between devices: 0.01 us -> 4.14 us  [spread(): return lax.all_to_all(array, axes, 0, 0, tiled=True)]
    all_to_all x3 -> x4, starting transfers between devices: 22.5 us -> 25.2 us  [spread(): return lax.all_to_all(array, axes, 0, 0, tiled=True)]
    concatenate x3 -> x0, other arithmetic: 1.59 us -> none  [the longest x1 0.84 us: shards(): block = jnp.concatenate([phi, code], axis=0)]
    broadcast_in_dim x1 -> x0, local copies, waits for them, and re-layouts: 1.54 us -> none  [shards(): rows = spread(jnp.broadcast_to(block[None], (npeer,) + block.shape))]
  transfers between devices with their start and end apart: 24 -> 20, of which waited for: 9 -> 12; matrix products, arithmetic and copies ran while one was open for 0% -> 0% of each run, Pallas kernels for 0% -> 17%
where the time goes in v2:
time: 113 us; the launch traced here: 111 us
  starting transfers between devices  50 us (44%)
  Pallas kernels  31.1 us (28%)
  waiting for transfers between devices  28.1 us (25%)
  local copies, waits for them, and re-layouts  1.49 us (1%)
    all_to_all x4, starting transfers between devices, spread(): return lax.all_to_all(array, axes, 0, 0, tiled=True)  25.2 us
    ppermute x14, starting transfers between devices, move(): return lax.ppermute(array, 'z', [(i, (i + shift) % nz) for i in range(nz)])  24.4 us
    ppermute x14, waiting for transfers between devices, move(): return lax.ppermute(array, 'z', [(i, (i + shift) % nz) for i in range(nz)])  23.5 us
    pallas_call x1, Pallas kernels, shards(): pl.pallas_call(functools.partial(cols_kernel, scale2, shard), out_shape=(...  7.54 us
    pallas_call x1, Pallas kernels, shards(): pl.pallas_call(functools.partial(probs_kernel, scale, scale2, shard), out...  5.01 us
    pallas_call x1, Pallas kernels, shards(): pl.pallas_call(functools.partial(weights_kernel, scale, shard), out_shape...  4.97 us
    all_to_all x4, waiting for transfers between devices, spread(): return lax.all_to_all(array, axes, 0, 0, tiled=True)  4.14 us
    pallas_call x1, Pallas kernels, shards(): pl.pallas_call(functools.partial(all_rows_kernel, scale2, shard), out_sha...  3.83 us
  transfers between devices with their start and end apart: 20, of which 12 were waited for; matrix products, arithmetic and copies ran while one was open for 0% of the time, Pallas kernels for 17%

profile of v2, /device:TPU:8, one launch (start us, length us, event | category | flops | bytes accessed | tf_op | source)
XLA Modules:
  0.0 111.5 jit_solution(16246832538483486696)
XLA Ops:
  0.6 0.0 copy-start
  0.6 0.8 copy-done
  1.5 0.0 copy-start.1
  1.5 0.7 copy-done.1
  2.1 1.2 %pack.1 = bf16[16,72,512]{2,1,0:T(8,128)(2,1)} custom-call(bf16[64,512]{1,0:T(8,128)(2,1)S(1)} %copy-done, s32[1,64]{1,0:T(1,128)S(1)} %bitcast.5), custom_call_target="tpu_custom_call" | custom-call | tf_op jit(solution)/shard_map/pack/pallas_call | solution.py:387
  3.4 0.0 copy-start.2
  3.4 7.5 %all-to-all-start = ((bf16[16,72,512]{2,1,0:T(8,128)(2,1)}), bf16[16,72,512]{2,1,0:T(8,128)(2,1)S(1)}, u32[]{:S(2)}, u32[]{:S(2)}) async-start(bf16[16,72,512]{2,1,0:T(8,128)(2,1)} %pack.1), calls=%async_computation | async-start | bytes 2359296 | tf_op jit(solution)/shard_map/all_to_all | solution.py:374
  10.9 0.0 copy-done.2
  10.9 6.4 %collective-permute-start.4 = (bf16[128,512]{1,0:T(8,128)(2,1)S(1)}, bf16[128,512]{1,0:T(8,128)(2,1)S(1)}, u32[]{:S(2)}, u32[]{:S(2)}) collective-permute-start(bf16[128,512]{1,0:T(8,128)(2,1)S(1)} %copy-done.2), channel_id=1, source_target_pairs={{0,6},{1,7},{2,0},{3,1},{4,2},{5,3},{6,4},{7,5},{8,14},{9,15},{10,... | collective-permute-start | bytes 393224 | tf_op jit(solution)/shard_map/ppermute | solution.py:380
  17.3 0.0 collective-permute-start.1
  17.3 1.0 collective-permute-start
  18.3 2.7 %collective-permute-start.6 = (bf16[128,512]{1,0:T(8,128)(2,1)S(1)}, bf16[128,512]{1,0:T(8,128)(2,1)S(1)}, u32[]{:S(2)}, u32[]{:S(2)}) collective-permute-start(bf16[128,512]{1,0:T(8,128)(2,1)S(1)} %copy-done.2), channel_id=1, source_target_pairs={{0,7},{1,0},{2,1},{3,2},{4,3},{5,4},{6,5},{7,6},{8,15},{9,8},{10,9... | collective-permute-start | bytes 393224 | tf_op jit(solution)/shard_map/ppermute | solution.py:380
  21.0 2.1 %collective-permute-done.4.refs_6_ = bf16[128,512]{1,0:T(8,128)(2,1)S(1)} collective-permute-done((bf16[128,512]{1,0:T(8,128)(2,1)S(1)}, bf16[128,512]{1,0:T(8,128)(2,1)S(1)}, u32[]{:S(2)}, u32[]{:S(2)}) %collective-permute-start.4) | collective-permute-done | bytes 131104 | tf_op jit(solution)/shard_map/ppermute | solution.py:380
  23.1 2.5 %collective-permute-start.5 = (bf16[128,512]{1,0:T(8,128)(2,1)S(1)}, bf16[128,512]{1,0:T(8,128)(2,1)S(1)}, u32[]{:S(2)}, u32[]{:S(2)}) collective-permute-start(bf16[128,512]{1,0:T(8,128)(2,1)S(1)} %collective-permute-done.4.refs_6_), channel_id=1, source_target_pairs={{0,7},{1,0},{2,1},{3,2},{4,3},{5,4},{6,5},{7,6},{8,15},{9,8},{10,9... | collective-permute-start | bytes 393224 | tf_op jit(solution)/shard_map/ppermute | solution.py:380
  25.6 1.8 %collective-permute-done.1.refs_2_ = bf16[128,512]{1,0:T(8,128)(2,1)S(1)} collective-permute-done((bf16[128,512]{1,0:T(8,128)(2,1)S(1)}, bf16[128,512]{1,0:T(8,128)(2,1)S(1)}, u32[]{:S(2)}, u32[]{:S(2)}) %collective-permute-start.1) | collective-permute-done | bytes 131104 | tf_op jit(solution)/shard_map/ppermute | solution.py:380
  27.4 0.0 collective-permute-start.3
  27.4 1.1 collective-permute-start.2
  28.5 0.7 collective-permute-done.refs_1_
  29.2 0.0 collective-permute-done.6.refs_7_
  29.2 0.0 collective-permute-done.5.refs_5_
  29.2 6.7 %collective-permute-done.3.refs_4_ = bf16[128,512]{1,0:T(8,128)(2,1)S(1)} collective-permute-done((bf16[128,512]{1,0:T(8,128)(2,1)S(1)}, bf16[128,512]{1,0:T(8,128)(2,1)S(1)}, u32[]{:S(2)}, u32[]{:S(2)}) %collective-permute-start.3) | collective-permute-done | bytes 131104 | tf_op jit(solution)/shard_map/ppermute | solution.py:380
  35.9 1.5 %collective-permute-done.2.refs_3_ = bf16[128,512]{1,0:T(8,128)(2,1)S(1)} collective-permute-done((bf16[128,512]{1,0:T(8,128)(2,1)S(1)}, bf16[128,512]{1,0:T(8,128)(2,1)S(1)}, u32[]{:S(2)}, u32[]{:S(2)}) %collective-permute-start.2) | collective-permute-done | bytes 131104 | tf_op jit(solution)/shard_map/ppermute | solution.py:380
  37.4 0.0 all-to-all-done.phi_ref.own_ref
  37.4 0.0 collective-permute-start.7
  37.4 0.1 pad_add_fusion.place_ref
  37.5 2.5 %own_rows.1 = (f32[8,128]{1,0:T(8,128)S(1)}, bf16[1024,512]{1,0:T(8,128)(2,1)S(1)}) custom-call(s32[3]{0:T(128)S(1)} %pad_add_fusion.place_ref, bf16[16,72,512]{2,1,0:T(8,128)(2,1)S(1)} %all-to-all-done.phi_ref.own_ref, bf16[128,512]{1,0:T(8,128)(2,1)S(1)} %copy-done.2, bf16[128,512]{1,0:T(8,128)(2,1)S(1)} %collective-permute-done.refs_1_, ...), custom_call_target="tpu_custom_call" | custom-call | flops 1073741824 | bytes 4194304 | tf_op jit(solution)/shard_map/own_rows/pallas_call | solution.py:424
  40.0 0.4 collective-permute-done.7.phi_ref.other_ref
  40.4 3.8 %all_rows.1 = f32[32,16,128]{2,1,0:T(8,128)} custom-call(s32[3]{0:T(128)S(1)} %pad_add_fusion.place_ref, bf16[16,72,512]{2,1,0:T(8,128)(2,1)} %collective-permute-done.7.phi_ref.other_ref, f32[8,128]{1,0:T(8,128)S(1)} %get-tuple-element.53.line_ref, bf16[1024,512]{1,0:T(8,128)(2,1)S(1)} %get-tuple-element.54.psi_in), custom_call_target="tpu_custom_call" | custom-call | flops 1073741824 | bytes 4194304 | tf_op jit(solution)/shard_map/all_rows/pallas_call | solution.py:437
  44.2 7.4 %all-to-all-start.1 = ((f32[32,16,128]{2,1,0:T(8,128)}), f32[32,16,128]{2,1,0:T(8,128)S(1)}, u32[]{:S(2)}, u32[]{:S(2)}) async-start(f32[32,16,128]{2,1,0:T(8,128)} %all_rows.1), calls=%async_computation.1 | async-start | bytes 524288 | tf_op jit(solution)/shard_map/all_to_all | solution.py:374
  51.6 7.5 %cols.1 = (f32[8,24,128]{2,1,0:T(8,128)}, f32[64,128]{1,0:T(8,128)S(1)}, bf16[2048,1024]{1,0:T(8,128)(2,1)}) custom-call(s32[3]{0:T(128)S(1)} %pad_add_fusion.place_ref, bf16[16,72,512]{2,1,0:T(8,128)(2,1)S(1)} %all-to-all-done.phi_ref.own_ref, bf16[16,72,512]{2,1,0:T(8,128)(2,1)} %collective-permute-done.7.phi_ref.other_ref, ...), custom_call_target="tpu_custom_call" | custom-call | flops 2147483648 | bytes 4194304 | tf_op jit(solution)/shard_map/cols/pallas_call | solution.py:449
  59.2 0.1 all-to-all-done.1.rows_ref
  59.3 3.4 %all-to-all-start.2 = ((f32[8,24,128]{2,1,0:T(8,128)}), f32[8,24,128]{2,1,0:T(8,128)S(1)}, u32[]{:S(2)}, u32[]{:S(2)}) async-start(f32[8,24,128]{2,1,0:T(8,128)} %get-tuple-element.56), calls=%async_computation.2 | async-start | bytes 196608 | tf_op jit(solution)/shard_map/all_to_all | solution.py:374
  62.6 5.0 %probs.1 = (bf16[2048,1024]{1,0:T(8,128)(2,1)}, bf16[8,512]{1,0:T(8,128)(2,1)S(1)}) custom-call(s32[3]{0:T(128)S(1)} %pad_add_fusion.place_ref, bf16[16,72,512]{2,1,0:T(8,128)(2,1)S(1)} %all-to-all-done.phi_ref.own_ref, bf16[16,72,512]{2,1,0:T(8,128)(2,1)} %collective-permute-done.7.phi_ref.other_ref, bf16[1024,512]{1,0:T(8,128)(2,1)S(1)} %get-tuple-element.54.psi_in, ...), custom_call_target="tpu_custom_call" | custom-call | flops 2147483648 | bytes 4194304 | tf_op jit(solution)/shard_map/probs/pallas_call | solution.py:466
  67.7 4.1 %all-to-all-done.2.cols_ref = f32[8,24,128]{2,1,0:T(8,128)S(1)} async-done(((f32[8,24,128]{2,1,0:T(8,128)}), f32[8,24,128]{2,1,0:T(8,128)S(1)}, u32[]{:S(2)}, u32[]{:S(2)}) %all-to-all-start.2) | async-done | bytes 98336 | tf_op jit(solution)/shard_map/all_to_all | solution.py:374
  71.7 5.0 %weights.1 = (bf16[16,72,512]{2,1,0:T(8,128)(2,1)S(1)}, bf16[16,72,512]{2,1,0:T(8,128)(2,1)S(1)}, bf16[2048,1024]{1,0:T(8,128)(2,1)S(1)}) custom-call(f32[8,24,128]{2,1,0:T(8,128)S(1)} %all-to-all-done.2.cols_ref, f32[64,128]{1,0:T(8,128)S(1)} %get-tuple-element.57.peak_ref, bf16[1024,512]{1,0:T(8,128)(2,1)S(1)} %get-tuple-element.54.psi_in, ...), custom_call_target="tpu_custom_call" | custom-call | flops 2147483648 | bytes 4194304 | tf_op jit(solution)/shard_map/weights/pallas_call | solution.py:484
  76.7 0.3 collective-permute-start.8
  77.0 3.7 %goals.1 = (bf16[136,512]{1,0:T(8,128)(2,1)S(1)}, bf16[136,512]{1,0:T(8,128)(2,1)S(1)}, bf16[136,512]{1,0:T(8,128)(2,1)S(1)}, bf16[136,512]{1,0:T(8,128)(2,1)S(1...) custom-call(s32[3]{0:T(128)S(1)} %pad_add_fusion.place_ref, ...), custom_call_target="tpu_custom_call" | custom-call | flops 2147483648 | bytes 4194304 | tf_op jit(solution)/shard_map/goals/pallas_call | solution.py:501
  80.7 0.0 collective-permute-done.8.other_ref
  80.7 1.3 %join.1 = bf16[16,72,512]{2,1,0:T(8,128)(2,1)} custom-call(bf16[16,72,512]{2,1,0:T(8,128)(2,1)S(1)} %get-tuple-element.61.own_ref, bf16[16,72,512]{2,1,0:T(8,128)(2,1)S(1)} %collective-permute-done.8.other_ref), custom_call_target="tpu_custom_call" | custom-call | tf_op jit(solution)/shard_map/join/pallas_call | solution.py:513
  82.0 6.9 %all-to-all-start.3 = ((bf16[16,72,512]{2,1,0:T(8,128)(2,1)}), bf16[16,72,512]{2,1,0:T(8,128)(2,1)S(1)}, u32[]{:S(2)}, u32[]{:S(2)}) async-start(bf16[16,72,512]{2,1,0:T(8,128)(2,1)} %join.1), calls=%async_computation.3 | async-start | bytes 2359296 | tf_op jit(solution)/shard_map/all_to_all | solution.py:374
  88.9 0.6 collective-permute-start.11
  89.5 0.4 collective-permute-start.12
  90.0 2.3 %collective-permute-start.14 = (bf16[136,512]{1,0:T(8,128)(2,1)S(1)}, bf16[136,512]{1,0:T(8,128)(2,1)S(1)}, u32[]{:S(2)}, u32[]{:S(2)}) collective-permute-start(bf16[136,512]{1,0:T(8,128)(2,1)S(1)} %get-tuple-element.81), channel_id=1, source_target_pairs={{0,7},{1,0},{2,1},{3,2},{4,3},{5,4},{6,5},{7,6},{8,15},{9,8},{10,9... | collective-permute-start | bytes 417800 | tf_op jit(solution)/shard_map/ppermute | solution.py:380
  92.3 0.0 collective-permute-start.9
  92.3 3.2 %collective-permute-start.10 = (bf16[136,512]{1,0:T(8,128)(2,1)S(1)}, bf16[136,512]{1,0:T(8,128)(2,1)S(1)}, u32[]{:S(2)}, u32[]{:S(2)}) collective-permute-start(bf16[136,512]{1,0:T(8,128)(2,1)S(1)} %get-tuple-element.76), channel_id=1, source_target_pairs={{0,7},{1,0},{2,1},{3,2},{4,3},{5,4},{6,5},{7,6},{8,15},{9,8},{10,9... | collective-permute-start | bytes 417800 | tf_op jit(solution)/shard_map/ppermute | solution.py:380
  95.5 3.7 %collective-permute-done.11.refs_1_ = bf16[136,512]{1,0:T(8,128)(2,1)S(1)} collective-permute-done((bf16[136,512]{1,0:T(8,128)(2,1)S(1)}, bf16[136,512]{1,0:T(8,128)(2,1)S(1)}, u32[]{:S(2)}, u32[]{:S(2)}) %collective-permute-start.11) | collective-permute-done | bytes 139296 | tf_op jit(solution)/shard_map/ppermute | solution.py:380
  99.2 1.7 %collective-permute-done.12.refs_2_ = bf16[136,512]{1,0:T(8,128)(2,1)S(1)} collective-permute-done((bf16[136,512]{1,0:T(8,128)(2,1)S(1)}, bf16[136,512]{1,0:T(8,128)(2,1)S(1)}, u32[]{:S(2)}, u32[]{:S(2)}) %collective-permute-start.12) | collective-permute-done | bytes 139296 | tf_op jit(solution)/shard_map/ppermute | solution.py:380
  100.9 0.1 relay.2
  101.0 0.1 collective-permute-start.13
  101.1 0.0 collective-permute-done.14.refs_1_
  101.1 0.1 relay.3
  101.2 4.2 %collective-permute-start.15 = (bf16[136,512]{1,0:T(8,128)(2,1)S(1)}, bf16[136,512]{1,0:T(8,128)(2,1)S(1)}, u32[]{:S(2)}, u32[]{:S(2)}) collective-permute-start(bf16[136,512]{1,0:T(8,128)(2,1)S(1)} %relay.3), channel_id=1, source_target_pairs={{0,6},{1,7},{2,0},{3,1},{4,2},{5,3},{6,4},{7,5},{8,14},{9,15},{10,... | collective-permute-start | bytes 417800 | tf_op jit(solution)/shard_map/ppermute | solution.py:380
  105.4 1.3 %collective-permute-done.9.refs_1_ = bf16[136,512]{1,0:T(8,128)(2,1)S(1)} collective-permute-done((bf16[136,512]{1,0:T(8,128)(2,1)S(1)}, bf16[136,512]{1,0:T(8,128)(2,1)S(1)}, u32[]{:S(2)}, u32[]{:S(2)}) %collective-permute-start.9) | collective-permute-done | bytes 139296 | tf_op jit(solution)/shard_map/ppermute | solution.py:380
  106.7 0.0 collective-permute-done.10.refs_2_
  106.7 3.9 %collective-permute-done.13.refs_3_ = bf16[136,512]{1,0:T(8,128)(2,1)S(1)} collective-permute-done((bf16[136,512]{1,0:T(8,128)(2,1)S(1)}, bf16[136,512]{1,0:T(8,128)(2,1)S(1)}, u32[]{:S(2)}, u32[]{:S(2)}) %collective-permute-start.13) | collective-permute-done | bytes 139296 | tf_op jit(solution)/shard_map/ppermute | solution.py:380
  110.6 0.0 collective-permute-done.15.refs_4_
  110.6 0.0 all-to-all-done.3.phi_parts_ref
  110.6 0.9 totals.1
Async XLA Ops:
  0.6 0.8 copy-start
  1.5 0.7 copy-start.1
  3.4 7.6 %copy-start.2 = (bf16[128,512]{1,0:T(8,128)(2,1)S(1)}, bf16[128,512]{1,0:T(8,128)(2,1)}, u32[]{:S(2)}) copy-start(bf16[128,512]{1,0:T(8,128)(2,1)} %refs_0_) | copy-start | bytes 393220
  3.4 34.0 %all-to-all-start = ((bf16[16,72,512]{2,1,0:T(8,128)(2,1)}), bf16[16,72,512]{2,1,0:T(8,128)(2,1)S(1)}, u32[]{:S(2)}, u32[]{:S(2)}) async-start(bf16[16,72,512]{2,1,0:T(8,128)(2,1)} %pack.1), calls=%async_computation | async-start | bytes 2359296 | tf_op jit(solution)/shard_map/all_to_all | solution.py:374
  10.9 12.2 %collective-permute-start.4 = (bf16[128,512]{1,0:T(8,128)(2,1)S(1)}, bf16[128,512]{1,0:T(8,128)(2,1)S(1)}, u32[]{:S(2)}, u32[]{:S(2)}) collective-permute-start(bf16[128,512]{1,0:T(8,128)(2,1)S(1)} %copy-done.2), channel_id=1, source_target_pairs={{0,6},{1,7},{2,0},{3,1},{4,2},{5,3},{6,4},{7,5},{8,14},{9,15},{10,... | collective-permute-start | bytes 393224 | tf_op jit(solution)/shard_map/ppermute | solution.py:380
  17.3 10.1 %collective-permute-start.1 = (bf16[128,512]{1,0:T(8,128)(2,1)S(1)}, bf16[128,512]{1,0:T(8,128)(2,1)S(1)}, u32[]{:S(2)}, u32[]{:S(2)}) collective-permute-start(bf16[128,512]{1,0:T(8,128)(2,1)S(1)} %copy-done.2), channel_id=1, source_target_pairs={{0,2},{1,3},{2,4},{3,5},{4,6},{5,7},{6,0},{7,1},{8,10},{9,11},{10,... | collective-permute-start | bytes 393224 | tf_op jit(solution)/shard_map/ppermute | solution.py:380
  17.3 11.9 %collective-permute-start = (bf16[128,512]{1,0:T(8,128)(2,1)S(1)}, bf16[128,512]{1,0:T(8,128)(2,1)S(1)}, u32[]{:S(2)}, u32[]{:S(2)}) collective-permute-start(bf16[128,512]{1,0:T(8,128)(2,1)S(1)} %copy-done.2), channel_id=1, source_target_pairs={{0,1},{1,2},{2,3},{3,4},{4,5},{5,6},{6,7},{7,0},{8,9},{9,10},{10,1... | collective-permute-start | bytes 393224 | tf_op jit(solution)/shard_map/ppermute | solution.py:380
  18.3 10.8 %collective-permute-start.6 = (bf16[128,512]{1,0:T(8,128)(2,1)S(1)}, bf16[128,512]{1,0:T(8,128)(2,1)S(1)}, u32[]{:S(2)}, u32[]{:S(2)}) collective-permute-start(bf16[128,512]{1,0:T(8,128)(2,1)S(1)} %copy-done.2), channel_id=1, source_target_pairs={{0,7},{1,0},{2,1},{3,2},{4,3},{5,4},{6,5},{7,6},{8,15},{9,8},{10,9... | collective-permute-start | bytes 393224 | tf_op jit(solution)/shard_map/ppermute | solution.py:380
  23.1 6.1 %collective-permute-start.5 = (bf16[128,512]{1,0:T(8,128)(2,1)S(1)}, bf16[128,512]{1,0:T(8,128)(2,1)S(1)}, u32[]{:S(2)}, u32[]{:S(2)}) collective-permute-start(bf16[128,512]{1,0:T(8,128)(2,1)S(1)} %collective-permute-done.4.refs_6_), channel_id=1, source_target_pairs={{0,7},{1,0},{2,1},{3,2},{4,3},{5,4},{6,5},{7,6},{8,15},{9,8},{10,9... | collective-permute-start | bytes 393224 | tf_op jit(solution)/shard_map/ppermute | solution.py:380
  27.4 8.5 %collective-permute-start.3 = (bf16[128,512]{1,0:T(8,128)(2,1)S(1)}, bf16[128,512]{1,0:T(8,128)(2,1)S(1)}, u32[]{:S(2)}, u32[]{:S(2)}) collective-permute-start(bf16[128,512]{1,0:T(8,128)(2,1)S(1)} %collective-permute-done.1.refs_2_), channel_id=1, source_target_pairs={{0,2},{1,3},{2,4},{3,5},{4,6},{5,7},{6,0},{7,1},{8,10},{9,11},{10,... | collective-permute-start | bytes 393224 | tf_op jit(solution)/shard_map/ppermute | solution.py:380
  27.4 10.0 %collective-permute-start.2 = (bf16[128,512]{1,0:T(8,128)(2,1)S(1)}, bf16[128,512]{1,0:T(8,128)(2,1)S(1)}, u32[]{:S(2)}, u32[]{:S(2)}) collective-permute-start(bf16[128,512]{1,0:T(8,128)(2,1)S(1)} %collective-permute-done.1.refs_2_), channel_id=1, source_target_pairs={{0,1},{1,2},{2,3},{3,4},{4,5},{5,6},{6,7},{7,0},{8,9},{9,10},{10,1... | collective-permute-start | bytes 393224 | tf_op jit(solution)/shard_map/ppermute | solution.py:380
  37.4 3.0 %collective-permute-start.7 = (bf16[16,72,512]{2,1,0:T(8,128)(2,1)S(1)}, bf16[16,72,512]{2,1,0:T(8,128)(2,1)}, u32[]{:S(2)}, u32[]{:S(2)}) collective-permute-start(bf16[16,72,512]{2,1,0:T(8,128)(2,1)S(1)} %all-to-all-done.phi_ref.own_ref), channel_id=1, source_target_pairs={{0,32},{32,0},{1,33},{33,1},{2,34},{34,2},{3,35},{35,3},{4,36},{36... | collective-permute-start | bytes 3538952 | tf_op jit(solution)/shard_map/ppermute | solution.py:377
  44.2 15.0 %all-to-all-start.1 = ((f32[32,16,128]{2,1,0:T(8,128)}), f32[32,16,128]{2,1,0:T(8,128)S(1)}, u32[]{:S(2)}, u32[]{:S(2)}) async-start(f32[32,16,128]{2,1,0:T(8,128)} %all_rows.1), calls=%async_computation.1 | async-start | bytes 524288 | tf_op jit(solution)/shard_map/all_to_all | solution.py:374
  59.3 12.4 %all-to-all-start.2 = ((f32[8,24,128]{2,1,0:T(8,128)}), f32[8,24,128]{2,1,0:T(8,128)S(1)}, u32[]{:S(2)}, u32[]{:S(2)}) async-start(f32[8,24,128]{2,1,0:T(8,128)} %get-tuple-element.56), calls=%async_computation.2 | async-start | bytes 196608 | tf_op jit(solution)/shard_map/all_to_all | solution.py:374
  76.7 4.0 %collective-permute-start.8 = (bf16[16,72,512]{2,1,0:T(8,128)(2,1)S(1)}, bf16[16,72,512]{2,1,0:T(8,128)(2,1)S(1)}, u32[]{:S(2)}, u32[]{:S(2)}) collective-permute-start(bf16[16,72,512]{2,1,0:T(8,128)(2,1)S(1)} %get-tuple-element.62), channel_id=1, source_target_pairs={{0,32},{32,0},{1,33},{33,1},{2,34},{34,2},{3,35},{35,3},{4,36},{36... | collective-permute-start | bytes 3538952 | tf_op jit(solution)/shard_map/ppermute | solution.py:377
  82.0 28.6 %all-to-all-start.3 = ((bf16[16,72,512]{2,1,0:T(8,128)(2,1)}), bf16[16,72,512]{2,1,0:T(8,128)(2,1)S(1)}, u32[]{:S(2)}, u32[]{:S(2)}) async-start(bf16[16,72,512]{2,1,0:T(8,128)(2,1)} %join.1), calls=%async_computation.3 | async-start | bytes 2359296 | tf_op jit(solution)/shard_map/all_to_all | solution.py:374
  88.9 10.3 %collective-permute-start.11 = (bf16[136,512]{1,0:T(8,128)(2,1)S(1)}, bf16[136,512]{1,0:T(8,128)(2,1)S(1)}, u32[]{:S(2)}, u32[]{:S(2)}) collective-permute-start(bf16[136,512]{1,0:T(8,128)(2,1)S(1)} %get-tuple-element.78), channel_id=1, source_target_pairs={{0,1},{1,2},{2,3},{3,4},{4,5},{5,6},{6,7},{7,0},{8,9},{9,10},{10,1... | collective-permute-start | bytes 417800 | tf_op jit(solution)/shard_map/ppermute | solution.py:380
  89.5 11.4 %collective-permute-start.12 = (bf16[136,512]{1,0:T(8,128)(2,1)S(1)}, bf16[136,512]{1,0:T(8,128)(2,1)S(1)}, u32[]{:S(2)}, u32[]{:S(2)}) collective-permute-start(bf16[136,512]{1,0:T(8,128)(2,1)S(1)} %get-tuple-element.79), channel_id=1, source_target_pairs={{0,2},{1,3},{2,4},{3,5},{4,6},{5,7},{6,0},{7,1},{8,10},{9,11},{10,... | collective-permute-start | bytes 417800 | tf_op jit(solution)/shard_map/ppermute | solution.py:380
  90.0 11.1 %collective-permute-start.14 = (bf16[136,512]{1,0:T(8,128)(2,1)S(1)}, bf16[136,512]{1,0:T(8,128)(2,1)S(1)}, u32[]{:S(2)}, u32[]{:S(2)}) collective-permute-start(bf16[136,512]{1,0:T(8,128)(2,1)S(1)} %get-tuple-element.81), channel_id=1, source_target_pairs={{0,7},{1,0},{2,1},{3,2},{4,3},{5,4},{6,5},{7,6},{8,15},{9,8},{10,9... | collective-permute-start | bytes 417800 | tf_op jit(solution)/shard_map/ppermute | solution.py:380
  92.3 14.4 %collective-permute-start.9 = (bf16[136,512]{1,0:T(8,128)(2,1)S(1)}, bf16[136,512]{1,0:T(8,128)(2,1)S(1)}, u32[]{:S(2)}, u32[]{:S(2)}) collective-permute-start(bf16[136,512]{1,0:T(8,128)(2,1)S(1)} %get-tuple-element.75), channel_id=1, source_target_pairs={{0,1},{1,2},{2,3},{3,4},{4,5},{5,6},{6,7},{7,0},{8,9},{9,10},{10,1... | collective-permute-start | bytes 417800 | tf_op jit(solution)/shard_map/ppermute | solution.py:380
  92.3 14.4 %collective-permute-start.10 = (bf16[136,512]{1,0:T(8,128)(2,1)S(1)}, bf16[136,512]{1,0:T(8,128)(2,1)S(1)}, u32[]{:S(2)}, u32[]{:S(2)}) collective-permute-start(bf16[136,512]{1,0:T(8,128)(2,1)S(1)} %get-tuple-element.76), channel_id=1, source_target_pairs={{0,7},{1,0},{2,1},{3,2},{4,3},{5,4},{6,5},{7,6},{8,15},{9,8},{10,9... | collective-permute-start | bytes 417800 | tf_op jit(solution)/shard_map/ppermute | solution.py:380
  101.0 9.6 %collective-permute-start.13 = (bf16[136,512]{1,0:T(8,128)(2,1)S(1)}, bf16[136,512]{1,0:T(8,128)(2,1)S(1)}, u32[]{:S(2)}, u32[]{:S(2)}) collective-permute-start(bf16[136,512]{1,0:T(8,128)(2,1)S(1)} %relay.2), channel_id=1, source_target_pairs={{0,2},{1,3},{2,4},{3,5},{4,6},{5,7},{6,0},{7,1},{8,10},{9,11},{10,... | collective-permute-start | bytes 417800 | tf_op jit(solution)/shard_map/ppermute | solution.py:380
  101.2 9.4 %collective-permute-start.15 = (bf16[136,512]{1,0:T(8,128)(2,1)S(1)}, bf16[136,512]{1,0:T(8,128)(2,1)S(1)}, u32[]{:S(2)}, u32[]{:S(2)}) collective-permute-start(bf16[136,512]{1,0:T(8,128)(2,1)S(1)} %relay.3), channel_id=1, source_target_pairs={{0,6},{1,7},{2,0},{3,1},{4,2},{5,3},{6,4},{7,5},{8,14},{9,15},{10,... | collective-permute-start | bytes 417800 | tf_op jit(solution)/shard_map/ppermute | solution.py:380

commit v3 on v2

--- a/solution.py
+++ b/solution.py
@@ -72,14 +72,21 @@
     )
 
 
-def pack_kernel(phi_ref, pos_ref, out_ref, block_ref, sem):
-    shard, width = phi_ref.shape
-    block_ref[:shard, :] = phi_ref[...]
+def pack_kernel(phi_in, pos_in, out_ref, block_ref, pos_ref, sems, sem):
+    shard, width = phi_in.shape
+    loads = [
+        pltpu.make_async_copy(pos_in, pos_ref, sems.at[0]),
+        pltpu.make_async_copy(phi_in, block_ref.at[:shard], sems.at[1]),
+    ]
+    for load in loads:
+        load.start()
+    loads[0].wait()
     places = pos_ref[...]
     high = lax.shift_right_logical(places, 8)
     code = jnp.concatenate([high, places - high * 256], axis=1).astype(jnp.float32)
     code = jnp.concatenate([code, jnp.zeros((1, width - 2 * shard), jnp.float32)], axis=1)
     block_ref[shard:, :] = jnp.broadcast_to(code, (EXTRA, width)).astype(jnp.bfloat16)
+    loads[1].wait()
     copies = [
         pltpu.make_async_copy(block_ref, out_ref.at[k], sem.at[k])
         for k in range(out_ref.shape[0])
@@ -159,9 +166,8 @@
 
 
 def cols_kernel(
-    scale2, shard, place_ref, own_ref, other_ref, psi_in, col_ref, peak_ref, exp_out, *refs
+    scale2, shard, place_ref, own_ref, other_ref, psi_in, col_ref, peak_ref, psi_ref, sem
 ):
-    psi_ref, exp_ref, sem, sems = refs
     copy = pltpu.make_async_copy(psi_in, psi_ref, sem)
     copy.start()
     nz = col_ref.shape[0]
@@ -169,37 +175,39 @@
     nline = ncol // LANES
     per = CHUNK // shard
     base = place_ref[1].astype(jnp.float32)
+    lane = lax.broadcasted_iota(jnp.int32, (CHUNK, LANES), 1).astype(jnp.float32)
     copy.wait()
     psi = psi_ref[...]
-    (stores,) = block_copies([(exp_ref, exp_out)], sems)
     col_max = jnp.full((1, ncol), -1e30, jnp.float32)
     col_sum = jnp.zeros((1, ncol), jnp.float32)
-    count = jnp.zeros((1, ncol), jnp.float32)
+    count = jnp.zeros((LANES, LANES), jnp.float32)
     hit_sum = jnp.zeros((1, ncol), jnp.float32)
-    for number, _, first, phi_ref in chunks_of((own_ref, other_ref), shard):
+    for _, _, first, phi_ref in chunks_of((own_ref, other_ref), shard):
         rows = phi_ref[first : first + per, :shard, :].reshape(CHUNK, -1)
         logits = nt(rows, psi) * scale2
         new_max = jnp.maximum(col_max, jnp.max(logits, axis=0, keepdims=True))
-        part = jnp.exp2(logits - new_max)
-        exp_ref[number * CHUNK : (number + 1) * CHUNK, :] = part.astype(jnp.bfloat16)
-        stores[number].start()
-        part = jnp.sum(part, axis=0, keepdims=True)
+        part = jnp.sum(jnp.exp2(logits - new_max), axis=0, keepdims=True)
         col_sum = col_sum * jnp.exp2(col_max - new_max) + part
         col_max = new_max
-        for t in range(nline):
-            at = number * nline + t
-            peak_ref[at : at + 1, :] = new_max[:, t * LANES : (t + 1) * LANES]
-        hit = hit_mask(row_places(phi_ref, first, per, shard), base, ncol)
-        count = count + jnp.sum(jnp.where(hit, 1.0, 0.0), axis=0, keepdims=True)
+        places = row_places(phi_ref, first, per, shard)
+        hit = hit_mask(places, base, ncol)
         hit_sum = hit_sum + jnp.sum(jnp.where(hit, logits, 0.0), axis=0, keepdims=True)
+        high = jnp.floor((places - base) * (1.0 / LANES))
+        low = places - base - high * LANES
+        high = jnp.where(high == lane, 1.0, 0.0).astype(jnp.bfloat16)
+        low = jnp.where(low == lane, 1.0, 0.0).astype(jnp.bfloat16)
+        count = count + tn(high, low)
     col_lse = col_max + jnp.log2(col_sum)
-    for k, line in enumerate((col_lse, count, hit_sum)):
+    for k, line in enumerate((col_lse, hit_sum)):
         for t in range(nline):
             cut = line[:, t * LANES : (t + 1) * LANES]
-            at = k * nline + t
+            at = 2 * k * nline + t
             col_ref[:, at : at + 1, :] = jnp.broadcast_to(cut[None], (nz, 1, LANES))
-    for store in stores:
-        store.wait()
+    for t in range(nline):
+        peak_ref[t : t + 1, :] = col_max[:, t * LANES : (t + 1) * LANES]
+    col_ref[:, nline : 2 * nline, :] = jnp.broadcast_to(
+        count[None, :nline, :], (nz, nline, LANES)
+    )
 
 
 def tail_rows(value, width):
@@ -215,9 +223,9 @@
 
 
 def probs_kernel(
-    scale, scale2, shard, place_ref, own_ref, other_ref, psi_in, rows_ref, *refs
+    scale, scale2, shard, place_ref, own_ref, other_ref, psi_in, rows_ref, peak_ref, *refs
 ):
-    prob_out, tail_ref, shift_ref, psi_ref, prob_ref, sem, sems = refs
+    prob_out, exp_out, tail_ref, shift_ref, psi_ref, prob_ref, exp_ref, sem, sems = refs
     copy = pltpu.make_async_copy(psi_in, psi_ref, sem)
     copy.start()
     ncol, width = psi_ref.shape
@@ -230,7 +238,8 @@
     shift_ref[...] = row_lse - math.log2(scale)
     copy.wait()
     psi = psi_ref[...]
-    (stores,) = block_copies([(prob_ref, prob_out)], sems)
+    prob_stores, exp_stores = block_copies([(prob_ref, prob_out), (exp_ref, exp_out)], sems)
+    peak = jnp.concatenate([peak_ref[t : t + 1] for t in range(ncol // LANES)], axis=1)
     chunks = chunks_of((own_ref, other_ref), shard)
     for number, half, first, phi_ref in chunks:
         rows = phi_ref[first : first + per, :shard, :].reshape(CHUNK, width)
@@ -244,8 +253,11 @@
         hit = hit_mask(row_places(phi_ref, first, per, shard), base, ncol)
         prob = jnp.exp2(logits - lse) - jnp.where(hit, 2.0 * scale, 0.0)
         prob_ref[number * CHUNK : (number + 1) * CHUNK, :] = prob.astype(jnp.bfloat16)
-        stores[number].start()
-    for store in stores:
+        prob_stores[number].start()
+        part = jnp.exp2(logits - peak).astype(jnp.bfloat16)
+        exp_ref[number * CHUNK : (number + 1) * CHUNK, :] = part
+        exp_stores[number].start()
+    for store in prob_stores + exp_stores:
         store.wait()
 
 
@@ -269,14 +281,13 @@
     hits = jnp.sum(cols_ref[:, 2 * nline :, :], axis=0)
     col_total = jnp.sum(counts * col_lse - 2.0 * hits, keepdims=True)
     tail = jnp.broadcast_to(tail_rows(col_total, width)[None], (per, EXTRA, width))
+    factor = counts * scale * jnp.exp2(peak_ref[...] - col_lse)
+    factor = jnp.concatenate([factor[t : t + 1] for t in range(nline)], axis=1)
     copy.wait()
     psi = psi_ref[...]
     plane = gown_ref.shape[0]
     for number in range(len(loads[0])):
         cut = slice(number * CHUNK, (number + 1) * CHUNK)
-        peak = peak_ref[number * nline : (number + 1) * nline, :]
-        factor = counts * scale * jnp.exp2(peak - col_lse)
-        factor = jnp.concatenate([factor[t : t + 1] for t in range(nline)], axis=1)
         loads[0][number].wait()
         loads[1][number].wait()
         weights = exp_ref[cut, :].astype(jnp.float32) * factor
@@ -321,13 +332,15 @@
         out[piece:, :] = tail_ref[...]
 
 
-def relay_kernel(*refs):
+def relay_kernel(parity, place_ref, *refs):
     out = refs[-1]
     piece = out.shape[0] - EXTRA
     width = out.shape[1]
     total = refs[0][...].astype(jnp.float32)
-    for ref in refs[1:-1]:
+    for ref in refs[1:-2]:
         total = total + ref[...].astype(jnp.float32)
+    counts = lax.rem(place_ref[0], 2) == parity
+    total = total + jnp.where(counts, refs[-2][...].astype(jnp.float32), 0.0)
     out[:piece, :] = total[:piece].astype(jnp.bfloat16)
     loss = jnp.zeros((1, LANES), jnp.float32)
     for r in range(3):
@@ -381,26 +394,34 @@
 
     smem = pl.BlockSpec(memory_space=pltpu.SMEM)
     vmem = pl.BlockSpec(memory_space=pltpu.VMEM)
+    hbm = pl.BlockSpec(memory_space=pltpu.HBM)
     params = pltpu.CompilerParams(vmem_limit_bytes=VMEM_LIMIT)
 
     nplane = npeer // 2
     packed = pl.pallas_call(
         pack_kernel,
-        out_shape=jax.ShapeDtypeStruct((nplane, shard + EXTRA, width), jnp.bfloat16),
-        in_specs=[vmem] * 2,
-        out_specs=pl.BlockSpec(memory_space=pl.ANY),
+        out_shape=pltpu.HBM((nplane, shard + EXTRA, width), jnp.bfloat16),
+        in_specs=[hbm] * 2,
+        out_specs=hbm,
         scratch_shapes=[
             pltpu.VMEM((shard + EXTRA, width), jnp.bfloat16),
+            pltpu.VMEM((1, shard), jnp.int32),
+            pltpu.SemaphoreType.DMA((2,)),
             pltpu.SemaphoreType.DMA((nplane,)),
         ],
         compiler_params=params,
         name="pack",
-    )(phi, positives.reshape(1, shard))
+    )(
+        pltpu.with_memory_space_constraint(phi, pltpu.HBM),
+        pltpu.with_memory_space_constraint(positives.reshape(1, shard), pltpu.HBM),
+    )
     own = spread(packed, PLANE)
     near = {0: psi, 2: move(psi, 2), 6: move(psi, 6), 1: move(psi, 1), 7: move(psi, 7)}
     near[3] = move(near[2], 1)
     near[5] = move(near[6], 7)
-    near[4] = move(near[2], 2)
+    even = lax.rem(lax.axis_index("z"), 2) == 0
+    across = [(i, (i + (2 if i % 2 == 0 else 6)) % nz) for i in range(nz)]
+    near[4] = lax.ppermute(jnp.where(even, near[2], near[6]), "z", across)
     tied = lax.optimization_barrier((own, *[near[k] for k in range(nz)]))
     own = tied[0]
     near = dict(enumerate(tied[1:]))
@@ -414,7 +435,6 @@
         )
 
     anywhere = pl.BlockSpec(memory_space=pl.ANY)
-    hbm = pl.BlockSpec(memory_space=pltpu.HBM)
     dma = pltpu.SemaphoreType.DMA
     nchunk = nrow // CHUNK
     psi_scratch = pltpu.VMEM((ncol, width), jnp.bfloat16)
@@ -446,16 +466,15 @@
     )(place, other, own_lines, psi_all)
     row_parts = spread(row_stats, PEERS)
 
-    col_stats, peaks, exps = pl.pallas_call(
+    col_stats, peaks = pl.pallas_call(
         functools.partial(cols_kernel, scale2, shard),
         out_shape=(
             jax.ShapeDtypeStruct((nz, 3 * ncol // LANES, LANES), jnp.float32),
-            jax.ShapeDtypeStruct((nchunk * ncol // LANES, LANES), jnp.float32),
-            tile_hbm,
+            jax.ShapeDtypeStruct((ncol // LANES, LANES), jnp.float32),
         ),
         in_specs=[smem] + [vmem] * 2 + [anywhere],
-        out_specs=(vmem, vmem, hbm),
-        scratch_shapes=[psi_scratch, tile_scratch, dma, dma((1, nchunk))],
+        out_specs=(vmem, vmem),
+        scratch_shapes=[psi_scratch, dma],
         compiler_params=params,
         cost_estimate=cost(1),
         name="cols",
@@ -463,22 +482,23 @@
     row_parts, col_stats = lax.optimization_barrier((row_parts, col_stats))
     col_parts = spread(col_stats, "z")
 
-    probs, tail = pl.pallas_call(
+    probs, exps, tail = pl.pallas_call(
         functools.partial(probs_kernel, scale, scale2, shard),
-        out_shape=(tile_hbm, jax.ShapeDtypeStruct((EXTRA, width), jnp.bfloat16)),
-        in_specs=[smem] + [vmem] * 2 + [anywhere, vmem],
-        out_specs=(hbm, vmem),
+        out_shape=(tile_hbm, tile_hbm, jax.ShapeDtypeStruct((EXTRA, width), jnp.bfloat16)),
+        in_specs=[smem] + [vmem] * 2 + [anywhere, vmem, vmem],
+        out_specs=(hbm, hbm, vmem),
         scratch_shapes=[
             pltpu.VMEM((nrow // LANES, LANES), jnp.float32),
             psi_scratch,
             tile_scratch,
+            tile_scratch,
             dma,
-            dma((1, nchunk)),
+            dma((2, nchunk)),
         ],
         compiler_params=params,
         cost_estimate=cost(1),
         name="probs",
-    )(place, own, other, psi_all, row_parts)
+    )(place, own, other, psi_all, row_parts, peaks)
 
     half = jax.ShapeDtypeStruct((nplane, shard + EXTRA, width), jnp.bfloat16)
     gown, gother, weights = pl.pallas_call(
@@ -520,20 +540,21 @@
     )(gown, other_part)
     phi_parts = spread(joined, PLANE)
 
-    def relay(*parts):
+    def relay(parity, *parts):
         return pl.pallas_call(
-            relay_kernel,
+            functools.partial(relay_kernel, parity),
             out_shape=part,
-            in_specs=[vmem] * len(parts),
+            in_specs=[smem] + [vmem] * len(parts),
             out_specs=vmem,
             compiler_params=params,
             name="relay",
-        )(*parts)
-
-    over3, over4, over5 = move(gpsi[3], 1), move(gpsi[4], 2), move(gpsi[5], 7)
+        )(place, *parts)
+
+    over3, over5 = move(gpsi[3], 1), move(gpsi[5], 7)
+    over4 = lax.ppermute(gpsi[4], "z", across)
     psi_parts = [gpsi[0], move(gpsi[1], 1), move(gpsi[7], 7)]
-    psi_parts.append(move(relay(gpsi[2], over3, over4), 2))
-    psi_parts.append(move(relay(gpsi[6], over5), 6))
+    psi_parts.append(move(relay(0, gpsi[2], over3, over4), 2))
+    psi_parts.append(move(relay(1, gpsi[6], over5, over4), 6))
 
     grad_phi, grad_psi, loss = pl.pallas_call(
         functools.partial(total_kernel, nrow * nz),

time: 113 us -> 107 us (0.947)
  waiting for transfers between devices: 28.1 us -> 22.6 us
  Pallas kernels: 31.1 us -> 32.7 us
  local copies, waits for them, and re-layouts: 1.49 us -> 0.01 us
    ppermute x14 -> x12, waiting for transfers between devices: 23.5 us -> 14.1 us  [move(): return lax.ppermute(array, 'z', [(i, (i + shift) % nz) for i in range(nz)])]
    ppermute x0 -> x2, waiting for transfers between devices: none -> 3.64 us  [the longest x1 3.63 us: shards(): near[4] = lax.ppermute(jnp.where(even, near[2], near[6]), 'z', across)]
    pallas_call x3, Pallas kernels: 1.41 us -> 3.31 us  [the longest x1 2.04 us: shards(): pl.pallas_call(pack_kernel, out_shape=pltpu.HBM((nplane, shard + EXTRA, w...]
    pallas_call x1, Pallas kernels: 7.54 us -> 6.04 us  [shards(): pl.pallas_call(functools.partial(cols_kernel, scale2, shard), out_shape=(...]
    unnamed x6 -> x2, local copies, waits for them, and re-layouts: 1.49 us -> 0.01 us
    ppermute x0 -> x2, starting transfers between devices: none -> 1.28 us  [the longest x1 1.2 us: shards(): over4 = lax.ppermute(gpsi[4], 'z', across)]
    ppermute x14 -> x12, starting transfers between devices: 24.4 us -> 24.1 us  [move(): return lax.ppermute(array, 'z', [(i, (i + shift) % nz) for i in range(nz)])]
  transfers between devices with their start and end apart: 20 -> 20, of which waited for: 12 -> 12; matrix products, arithmetic and copies ran while one was open for 0% -> 0% of each run, Pallas kernels for 17% -> 18%
where the time goes in v3:
time: 107 us; the launch traced here: 106 us
  starting transfers between devices  50 us (47%)
  Pallas kernels  32.7 us (31%)
  waiting for transfers between devices  22.6 us (21%)
    all_to_all x4, starting transfers between devices, spread(): return lax.all_to_all(array, axes, 0, 0, tiled=True)  24.3 us
    ppermute x12, starting transfers between devices, move(): return lax.ppermute(array, 'z', [(i, (i + shift) % nz) for i in range(nz)])  24.1 us
    ppermute x12, waiting for transfers between devices, move(): return lax.ppermute(array, 'z', [(i, (i + shift) % nz) for i in range(nz)])  14.1 us
    pallas_call x1, Pallas kernels, shards(): pl.pallas_call(functools.partial(probs_kernel, scale, scale2, shard), out...  6.1 us
    pallas_call x1, Pallas kernels, shards(): pl.pallas_call(functools.partial(cols_kernel, scale2, shard), out_shape=(...  6.04 us
    pallas_call x1, Pallas kernels, shards(): pl.pallas_call(functools.partial(weights_kernel, scale, shard), out_shape...  5.01 us
    all_to_all x4, waiting for transfers between devices, spread(): return lax.all_to_all(array, axes, 0, 0, tiled=True)  4.37 us
    pallas_call x1, Pallas kernels, shards(): pl.pallas_call(functools.partial(all_rows_kernel, scale2, shard), out_sha...  3.84 us
  transfers between devices with their start and end apart: 20, of which 12 were waited for; matrix products, arithmetic and copies ran while one was open for 0% of the time, Pallas kernels for 18%

profile of v3, /device:TPU:8, one launch (start us, length us, event | category | flops | bytes accessed | tf_op | source)
XLA Modules:
  0.0 106.1 jit_solution(13767137087019203770)
XLA Ops:
  0.6 2.0 %pack.1 = bf16[16,72,512]{2,1,0:T(8,128)(2,1)} custom-call(bf16[64,512]{1,0:T(8,128)(2,1)} %phi_in.1, s32[1,64]{1,0:T(1,128)} %bitcast.5), custom_call_target="tpu_custom_call" | custom-call | tf_op jit(solution)/shard_map/pack/pallas_call | solution.py:401
  2.7 0.0 copy-start
  2.7 7.5 %all-to-all-start = ((bf16[16,72,512]{2,1,0:T(8,128)(2,1)}), bf16[16,72,512]{2,1,0:T(8,128)(2,1)S(1)}, u32[]{:S(2)}, u32[]{:S(2)}) async-start(bf16[16,72,512]{2,1,0:T(8,128)(2,1)} %pack.1), calls=%async_computation | async-start | bytes 2359296 | tf_op jit(solution)/shard_map/all_to_all | solution.py:387
  10.2 0.0 copy-done
  10.2 6.4 %collective-permute-start.3 = (bf16[128,512]{1,0:T(8,128)(2,1)S(1)}, bf16[128,512]{1,0:T(8,128)(2,1)S(1)}, u32[]{:S(2)}, u32[]{:S(2)}) collective-permute-start(bf16[128,512]{1,0:T(8,128)(2,1)S(1)} %copy-done), channel_id=1, source_target_pairs={{0,6},{1,7},{2,0},{3,1},{4,2},{5,3},{6,4},{7,5},{8,14},{9,15},{10,... | collective-permute-start | bytes 393224 | tf_op jit(solution)/shard_map/ppermute | solution.py:393
  16.6 0.0 collective-permute-start.1
  16.6 1.0 collective-permute-start
  17.6 2.7 %collective-permute-start.6 = (bf16[128,512]{1,0:T(8,128)(2,1)S(1)}, bf16[128,512]{1,0:T(8,128)(2,1)S(1)}, u32[]{:S(2)}, u32[]{:S(2)}) collective-permute-start(bf16[128,512]{1,0:T(8,128)(2,1)S(1)} %copy-done), channel_id=1, source_target_pairs={{0,7},{1,0},{2,1},{3,2},{4,3},{5,4},{6,5},{7,6},{8,15},{9,8},{10,9... | collective-permute-start | bytes 393224 | tf_op jit(solution)/shard_map/ppermute | solution.py:393
  20.3 2.1 %collective-permute-done.3.refs_6_ = bf16[128,512]{1,0:T(8,128)(2,1)S(1)} collective-permute-done((bf16[128,512]{1,0:T(8,128)(2,1)S(1)}, bf16[128,512]{1,0:T(8,128)(2,1)S(1)}, u32[]{:S(2)}, u32[]{:S(2)}) %collective-permute-start.3) | collective-permute-done | bytes 131104 | tf_op jit(solution)/shard_map/ppermute | solution.py:393
  22.4 2.5 %collective-permute-start.5 = (bf16[128,512]{1,0:T(8,128)(2,1)S(1)}, bf16[128,512]{1,0:T(8,128)(2,1)S(1)}, u32[]{:S(2)}, u32[]{:S(2)}) collective-permute-start(bf16[128,512]{1,0:T(8,128)(2,1)S(1)} %collective-permute-done.3.refs_6_), channel_id=1, source_target_pairs={{0,7},{1,0},{2,1},{3,2},{4,3},{5,4},{6,5},{7,6},{8,15},{9,8},{10,9... | collective-permute-start | bytes 393224 | tf_op jit(solution)/shard_map/ppermute | solution.py:393
  24.9 1.8 %collective-permute-done.1.refs_2_ = bf16[128,512]{1,0:T(8,128)(2,1)S(1)} collective-permute-done((bf16[128,512]{1,0:T(8,128)(2,1)S(1)}, bf16[128,512]{1,0:T(8,128)(2,1)S(1)}, u32[]{:S(2)}, u32[]{:S(2)}) %collective-permute-start.1) | collective-permute-done | bytes 131104 | tf_op jit(solution)/shard_map/ppermute | solution.py:393
  26.7 0.1 collective-permute-start.4
  26.8 2.5 %collective-permute-start.2 = (bf16[128,512]{1,0:T(8,128)(2,1)S(1)}, bf16[128,512]{1,0:T(8,128)(2,1)S(1)}, u32[]{:S(2)}, u32[]{:S(2)}) collective-permute-start(bf16[128,512]{1,0:T(8,128)(2,1)S(1)} %collective-permute-done.1.refs_2_), channel_id=1, source_target_pairs={{0,1},{1,2},{2,3},{3,4},{4,5},{5,6},{6,7},{7,0},{8,9},{9,10},{10,1... | collective-permute-start | bytes 393224 | tf_op jit(solution)/shard_map/ppermute | solution.py:393
  29.3 1.1 %collective-permute-done.refs_1_ = bf16[128,512]{1,0:T(8,128)(2,1)S(1)} collective-permute-done((bf16[128,512]{1,0:T(8,128)(2,1)S(1)}, bf16[128,512]{1,0:T(8,128)(2,1)S(1)}, u32[]{:S(2)}, u32[]{:S(2)}) %collective-permute-start) | collective-permute-done | bytes 131104 | tf_op jit(solution)/shard_map/ppermute | solution.py:393
  30.3 0.0 collective-permute-done.6.refs_7_
  30.4 0.0 collective-permute-done.5.refs_5_
  30.4 3.6 %collective-permute-done.4.refs_4_ = bf16[128,512]{1,0:T(8,128)(2,1)S(1)} collective-permute-done((bf16[128,512]{1,0:T(8,128)(2,1)S(1)}, bf16[128,512]{1,0:T(8,128)(2,1)S(1)}, u32[]{:S(2)}, u32[]{:S(2)}) %collective-permute-start.4) | collective-permute-done | bytes 131104 | tf_op jit(solution)/shard_map/ppermute | solution.py:424
  34.0 0.5 collective-permute-done.2.refs_3_
  34.5 0.0 all-to-all-done.phi_ref.own_ref
  34.5 0.0 collective-permute-start.7
  34.5 0.1 pad_add_fusion.place_ref
  34.6 2.5 %own_rows.1 = (f32[8,128]{1,0:T(8,128)S(1)}, bf16[1024,512]{1,0:T(8,128)(2,1)S(1)}) custom-call(s32[3]{0:T(128)S(1)} %pad_add_fusion.place_ref, bf16[16,72,512]{2,1,0:T(8,128)(2,1)S(1)} %all-to-all-done.phi_ref.own_ref, bf16[128,512]{1,0:T(8,128)(2,1)S(1)} %copy-done, bf16[128,512]{1,0:T(8,128)(2,1)S(1)} %collective-permute-done.refs_1_, ...), custom_call_target="tpu_custom_call" | custom-call | flops 1073741824 | bytes 4194304 | tf_op jit(solution)/shard_map/own_rows/pallas_call | solution.py:444
  37.1 0.4 collective-permute-done.7.phi_ref.other_ref
  37.5 3.8 %all_rows.1 = f32[32,16,128]{2,1,0:T(8,128)} custom-call(s32[3]{0:T(128)S(1)} %pad_add_fusion.place_ref, bf16[16,72,512]{2,1,0:T(8,128)(2,1)} %collective-permute-done.7.phi_ref.other_ref, f32[8,128]{1,0:T(8,128)S(1)} %get-tuple-element.53.line_ref, bf16[1024,512]{1,0:T(8,128)(2,1)S(1)} %get-tuple-element.54.psi_in), custom_call_target="tpu_custom_call" | custom-call | flops 1073741824 | bytes 4194304 | tf_op jit(solution)/shard_map/all_rows/pallas_call | solution.py:457
  41.3 7.3 %all-to-all-start.1 = ((f32[32,16,128]{2,1,0:T(8,128)}), f32[32,16,128]{2,1,0:T(8,128)S(1)}, u32[]{:S(2)}, u32[]{:S(2)}) async-start(f32[32,16,128]{2,1,0:T(8,128)} %all_rows.1), calls=%async_computation.1 | async-start | bytes 524288 | tf_op jit(solution)/shard_map/all_to_all | solution.py:387
  48.6 6.0 %cols.1 = (f32[8,24,128]{2,1,0:T(8,128)}, f32[8,128]{1,0:T(8,128)S(1)}) custom-call(s32[3]{0:T(128)S(1)} %pad_add_fusion.place_ref, bf16[16,72,512]{2,1,0:T(8,128)(2,1)S(1)} %all-to-all-done.phi_ref.own_ref, bf16[16,72,512]{2,1,0:T(8,128)(2,1)} %collective-permute-done.7.phi_ref.other_ref, bf16[1024,512]{1,0:T(8,128)(2,1)S(1)} %get-tuple-element.54.psi_in), custom_call_target="tpu_custom_call" | custom-call | flops 2147483648 | bytes 4194304 | tf_op jit(solution)/shard_map/cols/pallas_call | solution.py:469
  54.7 1.6 %all-to-all-done.1.rows_ref = f32[32,16,128]{2,1,0:T(8,128)S(1)} async-done(((f32[32,16,128]{2,1,0:T(8,128)}), f32[32,16,128]{2,1,0:T(8,128)S(1)}, u32[]{:S(2)}, u32[]{:S(2)}) %all-to-all-start.1) | async-done | bytes 262176 | tf_op jit(solution)/shard_map/all_to_all | solution.py:387
  56.2 3.9 %all-to-all-start.2 = ((f32[8,24,128]{2,1,0:T(8,128)}), f32[8,24,128]{2,1,0:T(8,128)S(1)}, u32[]{:S(2)}, u32[]{:S(2)}) async-start(f32[8,24,128]{2,1,0:T(8,128)} %get-tuple-element.56), calls=%async_computation.2 | async-start | bytes 196608 | tf_op jit(solution)/shard_map/all_to_all | solution.py:387
  60.1 6.1 %probs.1 = (bf16[2048,1024]{1,0:T(8,128)(2,1)}, bf16[2048,1024]{1,0:T(8,128)(2,1)}, bf16[8,512]{1,0:T(8,128)(2,1)S(1)}) custom-call(s32[3]{0:T(128)S(1)} %pad_add_fusion.place_ref, bf16[16,72,512]{2,1,0:T(8,128)(2,1)S(1)} %all-to-all-done.phi_ref.own_ref, bf16[16,72,512]{2,1,0:T(8,128)(2,1)} %collective-permute-done.7.phi_ref.other_ref, ...), custom_call_target="tpu_custom_call" | custom-call | flops 2147483648 | bytes 4194304 | tf_op jit(solution)/shard_map/probs/pallas_call | solution.py:485
  66.2 2.8 %all-to-all-done.2.cols_ref = f32[8,24,128]{2,1,0:T(8,128)S(1)} async-done(((f32[8,24,128]{2,1,0:T(8,128)}), f32[8,24,128]{2,1,0:T(8,128)S(1)}, u32[]{:S(2)}, u32[]{:S(2)}) %all-to-all-start.2) | async-done | bytes 98336 | tf_op jit(solution)/shard_map/all_to_all | solution.py:387
  69.0 5.0 %weights.1 = (bf16[16,72,512]{2,1,0:T(8,128)(2,1)S(1)}, bf16[16,72,512]{2,1,0:T(8,128)(2,1)S(1)}, bf16[2048,1024]{1,0:T(8,128)(2,1)S(1)}) custom-call(f32[8,24,128]{2,1,0:T(8,128)S(1)} %all-to-all-done.2.cols_ref, f32[8,128]{1,0:T(8,128)S(1)} %get-tuple-element.57.peak_ref, bf16[1024,512]{1,0:T(8,128)(2,1)S(1)} %get-tuple-element.54.psi_in, ...), custom_call_target="tpu_custom_call" | custom-call | flops 2147483648 | bytes 4194304 | tf_op jit(solution)/shard_map/weights/pallas_call | solution.py:504
  74.0 0.3 collective-permute-start.8
  74.3 3.7 %goals.1 = (bf16[136,512]{1,0:T(8,128)(2,1)S(1)}, bf16[136,512]{1,0:T(8,128)(2,1)S(1)}, bf16[136,512]{1,0:T(8,128)(2,1)S(1)}, bf16[136,512]{1,0:T(8,128)(2,1)S(1...) custom-call(s32[3]{0:T(128)S(1)} %pad_add_fusion.place_ref, ...), custom_call_target="tpu_custom_call" | custom-call | flops 2147483648 | bytes 4194304 | tf_op jit(solution)/shard_map/goals/pallas_call | solution.py:521
  78.1 0.0 collective-permute-done.8.other_ref
  78.1 1.3 %join.1 = bf16[16,72,512]{2,1,0:T(8,128)(2,1)} custom-call(bf16[16,72,512]{2,1,0:T(8,128)(2,1)S(1)} %get-tuple-element.61.own_ref, bf16[16,72,512]{2,1,0:T(8,128)(2,1)S(1)} %collective-permute-done.8.other_ref), custom_call_target="tpu_custom_call" | custom-call | tf_op jit(solution)/shard_map/join/pallas_call | solution.py:533
  79.3 5.6 %all-to-all-start.3 = ((bf16[16,72,512]{2,1,0:T(8,128)(2,1)}), bf16[16,72,512]{2,1,0:T(8,128)(2,1)S(1)}, u32[]{:S(2)}, u32[]{:S(2)}) async-start(bf16[16,72,512]{2,1,0:T(8,128)(2,1)} %join.1), calls=%async_computation.3 | async-start | bytes 2359296 | tf_op jit(solution)/shard_map/all_to_all | solution.py:387
  85.0 0.5 collective-permute-start.11
  85.4 1.2 %collective-permute-start.12 = (bf16[136,512]{1,0:T(8,128)(2,1)S(1)}, bf16[136,512]{1,0:T(8,128)(2,1)S(1)}, u32[]{:S(2)}, u32[]{:S(2)}) collective-permute-start(bf16[136,512]{1,0:T(8,128)(2,1)S(1)} %get-tuple-element.79), channel_id=1, source_target_pairs={{0,2},{1,7},{2,4},{3,1},{4,6},{5,3},{6,0},{7,5},{8,10},{9,15},{10,... | collective-permute-start | bytes 417800 | tf_op jit(solution)/shard_map/ppermute | solution.py:554
  86.6 1.8 %collective-permute-start.14 = (bf16[136,512]{1,0:T(8,128)(2,1)S(1)}, bf16[136,512]{1,0:T(8,128)(2,1)S(1)}, u32[]{:S(2)}, u32[]{:S(2)}) collective-permute-start(bf16[136,512]{1,0:T(8,128)(2,1)S(1)} %get-tuple-element.81), channel_id=1, source_target_pairs={{0,7},{1,0},{2,1},{3,2},{4,3},{5,4},{6,5},{7,6},{8,15},{9,8},{10,9... | collective-permute-start | bytes 417800 | tf_op jit(solution)/shard_map/ppermute | solution.py:393
  88.4 1.3 %collective-permute-start.9 = (bf16[136,512]{1,0:T(8,128)(2,1)S(1)}, bf16[136,512]{1,0:T(8,128)(2,1)S(1)}, u32[]{:S(2)}, u32[]{:S(2)}) collective-permute-start(bf16[136,512]{1,0:T(8,128)(2,1)S(1)} %get-tuple-element.75), channel_id=1, source_target_pairs={{0,1},{1,2},{2,3},{3,4},{4,5},{5,6},{6,7},{7,0},{8,9},{9,10},{10,1... | collective-permute-start | bytes 417800 | tf_op jit(solution)/shard_map/ppermute | solution.py:393
  89.7 2.0 %collective-permute-start.10 = (bf16[136,512]{1,0:T(8,128)(2,1)S(1)}, bf16[136,512]{1,0:T(8,128)(2,1)S(1)}, u32[]{:S(2)}, u32[]{:S(2)}) collective-permute-start(bf16[136,512]{1,0:T(8,128)(2,1)S(1)} %get-tuple-element.76), channel_id=1, source_target_pairs={{0,7},{1,0},{2,1},{3,2},{4,3},{5,4},{6,5},{7,6},{8,15},{9,8},{10,9... | collective-permute-start | bytes 417800 | tf_op jit(solution)/shard_map/ppermute | solution.py:393
  91.6 4.1 %collective-permute-done.11.refs_1_ = bf16[136,512]{1,0:T(8,128)(2,1)S(1)} collective-permute-done((bf16[136,512]{1,0:T(8,128)(2,1)S(1)}, bf16[136,512]{1,0:T(8,128)(2,1)S(1)}, u32[]{:S(2)}, u32[]{:S(2)}) %collective-permute-start.11) | collective-permute-done | bytes 139296 | tf_op jit(solution)/shard_map/ppermute | solution.py:393
  95.7 0.0 collective-permute-done.12.refs_2_
  95.7 0.6 relay.2
  96.3 0.2 collective-permute-start.13
  96.6 0.6 collective-permute-done.14.refs_1_
  97.2 0.6 relay.3
  97.8 3.4 %collective-permute-start.15 = (bf16[136,512]{1,0:T(8,128)(2,1)S(1)}, bf16[136,512]{1,0:T(8,128)(2,1)S(1)}, u32[]{:S(2)}, u32[]{:S(2)}) collective-permute-start(bf16[136,512]{1,0:T(8,128)(2,1)S(1)} %relay.3), channel_id=1, source_target_pairs={{0,6},{1,7},{2,0},{3,1},{4,2},{5,3},{6,4},{7,5},{8,14},{9,15},{10,... | collective-permute-start | bytes 417800 | tf_op jit(solution)/shard_map/ppermute | solution.py:393
  101.3 0.0 collective-permute-done.9.refs_1_
  101.3 0.0 collective-permute-done.10.refs_2_
  101.3 3.7 %collective-permute-done.13.refs_3_ = bf16[136,512]{1,0:T(8,128)(2,1)S(1)} collective-permute-done((bf16[136,512]{1,0:T(8,128)(2,1)S(1)}, bf16[136,512]{1,0:T(8,128)(2,1)S(1)}, u32[]{:S(2)}, u32[]{:S(2)}) %collective-permute-start.13) | collective-permute-done | bytes 139296 | tf_op jit(solution)/shard_map/ppermute | solution.py:393
  104.9 0.3 collective-permute-done.15.refs_4_
  105.2 0.0 all-to-all-done.3.phi_parts_ref
  105.2 0.9 totals.1
  (1 shorter events, 0.0 us)
Async XLA Ops:
  2.7 7.6 %copy-start = (bf16[128,512]{1,0:T(8,128)(2,1)S(1)}, bf16[128,512]{1,0:T(8,128)(2,1)}, u32[]{:S(2)}) copy-start(bf16[128,512]{1,0:T(8,128)(2,1)} %refs_0_) | copy-start | bytes 393220
  2.7 31.8 %all-to-all-start = ((bf16[16,72,512]{2,1,0:T(8,128)(2,1)}), bf16[16,72,512]{2,1,0:T(8,128)(2,1)S(1)}, u32[]{:S(2)}, u32[]{:S(2)}) async-start(bf16[16,72,512]{2,1,0:T(8,128)(2,1)} %pack.1), calls=%async_computation | async-start | bytes 2359296 | tf_op jit(solution)/shard_map/all_to_all | solution.py:387
  10.2 12.2 %collective-permute-start.3 = (bf16[128,512]{1,0:T(8,128)(2,1)S(1)}, bf16[128,512]{1,0:T(8,128)(2,1)S(1)}, u32[]{:S(2)}, u32[]{:S(2)}) collective-permute-start(bf16[128,512]{1,0:T(8,128)(2,1)S(1)} %copy-done), channel_id=1, source_target_pairs={{0,6},{1,7},{2,0},{3,1},{4,2},{5,3},{6,4},{7,5},{8,14},{9,15},{10,... | collective-permute-start | bytes 393224 | tf_op jit(solution)/shard_map/ppermute | solution.py:393
  16.6 10.1 %collective-permute-start.1 = (bf16[128,512]{1,0:T(8,128)(2,1)S(1)}, bf16[128,512]{1,0:T(8,128)(2,1)S(1)}, u32[]{:S(2)}, u32[]{:S(2)}) collective-permute-start(bf16[128,512]{1,0:T(8,128)(2,1)S(1)} %copy-done), channel_id=1, source_target_pairs={{0,2},{1,3},{2,4},{3,5},{4,6},{5,7},{6,0},{7,1},{8,10},{9,11},{10,... | collective-permute-start | bytes 393224 | tf_op jit(solution)/shard_map/ppermute | solution.py:393
  16.6 13.7 %collective-permute-start = (bf16[128,512]{1,0:T(8,128)(2,1)S(1)}, bf16[128,512]{1,0:T(8,128)(2,1)S(1)}, u32[]{:S(2)}, u32[]{:S(2)}) collective-permute-start(bf16[128,512]{1,0:T(8,128)(2,1)S(1)} %copy-done), channel_id=1, source_target_pairs={{0,1},{1,2},{2,3},{3,4},{4,5},{5,6},{6,7},{7,0},{8,9},{9,10},{10,1... | collective-permute-start | bytes 393224 | tf_op jit(solution)/shard_map/ppermute | solution.py:393
  17.6 12.7 %collective-permute-start.6 = (bf16[128,512]{1,0:T(8,128)(2,1)S(1)}, bf16[128,512]{1,0:T(8,128)(2,1)S(1)}, u32[]{:S(2)}, u32[]{:S(2)}) collective-permute-start(bf16[128,512]{1,0:T(8,128)(2,1)S(1)} %copy-done), channel_id=1, source_target_pairs={{0,7},{1,0},{2,1},{3,2},{4,3},{5,4},{6,5},{7,6},{8,15},{9,8},{10,9... | collective-permute-start | bytes 393224 | tf_op jit(solution)/shard_map/ppermute | solution.py:393
  22.4 7.9 %collective-permute-start.5 = (bf16[128,512]{1,0:T(8,128)(2,1)S(1)}, bf16[128,512]{1,0:T(8,128)(2,1)S(1)}, u32[]{:S(2)}, u32[]{:S(2)}) collective-permute-start(bf16[128,512]{1,0:T(8,128)(2,1)S(1)} %collective-permute-done.3.refs_6_), channel_id=1, source_target_pairs={{0,7},{1,0},{2,1},{3,2},{4,3},{5,4},{6,5},{7,6},{8,15},{9,8},{10,9... | collective-permute-start | bytes 393224 | tf_op jit(solution)/shard_map/ppermute | solution.py:393
  26.7 7.3 %collective-permute-start.4 = (bf16[128,512]{1,0:T(8,128)(2,1)S(1)}, bf16[128,512]{1,0:T(8,128)(2,1)S(1)}, u32[]{:S(2)}, u32[]{:S(2)}) collective-permute-start(bf16[128,512]{1,0:T(8,128)(2,1)S(1)} %broadcast_select_fusion), channel_id=1, source_target_pairs={{0,2},{1,7},{2,4},{3,1},{4,6},{5,3},{6,0},{7,5},{8,10},{9,15},{10,... | collective-permute-start | bytes 393224 | tf_op jit(solution)/shard_map/ppermute | solution.py:424
  26.8 7.7 %collective-permute-start.2 = (bf16[128,512]{1,0:T(8,128)(2,1)S(1)}, bf16[128,512]{1,0:T(8,128)(2,1)S(1)}, u32[]{:S(2)}, u32[]{:S(2)}) collective-permute-start(bf16[128,512]{1,0:T(8,128)(2,1)S(1)} %collective-permute-done.1.refs_2_), channel_id=1, source_target_pairs={{0,1},{1,2},{2,3},{3,4},{4,5},{5,6},{6,7},{7,0},{8,9},{9,10},{10,1... | collective-permute-start | bytes 393224 | tf_op jit(solution)/shard_map/ppermute | solution.py:393
  34.5 3.0 %collective-permute-start.7 = (bf16[16,72,512]{2,1,0:T(8,128)(2,1)S(1)}, bf16[16,72,512]{2,1,0:T(8,128)(2,1)}, u32[]{:S(2)}, u32[]{:S(2)}) collective-permute-start(bf16[16,72,512]{2,1,0:T(8,128)(2,1)S(1)} %all-to-all-done.phi_ref.own_ref), channel_id=1, source_target_pairs={{0,32},{32,0},{1,33},{33,1},{2,34},{34,2},{3,35},{35,3},{4,36},{36... | collective-permute-start | bytes 3538952 | tf_op jit(solution)/shard_map/ppermute | solution.py:390
  41.3 14.9 %all-to-all-start.1 = ((f32[32,16,128]{2,1,0:T(8,128)}), f32[32,16,128]{2,1,0:T(8,128)S(1)}, u32[]{:S(2)}, u32[]{:S(2)}) async-start(f32[32,16,128]{2,1,0:T(8,128)} %all_rows.1), calls=%async_computation.1 | async-start | bytes 524288 | tf_op jit(solution)/shard_map/all_to_all | solution.py:387
  56.2 12.8 %all-to-all-start.2 = ((f32[8,24,128]{2,1,0:T(8,128)}), f32[8,24,128]{2,1,0:T(8,128)S(1)}, u32[]{:S(2)}, u32[]{:S(2)}) async-start(f32[8,24,128]{2,1,0:T(8,128)} %get-tuple-element.56), calls=%async_computation.2 | async-start | bytes 196608 | tf_op jit(solution)/shard_map/all_to_all | solution.py:387
  74.0 4.0 %collective-permute-start.8 = (bf16[16,72,512]{2,1,0:T(8,128)(2,1)S(1)}, bf16[16,72,512]{2,1,0:T(8,128)(2,1)S(1)}, u32[]{:S(2)}, u32[]{:S(2)}) collective-permute-start(bf16[16,72,512]{2,1,0:T(8,128)(2,1)S(1)} %get-tuple-element.62), channel_id=1, source_target_pairs={{0,32},{32,0},{1,33},{33,1},{2,34},{34,2},{3,35},{35,3},{4,36},{36... | collective-permute-start | bytes 3538952 | tf_op jit(solution)/shard_map/ppermute | solution.py:390
  79.3 25.9 %all-to-all-start.3 = ((bf16[16,72,512]{2,1,0:T(8,128)(2,1)}), bf16[16,72,512]{2,1,0:T(8,128)(2,1)S(1)}, u32[]{:S(2)}, u32[]{:S(2)}) async-start(bf16[16,72,512]{2,1,0:T(8,128)(2,1)} %join.1), calls=%async_computation.3 | async-start | bytes 2359296 | tf_op jit(solution)/shard_map/all_to_all | solution.py:387
  85.0 10.7 %collective-permute-start.11 = (bf16[136,512]{1,0:T(8,128)(2,1)S(1)}, bf16[136,512]{1,0:T(8,128)(2,1)S(1)}, u32[]{:S(2)}, u32[]{:S(2)}) collective-permute-start(bf16[136,512]{1,0:T(8,128)(2,1)S(1)} %get-tuple-element.78), channel_id=1, source_target_pairs={{0,1},{1,2},{2,3},{3,4},{4,5},{5,6},{6,7},{7,0},{8,9},{9,10},{10,1... | collective-permute-start | bytes 417800 | tf_op jit(solution)/shard_map/ppermute | solution.py:393
  85.4 10.3 %collective-permute-start.12 = (bf16[136,512]{1,0:T(8,128)(2,1)S(1)}, bf16[136,512]{1,0:T(8,128)(2,1)S(1)}, u32[]{:S(2)}, u32[]{:S(2)}) collective-permute-start(bf16[136,512]{1,0:T(8,128)(2,1)S(1)} %get-tuple-element.79), channel_id=1, source_target_pairs={{0,2},{1,7},{2,4},{3,1},{4,6},{5,3},{6,0},{7,5},{8,10},{9,15},{10,... | collective-permute-start | bytes 417800 | tf_op jit(solution)/shard_map/ppermute | solution.py:554
  86.6 10.6 %collective-permute-start.14 = (bf16[136,512]{1,0:T(8,128)(2,1)S(1)}, bf16[136,512]{1,0:T(8,128)(2,1)S(1)}, u32[]{:S(2)}, u32[]{:S(2)}) collective-permute-start(bf16[136,512]{1,0:T(8,128)(2,1)S(1)} %get-tuple-element.81), channel_id=1, source_target_pairs={{0,7},{1,0},{2,1},{3,2},{4,3},{5,4},{6,5},{7,6},{8,15},{9,8},{10,9... | collective-permute-start | bytes 417800 | tf_op jit(solution)/shard_map/ppermute | solution.py:393
  88.4 12.9 %collective-permute-start.9 = (bf16[136,512]{1,0:T(8,128)(2,1)S(1)}, bf16[136,512]{1,0:T(8,128)(2,1)S(1)}, u32[]{:S(2)}, u32[]{:S(2)}) collective-permute-start(bf16[136,512]{1,0:T(8,128)(2,1)S(1)} %get-tuple-element.75), channel_id=1, source_target_pairs={{0,1},{1,2},{2,3},{3,4},{4,5},{5,6},{6,7},{7,0},{8,9},{9,10},{10,1... | collective-permute-start | bytes 417800 | tf_op jit(solution)/shard_map/ppermute | solution.py:393
  89.7 11.6 %collective-permute-start.10 = (bf16[136,512]{1,0:T(8,128)(2,1)S(1)}, bf16[136,512]{1,0:T(8,128)(2,1)S(1)}, u32[]{:S(2)}, u32[]{:S(2)}) collective-permute-start(bf16[136,512]{1,0:T(8,128)(2,1)S(1)} %get-tuple-element.76), channel_id=1, source_target_pairs={{0,7},{1,0},{2,1},{3,2},{4,3},{5,4},{6,5},{7,6},{8,15},{9,8},{10,9... | collective-permute-start | bytes 417800 | tf_op jit(solution)/shard_map/ppermute | solution.py:393
  96.3 8.6 %collective-permute-start.13 = (bf16[136,512]{1,0:T(8,128)(2,1)S(1)}, bf16[136,512]{1,0:T(8,128)(2,1)S(1)}, u32[]{:S(2)}, u32[]{:S(2)}) collective-permute-start(bf16[136,512]{1,0:T(8,128)(2,1)S(1)} %relay.2), channel_id=1, source_target_pairs={{0,2},{1,3},{2,4},{3,5},{4,6},{5,7},{6,0},{7,1},{8,10},{9,11},{10,... | collective-permute-start | bytes 417800 | tf_op jit(solution)/shard_map/ppermute | solution.py:393
  97.8 7.4 %collective-permute-start.15 = (bf16[136,512]{1,0:T(8,128)(2,1)S(1)}, bf16[136,512]{1,0:T(8,128)(2,1)S(1)}, u32[]{:S(2)}, u32[]{:S(2)}) collective-permute-start(bf16[136,512]{1,0:T(8,128)(2,1)S(1)} %relay.3), channel_id=1, source_target_pairs={{0,6},{1,7},{2,0},{3,1},{4,2},{5,3},{6,4},{7,5},{8,14},{9,15},{10,... | collective-permute-start | bytes 417800 | tf_op jit(solution)/shard_map/ppermute | solution.py:393

commit v4 on v3

--- a/solution.py
+++ b/solution.py
@@ -138,14 +138,11 @@
 
 
 def all_rows_kernel(
-    scale2, shard, place_ref, phi_ref, line_ref, psi_in, row_ref, psi_ref, sem
+    scale2, shard, place_ref, phi_ref, line_ref, psi_ref, row_ref
 ):
-    copy = pltpu.make_async_copy(psi_in, psi_ref, sem)
-    copy.start()
     count = line_ref.shape[0]
     npeer = row_ref.shape[0]
     core = place_ref[2]
-    copy.wait()
     lines = row_lines(scale2, shard, phi_ref, psi_ref[...])
     for whose, part in ((core, line_ref[...]), (1 - core, lines)):
         at = pl.multiple_of(whose * count, count)
@@ -223,7 +220,7 @@
 
 
 def probs_kernel(
-    scale, scale2, shard, place_ref, own_ref, other_ref, psi_in, rows_ref, peak_ref, *refs
+    scale, scale2, shard, place_ref, own_ref, other_ref, psi_in, rows_ref, others_ref, peak_ref, *refs
 ):
     prob_out, exp_out, tail_ref, shift_ref, psi_ref, prob_ref, exp_ref, sem, sems = refs
     copy = pltpu.make_async_copy(psi_in, psi_ref, sem)
@@ -231,7 +228,7 @@
     ncol, width = psi_ref.shape
     per = CHUNK // shard
     base = place_ref[1].astype(jnp.float32)
-    row_parts = rows_ref[...]
+    row_parts = jnp.concatenate([rows_ref[...], others_ref[...]], axis=0)
     row_peak = jnp.max(row_parts, axis=0)
     row_lse = row_peak + jnp.log2(jnp.sum(jnp.exp2(row_parts - row_peak[None]), axis=0))
     tail_ref[...] = tail_rows(jnp.sum(row_lse, keepdims=True), width)
@@ -300,8 +297,9 @@
         out_ref[first : first + per, shard:, :] = tail
 
 
-def join_kernel(shard, own_ref, other_ref, out_ref):
+def join_kernel(shard, own_ref, other_ref, out, out_ref, sems):
     npeer, _, width = own_ref.shape
+    copies = []
     for k in range(npeer):
         total = own_ref[k].astype(jnp.float32) + other_ref[k].astype(jnp.float32)
         out_ref[k, :shard, :] = total[:shard].astype(jnp.bfloat16)
@@ -311,6 +309,14 @@
                 loss = loss + total[shard + r : shard + r + 1, :LANES]
             tail = tail_rows(loss[:, :1], width)
         out_ref[k, shard:, :] = tail
+        if k % 4 == 3:
+            cut = pl.ds(k - 3, 4)
+            copies.append(
+                pltpu.make_async_copy(out_ref.at[cut], out.at[cut], sems.at[k // 4])
+            )
+            copies[-1].start()
+    for copy in copies:
+        copy.wait()
 
 
 def goals_kernel(shard, place_ref, w_ref, own_ref, other_ref, tail_ref, *refs):
@@ -417,11 +423,11 @@
     )
     own = spread(packed, PLANE)
     near = {0: psi, 2: move(psi, 2), 6: move(psi, 6), 1: move(psi, 1), 7: move(psi, 7)}
-    near[3] = move(near[2], 1)
-    near[5] = move(near[6], 7)
     even = lax.rem(lax.axis_index("z"), 2) == 0
     across = [(i, (i + (2 if i % 2 == 0 else 6)) % nz) for i in range(nz)]
     near[4] = lax.ppermute(jnp.where(even, near[2], near[6]), "z", across)
+    near[3] = move(near[2], 1)
+    near[5] = move(near[6], 7)
     tied = lax.optimization_barrier((own, *[near[k] for k in range(nz)]))
     own = tied[0]
     near = dict(enumerate(tied[1:]))
@@ -441,30 +447,30 @@
     tile = jax.ShapeDtypeStruct((nrow, ncol), jnp.bfloat16)
     tile_hbm = pltpu.HBM((nrow, ncol), jnp.bfloat16)
     tile_scratch = pltpu.VMEM((nrow, ncol), jnp.bfloat16)
-    own_lines, psi_all = pl.pallas_call(
+    own_lines, psi_all, psi_near = pl.pallas_call(
         functools.partial(own_rows_kernel, scale2, shard),
         out_shape=(
             jax.ShapeDtypeStruct((nrow // LANES // 2, LANES), jnp.float32),
             jax.ShapeDtypeStruct((ncol, width), jnp.bfloat16),
+            jax.ShapeDtypeStruct((ncol, width), jnp.bfloat16),
         ),
         in_specs=[smem] + [vmem] * (1 + nz),
-        out_specs=(vmem, anywhere),
-        scratch_shapes=[psi_scratch, dma],
+        out_specs=(vmem, anywhere, vmem),
+        scratch_shapes=[dma],
         compiler_params=params,
         cost_estimate=cost(0.5),
         name="own_rows",
     )(place, own, *goals)
     row_stats = pl.pallas_call(
         functools.partial(all_rows_kernel, scale2, shard),
-        out_shape=jax.ShapeDtypeStruct((npeer, nrow // LANES, LANES), jnp.float32),
-        in_specs=[smem] + [vmem] * 2 + [anywhere],
+        out_shape=jax.ShapeDtypeStruct((nplane, nrow // LANES, LANES), jnp.float32),
+        in_specs=[smem] + [vmem] * 3,
         out_specs=vmem,
-        scratch_shapes=[psi_scratch, dma],
         compiler_params=params,
         cost_estimate=cost(0.5),
         name="all_rows",
-    )(place, other, own_lines, psi_all)
-    row_parts = spread(row_stats, PEERS)
+    )(place, other, own_lines, psi_near)
+    row_parts = spread(row_stats, PLANE)
 
     col_stats, peaks = pl.pallas_call(
         functools.partial(cols_kernel, scale2, shard),
@@ -480,12 +486,13 @@
         name="cols",
     )(place, own, other, psi_all)
     row_parts, col_stats = lax.optimization_barrier((row_parts, col_stats))
+    row_others = swap(row_parts)
     col_parts = spread(col_stats, "z")
 
     probs, exps, tail = pl.pallas_call(
         functools.partial(probs_kernel, scale, scale2, shard),
         out_shape=(tile_hbm, tile_hbm, jax.ShapeDtypeStruct((EXTRA, width), jnp.bfloat16)),
-        in_specs=[smem] + [vmem] * 2 + [anywhere, vmem, vmem],
+        in_specs=[smem] + [vmem] * 2 + [anywhere] + [vmem] * 3,
         out_specs=(hbm, hbm, vmem),
         scratch_shapes=[
             pltpu.VMEM((nrow // LANES, LANES), jnp.float32),
@@ -498,7 +505,7 @@
         compiler_params=params,
         cost_estimate=cost(1),
         name="probs",
-    )(place, own, other, psi_all, row_parts, peaks)
+    )(place, own, other, psi_all, row_parts, row_others, peaks)
 
     half = jax.ShapeDtypeStruct((nplane, shard + EXTRA, width), jnp.bfloat16)
     gown, gother, weights = pl.pallas_call(
@@ -532,9 +539,10 @@
     other_part, *gpsi = lax.optimization_barrier((swap(gother), *gpsi))
     joined = pl.pallas_call(
         functools.partial(join_kernel, shard),
-        out_shape=half,
+        out_shape=pltpu.HBM(half.shape, half.dtype),
         in_specs=[vmem] * 2,
-        out_specs=vmem,
+        out_specs=hbm,
+        scratch_shapes=[pltpu.VMEM(half.shape, half.dtype), dma((nplane // 4,))],
         compiler_params=params,
         name="join",
     )(gown, other_part)
@@ -550,8 +558,8 @@
             name="relay",
         )(place, *parts)
 
+    over4 = lax.ppermute(gpsi[4], "z", across)
     over3, over5 = move(gpsi[3], 1), move(gpsi[5], 7)
-    over4 = lax.ppermute(gpsi[4], "z", across)
     psi_parts = [gpsi[0], move(gpsi[1], 1), move(gpsi[7], 7)]
     psi_parts.append(move(relay(0, gpsi[2], over3, over4), 2))
     psi_parts.append(move(relay(1, gpsi[6], over5, over4), 6))

time: 107 us -> 107 us (level)
  starting transfers between devices: 50 us -> 51.2 us
  waiting for transfers between devices: 22.6 us -> 21.5 us
    all_to_all x4, starting transfers between devices: 24.3 us -> 25.6 us  [spread(): return lax.all_to_all(array, axes, 0, 0, tiled=True)]
    all_to_all x4, waiting for transfers between devices: 4.37 us -> 3.2 us  [spread(): return lax.all_to_all(array, axes, 0, 0, tiled=True)]
  transfers between devices with their start and end apart: 20 -> 21, of which waited for: 12 -> 12; matrix products, arithmetic and copies ran while one was open for 0% -> 0% of each run, Pallas kernels for 18% -> 19%
where the time goes in v4:
time: 107 us; the launch traced here: 106 us
  starting transfers between devices  51.2 us (48%)
  Pallas kernels  32.4 us (30%)
  waiting for transfers between devices  21.5 us (20%)
    all_to_all x4, starting transfers between devices, spread(): return lax.all_to_all(array, axes, 0, 0, tiled=True)  25.6 us
    ppermute x12, starting transfers between devices, move(): return lax.ppermute(array, 'z', [(i, (i + shift) % nz) for i in range(nz)])  24.3 us
    ppermute x12, waiting for transfers between devices, move(): return lax.ppermute(array, 'z', [(i, (i + shift) % nz) for i in range(nz)])  14.3 us
    pallas_call x1, Pallas kernels, shards(): pl.pallas_call(functools.partial(probs_kernel, scale, scale2, shard), out...  6.09 us
    pallas_call x1, Pallas kernels, shards(): pl.pallas_call(functools.partial(cols_kernel, scale2, shard), out_shape=(...  6.04 us
    pallas_call x1, Pallas kernels, shards(): pl.pallas_call(functools.partial(weights_kernel, scale, shard), out_shape...  5.01 us
    pallas_call x1, Pallas kernels, shards(): pl.pallas_call(functools.partial(all_rows_kernel, scale2, shard), out_sha...  3.72 us
    pallas_call x1, Pallas kernels, shards(): pl.pallas_call(functools.partial(goals_kernel, shard), out_shape=(part,)...  3.72 us
  transfers between devices with their start and end apart: 21, of which 12 were waited for; matrix products, arithmetic and copies ran while one was open for 0% of the time, Pallas kernels for 19%

profile of v4, /device:TPU:8, one launch (start us, length us, event | category | flops | bytes accessed | tf_op | source)
XLA Modules:
  0.0 106.0 jit_solution(16210458828864761370)
XLA Ops:
  0.6 2.0 %pack.1 = bf16[16,72,512]{2,1,0:T(8,128)(2,1)} custom-call(bf16[64,512]{1,0:T(8,128)(2,1)} %phi_in.1, s32[1,64]{1,0:T(1,128)} %bitcast.5), custom_call_target="tpu_custom_call" | custom-call | tf_op jit(solution)/shard_map/pack/pallas_call | solution.py:407
  2.7 0.0 copy-start
  2.7 7.5 %all-to-all-start = ((bf16[16,72,512]{2,1,0:T(8,128)(2,1)}), bf16[16,72,512]{2,1,0:T(8,128)(2,1)S(1)}, u32[]{:S(2)}, u32[]{:S(2)}) async-start(bf16[16,72,512]{2,1,0:T(8,128)(2,1)} %pack.1), calls=%async_computation | async-start | bytes 2359296 | tf_op jit(solution)/shard_map/all_to_all | solution.py:393
  10.2 0.0 copy-done
  10.2 6.4 %collective-permute-start.3 = (bf16[128,512]{1,0:T(8,128)(2,1)S(1)}, bf16[128,512]{1,0:T(8,128)(2,1)S(1)}, u32[]{:S(2)}, u32[]{:S(2)}) collective-permute-start(bf16[128,512]{1,0:T(8,128)(2,1)S(1)} %copy-done), channel_id=1, source_target_pairs={{0,6},{1,7},{2,0},{3,1},{4,2},{5,3},{6,4},{7,5},{8,14},{9,15},{10,... | collective-permute-start | bytes 393224 | tf_op jit(solution)/shard_map/ppermute | solution.py:399
  16.6 0.0 collective-permute-start.1
  16.6 1.0 collective-permute-start
  17.6 2.7 %collective-permute-start.6 = (bf16[128,512]{1,0:T(8,128)(2,1)S(1)}, bf16[128,512]{1,0:T(8,128)(2,1)S(1)}, u32[]{:S(2)}, u32[]{:S(2)}) collective-permute-start(bf16[128,512]{1,0:T(8,128)(2,1)S(1)} %copy-done), channel_id=1, source_target_pairs={{0,7},{1,0},{2,1},{3,2},{4,3},{5,4},{6,5},{7,6},{8,15},{9,8},{10,9... | collective-permute-start | bytes 393224 | tf_op jit(solution)/shard_map/ppermute | solution.py:399
  20.3 2.1 %collective-permute-done.3.refs_6_ = bf16[128,512]{1,0:T(8,128)(2,1)S(1)} collective-permute-done((bf16[128,512]{1,0:T(8,128)(2,1)S(1)}, bf16[128,512]{1,0:T(8,128)(2,1)S(1)}, u32[]{:S(2)}, u32[]{:S(2)}) %collective-permute-start.3) | collective-permute-done | bytes 131104 | tf_op jit(solution)/shard_map/ppermute | solution.py:399
  22.4 2.5 %collective-permute-start.5 = (bf16[128,512]{1,0:T(8,128)(2,1)S(1)}, bf16[128,512]{1,0:T(8,128)(2,1)S(1)}, u32[]{:S(2)}, u32[]{:S(2)}) collective-permute-start(bf16[128,512]{1,0:T(8,128)(2,1)S(1)} %collective-permute-done.3.refs_6_), channel_id=1, source_target_pairs={{0,7},{1,0},{2,1},{3,2},{4,3},{5,4},{6,5},{7,6},{8,15},{9,8},{10,9... | collective-permute-start | bytes 393224 | tf_op jit(solution)/shard_map/ppermute | solution.py:399
  24.9 1.8 %collective-permute-done.1.refs_2_ = bf16[128,512]{1,0:T(8,128)(2,1)S(1)} collective-permute-done((bf16[128,512]{1,0:T(8,128)(2,1)S(1)}, bf16[128,512]{1,0:T(8,128)(2,1)S(1)}, u32[]{:S(2)}, u32[]{:S(2)}) %collective-permute-start.1) | collective-permute-done | bytes 131104 | tf_op jit(solution)/shard_map/ppermute | solution.py:399
  26.7 0.1 collective-permute-start.4
  26.8 2.5 %collective-permute-start.2 = (bf16[128,512]{1,0:T(8,128)(2,1)S(1)}, bf16[128,512]{1,0:T(8,128)(2,1)S(1)}, u32[]{:S(2)}, u32[]{:S(2)}) collective-permute-start(bf16[128,512]{1,0:T(8,128)(2,1)S(1)} %collective-permute-done.1.refs_2_), channel_id=1, source_target_pairs={{0,1},{1,2},{2,3},{3,4},{4,5},{5,6},{6,7},{7,0},{8,9},{9,10},{10,1... | collective-permute-start | bytes 393224 | tf_op jit(solution)/shard_map/ppermute | solution.py:399
  29.3 1.1 %collective-permute-done.refs_1_ = bf16[128,512]{1,0:T(8,128)(2,1)S(1)} collective-permute-done((bf16[128,512]{1,0:T(8,128)(2,1)S(1)}, bf16[128,512]{1,0:T(8,128)(2,1)S(1)}, u32[]{:S(2)}, u32[]{:S(2)}) %collective-permute-start) | collective-permute-done | bytes 131104 | tf_op jit(solution)/shard_map/ppermute | solution.py:399
  30.3 0.0 collective-permute-done.6.refs_7_
  30.3 0.0 collective-permute-done.5.refs_5_
  30.3 3.6 %collective-permute-done.4.refs_4_ = bf16[128,512]{1,0:T(8,128)(2,1)S(1)} collective-permute-done((bf16[128,512]{1,0:T(8,128)(2,1)S(1)}, bf16[128,512]{1,0:T(8,128)(2,1)S(1)}, u32[]{:S(2)}, u32[]{:S(2)}) %collective-permute-start.4) | collective-permute-done | bytes 131104 | tf_op jit(solution)/shard_map/ppermute | solution.py:428
  34.0 0.5 collective-permute-done.2.refs_3_
  34.5 0.0 all-to-all-done.phi_ref.own_ref
  34.5 0.0 collective-permute-start.7
  34.5 0.1 pad_add_fusion.place_ref
  34.6 2.5 %own_rows.1 = (f32[8,128]{1,0:T(8,128)S(1)}, bf16[1024,512]{1,0:T(8,128)(2,1)S(1)}, bf16[1024,512]{1,0:T(8,128)(2,1)S(1)}) custom-call(s32[3]{0:T(128)S(1)} %pad_add_fusion.place_ref, bf16[16,72,512]{2,1,0:T(8,128)(2,1)S(1)} %all-to-all-done.phi_ref.own_ref, bf16[128,512]{1,0:T(8,128)(2,1)S(1)} %copy-done, ...), custom_call_target="tpu_custom_call" | custom-call | flops 1073741824 | bytes 4194304 | tf_op jit(solution)/shard_map/own_rows/pallas_call | solution.py:450
  37.1 0.4 collective-permute-done.7.phi_ref.other_ref
  37.5 3.7 %all_rows.1 = f32[16,16,128]{2,1,0:T(8,128)} custom-call(s32[3]{0:T(128)S(1)} %pad_add_fusion.place_ref, bf16[16,72,512]{2,1,0:T(8,128)(2,1)} %collective-permute-done.7.phi_ref.other_ref, f32[8,128]{1,0:T(8,128)S(1)} %get-tuple-element.54.line_ref, bf16[1024,512]{1,0:T(8,128)(2,1)S(1)} %get-tuple-element.55.psi_ref), custom_call_target="tpu_custom_call" | custom-call | flops 1073741824 | bytes 4194304 | tf_op jit(solution)/shard_map/all_rows/pallas_call | solution.py:464
  41.2 7.1 %all-to-all-start.1 = ((f32[16,16,128]{2,1,0:T(8,128)}), f32[16,16,128]{2,1,0:T(8,128)S(1)}, u32[]{:S(2)}, u32[]{:S(2)}) async-start(f32[16,16,128]{2,1,0:T(8,128)} %all_rows.1), calls=%async_computation.1 | async-start | bytes 262144 | tf_op jit(solution)/shard_map/all_to_all | solution.py:393
  48.3 6.0 %cols.1 = (f32[8,24,128]{2,1,0:T(8,128)}, f32[8,128]{1,0:T(8,128)S(1)}) custom-call(s32[3]{0:T(128)S(1)} %pad_add_fusion.place_ref, bf16[16,72,512]{2,1,0:T(8,128)(2,1)S(1)} %all-to-all-done.phi_ref.own_ref, bf16[16,72,512]{2,1,0:T(8,128)(2,1)} %collective-permute-done.7.phi_ref.other_ref, bf16[1024,512]{1,0:T(8,128)(2,1)S(1)} %get-tuple-element.56.psi_in), custom_call_target="tpu_custom_call" | custom-call | flops 2147483648 | bytes 4194304 | tf_op jit(solution)/shard_map/cols/pallas_call | solution.py:475
  54.4 0.3 all-to-all-done.1.rows_ref
  54.6 0.0 collective-permute-start.8
  54.6 3.9 %all-to-all-start.2 = ((f32[8,24,128]{2,1,0:T(8,128)}), f32[8,24,128]{2,1,0:T(8,128)S(1)}, u32[]{:S(2)}, u32[]{:S(2)}) async-start(f32[8,24,128]{2,1,0:T(8,128)} %get-tuple-element.58), calls=%async_computation.2 | async-start | bytes 196608 | tf_op jit(solution)/shard_map/all_to_all | solution.py:393
  58.5 0.0 collective-permute-done.8.others_ref
  58.5 6.1 %probs.1 = (bf16[2048,1024]{1,0:T(8,128)(2,1)}, bf16[2048,1024]{1,0:T(8,128)(2,1)}, bf16[8,512]{1,0:T(8,128)(2,1)S(1)}) custom-call(s32[3]{0:T(128)S(1)} %pad_add_fusion.place_ref, bf16[16,72,512]{2,1,0:T(8,128)(2,1)S(1)} %all-to-all-done.phi_ref.own_ref, bf16[16,72,512]{2,1,0:T(8,128)(2,1)} %collective-permute-done.7.phi_ref.other_ref, ...), custom_call_target="tpu_custom_call" | custom-call | flops 2147483648 | bytes 4194304 | tf_op jit(solution)/shard_map/probs/pallas_call | solution.py:492
  64.6 2.9 %all-to-all-done.2.cols_ref = f32[8,24,128]{2,1,0:T(8,128)S(1)} async-done(((f32[8,24,128]{2,1,0:T(8,128)}), f32[8,24,128]{2,1,0:T(8,128)S(1)}, u32[]{:S(2)}, u32[]{:S(2)}) %all-to-all-start.2) | async-done | bytes 98336 | tf_op jit(solution)/shard_map/all_to_all | solution.py:393
  67.5 5.0 %weights.1 = (bf16[16,72,512]{2,1,0:T(8,128)(2,1)S(1)}, bf16[16,72,512]{2,1,0:T(8,128)(2,1)S(1)}, bf16[2048,1024]{1,0:T(8,128)(2,1)S(1)}) custom-call(f32[8,24,128]{2,1,0:T(8,128)S(1)} %all-to-all-done.2.cols_ref, f32[8,128]{1,0:T(8,128)S(1)} %get-tuple-element.59.peak_ref, bf16[1024,512]{1,0:T(8,128)(2,1)S(1)} %get-tuple-element.56.psi_in, ...), custom_call_target="tpu_custom_call" | custom-call | flops 2147483648 | bytes 4194304 | tf_op jit(solution)/shard_map/weights/pallas_call | solution.py:511
  72.5 0.3 collective-permute-start.9
  72.9 3.7 %goals.1 = (bf16[136,512]{1,0:T(8,128)(2,1)S(1)}, bf16[136,512]{1,0:T(8,128)(2,1)S(1)}, bf16[136,512]{1,0:T(8,128)(2,1)S(1)}, bf16[136,512]{1,0:T(8,128)(2,1)S(1...) custom-call(s32[3]{0:T(128)S(1)} %pad_add_fusion.place_ref, ...), custom_call_target="tpu_custom_call" | custom-call | flops 2147483648 | bytes 4194304 | tf_op jit(solution)/shard_map/goals/pallas_call | solution.py:528
  76.6 0.0 collective-permute-done.9.other_ref
  76.6 1.1 %join.1 = bf16[16,72,512]{2,1,0:T(8,128)(2,1)} custom-call(bf16[16,72,512]{2,1,0:T(8,128)(2,1)S(1)} %get-tuple-element.63.own_ref, bf16[16,72,512]{2,1,0:T(8,128)(2,1)S(1)} %collective-permute-done.9.other_ref), custom_call_target="tpu_custom_call" | custom-call | tf_op jit(solution)/shard_map/join/pallas_call | solution.py:540
  77.8 7.1 %all-to-all-start.3 = ((bf16[16,72,512]{2,1,0:T(8,128)(2,1)}), bf16[16,72,512]{2,1,0:T(8,128)(2,1)S(1)}, u32[]{:S(2)}, u32[]{:S(2)}) async-start(bf16[16,72,512]{2,1,0:T(8,128)(2,1)} %join.1), calls=%async_computation.3 | async-start | bytes 2359296 | tf_op jit(solution)/shard_map/all_to_all | solution.py:393
  84.9 0.6 collective-permute-start.12
  85.4 0.9 collective-permute-start.13
  86.3 1.8 %collective-permute-start.15 = (bf16[136,512]{1,0:T(8,128)(2,1)S(1)}, bf16[136,512]{1,0:T(8,128)(2,1)S(1)}, u32[]{:S(2)}, u32[]{:S(2)}) collective-permute-start(bf16[136,512]{1,0:T(8,128)(2,1)S(1)} %get-tuple-element.83), channel_id=1, source_target_pairs={{0,7},{1,0},{2,1},{3,2},{4,3},{5,4},{6,5},{7,6},{8,15},{9,8},{10,9... | collective-permute-start | bytes 417800 | tf_op jit(solution)/shard_map/ppermute | solution.py:399
  88.1 1.5 %collective-permute-start.10 = (bf16[136,512]{1,0:T(8,128)(2,1)S(1)}, bf16[136,512]{1,0:T(8,128)(2,1)S(1)}, u32[]{:S(2)}, u32[]{:S(2)}) collective-permute-start(bf16[136,512]{1,0:T(8,128)(2,1)S(1)} %get-tuple-element.77), channel_id=1, source_target_pairs={{0,1},{1,2},{2,3},{3,4},{4,5},{5,6},{6,7},{7,0},{8,9},{9,10},{10,1... | collective-permute-start | bytes 417800 | tf_op jit(solution)/shard_map/ppermute | solution.py:399
  89.6 1.8 %collective-permute-start.11 = (bf16[136,512]{1,0:T(8,128)(2,1)S(1)}, bf16[136,512]{1,0:T(8,128)(2,1)S(1)}, u32[]{:S(2)}, u32[]{:S(2)}) collective-permute-start(bf16[136,512]{1,0:T(8,128)(2,1)S(1)} %get-tuple-element.78), channel_id=1, source_target_pairs={{0,7},{1,0},{2,1},{3,2},{4,3},{5,4},{6,5},{7,6},{8,15},{9,8},{10,9... | collective-permute-start | bytes 417800 | tf_op jit(solution)/shard_map/ppermute | solution.py:399
  91.3 4.3 %collective-permute-done.12.refs_1_ = bf16[136,512]{1,0:T(8,128)(2,1)S(1)} collective-permute-done((bf16[136,512]{1,0:T(8,128)(2,1)S(1)}, bf16[136,512]{1,0:T(8,128)(2,1)S(1)}, u32[]{:S(2)}, u32[]{:S(2)}) %collective-permute-start.12) | collective-permute-done | bytes 139296 | tf_op jit(solution)/shard_map/ppermute | solution.py:399
  95.6 0.0 collective-permute-done.13.refs_2_
  95.6 0.6 relay.2
  96.2 0.3 collective-permute-start.14
  96.6 0.6 collective-permute-done.15.refs_1_
  97.1 0.6 relay.3
  97.7 3.4 %collective-permute-start.16 = (bf16[136,512]{1,0:T(8,128)(2,1)S(1)}, bf16[136,512]{1,0:T(8,128)(2,1)S(1)}, u32[]{:S(2)}, u32[]{:S(2)}) collective-permute-start(bf16[136,512]{1,0:T(8,128)(2,1)S(1)} %relay.3), channel_id=1, source_target_pairs={{0,6},{1,7},{2,0},{3,1},{4,2},{5,3},{6,4},{7,5},{8,14},{9,15},{10,... | collective-permute-start | bytes 417800 | tf_op jit(solution)/shard_map/ppermute | solution.py:399
  101.2 0.0 collective-permute-done.10.refs_1_
  101.2 0.0 collective-permute-done.11.refs_2_
  101.2 3.7 %collective-permute-done.14.refs_3_ = bf16[136,512]{1,0:T(8,128)(2,1)S(1)} collective-permute-done((bf16[136,512]{1,0:T(8,128)(2,1)S(1)}, bf16[136,512]{1,0:T(8,128)(2,1)S(1)}, u32[]{:S(2)}, u32[]{:S(2)}) %collective-permute-start.14) | collective-permute-done | bytes 139296 | tf_op jit(solution)/shard_map/ppermute | solution.py:399
  104.9 0.2 collective-permute-done.16.refs_4_
  105.1 0.0 all-to-all-done.3.phi_parts_ref
  105.1 0.9 totals.1
  (1 shorter events, 0.0 us)
Async XLA Ops:
  2.7 7.6 %copy-start = (bf16[128,512]{1,0:T(8,128)(2,1)S(1)}, bf16[128,512]{1,0:T(8,128)(2,1)}, u32[]{:S(2)}) copy-start(bf16[128,512]{1,0:T(8,128)(2,1)} %refs_0_) | copy-start | bytes 393220
  2.7 31.8 %all-to-all-start = ((bf16[16,72,512]{2,1,0:T(8,128)(2,1)}), bf16[16,72,512]{2,1,0:T(8,128)(2,1)S(1)}, u32[]{:S(2)}, u32[]{:S(2)}) async-start(bf16[16,72,512]{2,1,0:T(8,128)(2,1)} %pack.1), calls=%async_computation | async-start | bytes 2359296 | tf_op jit(solution)/shard_map/all_to_all | solution.py:393
  10.2 12.2 %collective-permute-start.3 = (bf16[128,512]{1,0:T(8,128)(2,1)S(1)}, bf16[128,512]{1,0:T(8,128)(2,1)S(1)}, u32[]{:S(2)}, u32[]{:S(2)}) collective-permute-start(bf16[128,512]{1,0:T(8,128)(2,1)S(1)} %copy-done), channel_id=1, source_target_pairs={{0,6},{1,7},{2,0},{3,1},{4,2},{5,3},{6,4},{7,5},{8,14},{9,15},{10,... | collective-permute-start | bytes 393224 | tf_op jit(solution)/shard_map/ppermute | solution.py:399
  16.6 10.1 %collective-permute-start.1 = (bf16[128,512]{1,0:T(8,128)(2,1)S(1)}, bf16[128,512]{1,0:T(8,128)(2,1)S(1)}, u32[]{:S(2)}, u32[]{:S(2)}) collective-permute-start(bf16[128,512]{1,0:T(8,128)(2,1)S(1)} %copy-done), channel_id=1, source_target_pairs={{0,2},{1,3},{2,4},{3,5},{4,6},{5,7},{6,0},{7,1},{8,10},{9,11},{10,... | collective-permute-start | bytes 393224 | tf_op jit(solution)/shard_map/ppermute | solution.py:399
  16.6 13.7 %collective-permute-start = (bf16[128,512]{1,0:T(8,128)(2,1)S(1)}, bf16[128,512]{1,0:T(8,128)(2,1)S(1)}, u32[]{:S(2)}, u32[]{:S(2)}) collective-permute-start(bf16[128,512]{1,0:T(8,128)(2,1)S(1)} %copy-done), channel_id=1, source_target_pairs={{0,1},{1,2},{2,3},{3,4},{4,5},{5,6},{6,7},{7,0},{8,9},{9,10},{10,1... | collective-permute-start | bytes 393224 | tf_op jit(solution)/shard_map/ppermute | solution.py:399
  17.6 12.7 %collective-permute-start.6 = (bf16[128,512]{1,0:T(8,128)(2,1)S(1)}, bf16[128,512]{1,0:T(8,128)(2,1)S(1)}, u32[]{:S(2)}, u32[]{:S(2)}) collective-permute-start(bf16[128,512]{1,0:T(8,128)(2,1)S(1)} %copy-done), channel_id=1, source_target_pairs={{0,7},{1,0},{2,1},{3,2},{4,3},{5,4},{6,5},{7,6},{8,15},{9,8},{10,9... | collective-permute-start | bytes 393224 | tf_op jit(solution)/shard_map/ppermute | solution.py:399
  22.4 7.9 %collective-permute-start.5 = (bf16[128,512]{1,0:T(8,128)(2,1)S(1)}, bf16[128,512]{1,0:T(8,128)(2,1)S(1)}, u32[]{:S(2)}, u32[]{:S(2)}) collective-permute-start(bf16[128,512]{1,0:T(8,128)(2,1)S(1)} %collective-permute-done.3.refs_6_), channel_id=1, source_target_pairs={{0,7},{1,0},{2,1},{3,2},{4,3},{5,4},{6,5},{7,6},{8,15},{9,8},{10,9... | collective-permute-start | bytes 393224 | tf_op jit(solution)/shard_map/ppermute | solution.py:399
  26.7 7.3 %collective-permute-start.4 = (bf16[128,512]{1,0:T(8,128)(2,1)S(1)}, bf16[128,512]{1,0:T(8,128)(2,1)S(1)}, u32[]{:S(2)}, u32[]{:S(2)}) collective-permute-start(bf16[128,512]{1,0:T(8,128)(2,1)S(1)} %broadcast_select_fusion), channel_id=1, source_target_pairs={{0,2},{1,7},{2,4},{3,1},{4,6},{5,3},{6,0},{7,5},{8,10},{9,15},{10,... | collective-permute-start | bytes 393224 | tf_op jit(solution)/shard_map/ppermute | solution.py:428
  26.8 7.7 %collective-permute-start.2 = (bf16[128,512]{1,0:T(8,128)(2,1)S(1)}, bf16[128,512]{1,0:T(8,128)(2,1)S(1)}, u32[]{:S(2)}, u32[]{:S(2)}) collective-permute-start(bf16[128,512]{1,0:T(8,128)(2,1)S(1)} %collective-permute-done.1.refs_2_), channel_id=1, source_target_pairs={{0,1},{1,2},{2,3},{3,4},{4,5},{5,6},{6,7},{7,0},{8,9},{9,10},{10,1... | collective-permute-start | bytes 393224 | tf_op jit(solution)/shard_map/ppermute | solution.py:399
  34.5 3.0 %collective-permute-start.7 = (bf16[16,72,512]{2,1,0:T(8,128)(2,1)S(1)}, bf16[16,72,512]{2,1,0:T(8,128)(2,1)}, u32[]{:S(2)}, u32[]{:S(2)}) collective-permute-start(bf16[16,72,512]{2,1,0:T(8,128)(2,1)S(1)} %all-to-all-done.phi_ref.own_ref), channel_id=1, source_target_pairs={{0,32},{32,0},{1,33},{33,1},{2,34},{34,2},{3,35},{35,3},{4,36},{36... | collective-permute-start | bytes 3538952 | tf_op jit(solution)/shard_map/ppermute | solution.py:396
  41.2 13.4 %all-to-all-start.1 = ((f32[16,16,128]{2,1,0:T(8,128)}), f32[16,16,128]{2,1,0:T(8,128)S(1)}, u32[]{:S(2)}, u32[]{:S(2)}) async-start(f32[16,16,128]{2,1,0:T(8,128)} %all_rows.1), calls=%async_computation.1 | async-start | bytes 262144 | tf_op jit(solution)/shard_map/all_to_all | solution.py:393
  54.6 3.9 %collective-permute-start.8 = (f32[16,16,128]{2,1,0:T(8,128)S(1)}, f32[16,16,128]{2,1,0:T(8,128)S(1)}, u32[]{:S(2)}, u32[]{:S(2)}) collective-permute-start(f32[16,16,128]{2,1,0:T(8,128)S(1)} %all-to-all-done.1.rows_ref), channel_id=1, source_target_pairs={{0,32},{32,0},{1,33},{33,1},{2,34},{34,2},{3,35},{35,3},{4,36},{36... | collective-permute-start | bytes 393224 | tf_op jit(solution)/shard_map/ppermute | solution.py:396
  54.6 12.9 %all-to-all-start.2 = ((f32[8,24,128]{2,1,0:T(8,128)}), f32[8,24,128]{2,1,0:T(8,128)S(1)}, u32[]{:S(2)}, u32[]{:S(2)}) async-start(f32[8,24,128]{2,1,0:T(8,128)} %get-tuple-element.58), calls=%async_computation.2 | async-start | bytes 196608 | tf_op jit(solution)/shard_map/all_to_all | solution.py:393
  72.5 4.0 %collective-permute-start.9 = (bf16[16,72,512]{2,1,0:T(8,128)(2,1)S(1)}, bf16[16,72,512]{2,1,0:T(8,128)(2,1)S(1)}, u32[]{:S(2)}, u32[]{:S(2)}) collective-permute-start(bf16[16,72,512]{2,1,0:T(8,128)(2,1)S(1)} %get-tuple-element.64), channel_id=1, source_target_pairs={{0,32},{32,0},{1,33},{33,1},{2,34},{34,2},{3,35},{35,3},{4,36},{36... | collective-permute-start | bytes 3538952 | tf_op jit(solution)/shard_map/ppermute | solution.py:396
  77.8 27.4 %all-to-all-start.3 = ((bf16[16,72,512]{2,1,0:T(8,128)(2,1)}), bf16[16,72,512]{2,1,0:T(8,128)(2,1)S(1)}, u32[]{:S(2)}, u32[]{:S(2)}) async-start(bf16[16,72,512]{2,1,0:T(8,128)(2,1)} %join.1), calls=%async_computation.3 | async-start | bytes 2359296 | tf_op jit(solution)/shard_map/all_to_all | solution.py:393
  84.9 10.7 %collective-permute-start.12 = (bf16[136,512]{1,0:T(8,128)(2,1)S(1)}, bf16[136,512]{1,0:T(8,128)(2,1)S(1)}, u32[]{:S(2)}, u32[]{:S(2)}) collective-permute-start(bf16[136,512]{1,0:T(8,128)(2,1)S(1)} %get-tuple-element.80), channel_id=1, source_target_pairs={{0,1},{1,2},{2,3},{3,4},{4,5},{5,6},{6,7},{7,0},{8,9},{9,10},{10,1... | collective-permute-start | bytes 417800 | tf_op jit(solution)/shard_map/ppermute | solution.py:399
  85.4 10.2 %collective-permute-start.13 = (bf16[136,512]{1,0:T(8,128)(2,1)S(1)}, bf16[136,512]{1,0:T(8,128)(2,1)S(1)}, u32[]{:S(2)}, u32[]{:S(2)}) collective-permute-start(bf16[136,512]{1,0:T(8,128)(2,1)S(1)} %get-tuple-element.81), channel_id=1, source_target_pairs={{0,2},{1,7},{2,4},{3,1},{4,6},{5,3},{6,0},{7,5},{8,10},{9,15},{10,... | collective-permute-start | bytes 417800 | tf_op jit(solution)/shard_map/ppermute | solution.py:561
  86.3 10.8 %collective-permute-start.15 = (bf16[136,512]{1,0:T(8,128)(2,1)S(1)}, bf16[136,512]{1,0:T(8,128)(2,1)S(1)}, u32[]{:S(2)}, u32[]{:S(2)}) collective-permute-start(bf16[136,512]{1,0:T(8,128)(2,1)S(1)} %get-tuple-element.83), channel_id=1, source_target_pairs={{0,7},{1,0},{2,1},{3,2},{4,3},{5,4},{6,5},{7,6},{8,15},{9,8},{10,9... | collective-permute-start | bytes 417800 | tf_op jit(solution)/shard_map/ppermute | solution.py:399
  88.1 13.1 %collective-permute-start.10 = (bf16[136,512]{1,0:T(8,128)(2,1)S(1)}, bf16[136,512]{1,0:T(8,128)(2,1)S(1)}, u32[]{:S(2)}, u32[]{:S(2)}) collective-permute-start(bf16[136,512]{1,0:T(8,128)(2,1)S(1)} %get-tuple-element.77), channel_id=1, source_target_pairs={{0,1},{1,2},{2,3},{3,4},{4,5},{5,6},{6,7},{7,0},{8,9},{9,10},{10,1... | collective-permute-start | bytes 417800 | tf_op jit(solution)/shard_map/ppermute | solution.py:399
  89.6 11.6 %collective-permute-start.11 = (bf16[136,512]{1,0:T(8,128)(2,1)S(1)}, bf16[136,512]{1,0:T(8,128)(2,1)S(1)}, u32[]{:S(2)}, u32[]{:S(2)}) collective-permute-start(bf16[136,512]{1,0:T(8,128)(2,1)S(1)} %get-tuple-element.78), channel_id=1, source_target_pairs={{0,7},{1,0},{2,1},{3,2},{4,3},{5,4},{6,5},{7,6},{8,15},{9,8},{10,9... | collective-permute-start | bytes 417800 | tf_op jit(solution)/shard_map/ppermute | solution.py:399
  96.2 8.7 %collective-permute-start.14 = (bf16[136,512]{1,0:T(8,128)(2,1)S(1)}, bf16[136,512]{1,0:T(8,128)(2,1)S(1)}, u32[]{:S(2)}, u32[]{:S(2)}) collective-permute-start(bf16[136,512]{1,0:T(8,128)(2,1)S(1)} %relay.2), channel_id=1, source_target_pairs={{0,2},{1,3},{2,4},{3,5},{4,6},{5,7},{6,0},{7,1},{8,10},{9,11},{10,... | collective-permute-start | bytes 417800 | tf_op jit(solution)/shard_map/ppermute | solution.py:399
  97.7 7.4 %collective-permute-start.16 = (bf16[136,512]{1,0:T(8,128)(2,1)S(1)}, bf16[136,512]{1,0:T(8,128)(2,1)S(1)}, u32[]{:S(2)}, u32[]{:S(2)}) collective-permute-start(bf16[136,512]{1,0:T(8,128)(2,1)S(1)} %relay.3), channel_id=1, source_target_pairs={{0,6},{1,7},{2,0},{3,1},{4,2},{5,3},{6,4},{7,5},{8,14},{9,15},{10,... | collective-permute-start | bytes 417800 | tf_op jit(solution)/shard_map/ppermute | solution.py:399

commit v5 on v4

--- a/solution.py
+++ b/solution.py
@@ -12,6 +12,7 @@
 PEERS = ("y", "core", "x")
 PLANE = ("y", "x")
 EXTRA = 8
+GROUP = 16
 CHUNK = 256
 LANES = 128
 LOG2E = math.log2(math.e)
@@ -149,21 +150,8 @@
         row_ref[:, pl.ds(at, count), :] = jnp.broadcast_to(part[None], (npeer, count, LANES))
 
 
-def block_copies(pairs, sems):
-    out = []
-    for k, (src, dst) in enumerate(pairs):
-        cuts = [pl.ds(r, CHUNK) for r in range(0, src.shape[0], CHUNK)]
-        out.append(
-            [
-                pltpu.make_async_copy(src.at[cut], dst.at[cut], sems.at[k, i])
-                for i, cut in enumerate(cuts)
-            ]
-        )
-    return out
-
-
 def cols_kernel(
-    scale2, shard, place_ref, own_ref, other_ref, psi_in, col_ref, peak_ref, psi_ref, sem
+    scale2, shard, place_ref, own_ref, other_ref, psi_in, col_ref, psi_ref, sem
 ):
     copy = pltpu.make_async_copy(psi_in, psi_ref, sem)
     copy.start()
@@ -200,8 +188,6 @@
             cut = line[:, t * LANES : (t + 1) * LANES]
             at = 2 * k * nline + t
             col_ref[:, at : at + 1, :] = jnp.broadcast_to(cut[None], (nz, 1, LANES))
-    for t in range(nline):
-        peak_ref[t : t + 1, :] = col_max[:, t * LANES : (t + 1) * LANES]
     col_ref[:, nline : 2 * nline, :] = jnp.broadcast_to(
         count[None, :nline, :], (nz, nline, LANES)
     )
@@ -219,24 +205,37 @@
     return full.astype(jnp.bfloat16)
 
 
-def probs_kernel(
-    scale, scale2, shard, place_ref, own_ref, other_ref, psi_in, rows_ref, others_ref, peak_ref, *refs
+def weights_kernel(
+    scale, scale2, shard, place_ref, own_ref, other_ref, psi_in, rows_ref, others_ref, *refs
 ):
-    prob_out, exp_out, tail_ref, shift_ref, psi_ref, prob_ref, exp_ref, sem, sems = refs
+    cols_ref, gown_ref, gother_ref, w_ref, tail_ref, shift_ref, psi_ref, sem = refs
     copy = pltpu.make_async_copy(psi_in, psi_ref, sem)
     copy.start()
     ncol, width = psi_ref.shape
+    plane = gown_ref.shape[0]
     per = CHUNK // shard
+    nline = ncol // LANES
     base = place_ref[1].astype(jnp.float32)
+    shift2 = math.log2(scale)
+
     row_parts = jnp.concatenate([rows_ref[...], others_ref[...]], axis=0)
     row_peak = jnp.max(row_parts, axis=0)
     row_lse = row_peak + jnp.log2(jnp.sum(jnp.exp2(row_parts - row_peak[None]), axis=0))
     tail_ref[...] = tail_rows(jnp.sum(row_lse, keepdims=True), width)
-    shift_ref[...] = row_lse - math.log2(scale)
+    shift_ref[...] = row_lse - shift2
+
+    col_parts = cols_ref[:, :nline, :]
+    col_peak = jnp.max(col_parts, axis=0)
+    col_lse = col_peak + jnp.log2(jnp.sum(jnp.exp2(col_parts - col_peak[None]), axis=0))
+    counts = jnp.sum(cols_ref[:, nline : 2 * nline, :], axis=0)
+    hits = jnp.sum(cols_ref[:, 2 * nline :, :], axis=0)
+    col_total = jnp.sum(counts * col_lse - 2.0 * hits, keepdims=True)
+    tail = jnp.broadcast_to(tail_rows(col_total, width)[None], (plane, EXTRA, width))
+    line = col_lse - jnp.log2(counts) - shift2
+    line = jnp.concatenate([line[t : t + 1] for t in range(nline)], axis=1)
+
     copy.wait()
     psi = psi_ref[...]
-    prob_stores, exp_stores = block_copies([(prob_ref, prob_out), (exp_ref, exp_out)], sems)
-    peak = jnp.concatenate([peak_ref[t : t + 1] for t in range(ncol // LANES)], axis=1)
     chunks = chunks_of((own_ref, other_ref), shard)
     for number, half, first, phi_ref in chunks:
         rows = phi_ref[first : first + per, :shard, :].reshape(CHUNK, width)
@@ -246,55 +245,19 @@
             [to_rows(shift_ref[pl.ds(at + t, 1), :]) for t in range(CHUNK // LANES)],
             axis=0,
         )
-        lse = jnp.concatenate([lse] * (ncol // LANES), axis=1)
+        lse = jnp.concatenate([lse] * nline, axis=1)
         hit = hit_mask(row_places(phi_ref, first, per, shard), base, ncol)
-        prob = jnp.exp2(logits - lse) - jnp.where(hit, 2.0 * scale, 0.0)
-        prob_ref[number * CHUNK : (number + 1) * CHUNK, :] = prob.astype(jnp.bfloat16)
-        prob_stores[number].start()
-        part = jnp.exp2(logits - peak).astype(jnp.bfloat16)
-        exp_ref[number * CHUNK : (number + 1) * CHUNK, :] = part
-        exp_stores[number].start()
-    for store in prob_stores + exp_stores:
-        store.wait()
-
-
-def weights_kernel(scale, shard, cols_ref, peak_ref, psi_in, prob_in, exp_in, *refs):
-    gown_ref, gother_ref, w_ref, psi_ref, prob_ref, exp_ref, sem, sems = refs
-    copy = pltpu.make_async_copy(psi_in, psi_ref, sem)
-    loads = block_copies([(prob_in, prob_ref), (exp_in, exp_ref)], sems)
-    loads[0][0].start()
-    loads[1][0].start()
-    copy.start()
-    for pair in zip(loads[0][1:], loads[1][1:]):
-        for load in pair:
-            load.start()
-    ncol, width = psi_ref.shape
-    per = CHUNK // shard
-    nline = ncol // LANES
-    col_parts = cols_ref[:, :nline, :]
-    col_peak = jnp.max(col_parts, axis=0)
-    col_lse = col_peak + jnp.log2(jnp.sum(jnp.exp2(col_parts - col_peak[None]), axis=0))
-    counts = jnp.sum(cols_ref[:, nline : 2 * nline, :], axis=0)
-    hits = jnp.sum(cols_ref[:, 2 * nline :, :], axis=0)
-    col_total = jnp.sum(counts * col_lse - 2.0 * hits, keepdims=True)
-    tail = jnp.broadcast_to(tail_rows(col_total, width)[None], (per, EXTRA, width))
-    factor = counts * scale * jnp.exp2(peak_ref[...] - col_lse)
-    factor = jnp.concatenate([factor[t : t + 1] for t in range(nline)], axis=1)
-    copy.wait()
-    psi = psi_ref[...]
-    plane = gown_ref.shape[0]
-    for number in range(len(loads[0])):
-        cut = slice(number * CHUNK, (number + 1) * CHUNK)
-        loads[0][number].wait()
-        loads[1][number].wait()
-        weights = exp_ref[cut, :].astype(jnp.float32) * factor
-        weights = (prob_ref[cut, :].astype(jnp.float32) + weights).astype(jnp.bfloat16)
-        w_ref[cut, :] = weights
-        part = nn(weights, psi).astype(jnp.bfloat16)
-        half, first = divmod(number * per, plane)
+        weights = jnp.exp2(logits - lse) + jnp.exp2(logits - line)
+        weights = (weights - jnp.where(hit, 2.0 * scale, 0.0)).astype(jnp.bfloat16)
+        w_ref[number * CHUNK : (number + 1) * CHUNK, :] = weights
         out_ref = gother_ref if half else gown_ref
-        out_ref[first : first + per, :shard, :] = part.reshape(per, shard, width)
-        out_ref[first : first + per, shard:, :] = tail
+        if (first + per) % GROUP == 0:
+            end = (number + 1) * CHUNK
+            part = nn(w_ref[end - GROUP * shard : end, :], psi).astype(jnp.bfloat16)
+            block = slice(first + per - GROUP, first + per)
+            out_ref[block, :shard, :] = part.reshape(GROUP, shard, width)
+    gown_ref[:, shard:, :] = tail
+    gother_ref[:, shard:, :] = tail
 
 
 def join_kernel(shard, own_ref, other_ref, out, out_ref, sems):
@@ -440,27 +403,24 @@
             flops=int(products * flops), bytes_accessed=4 << 20, transcendentals=int(products * nrow * ncol)
         )
 
-    anywhere = pl.BlockSpec(memory_space=pl.ANY)
     dma = pltpu.SemaphoreType.DMA
-    nchunk = nrow // CHUNK
     psi_scratch = pltpu.VMEM((ncol, width), jnp.bfloat16)
     tile = jax.ShapeDtypeStruct((nrow, ncol), jnp.bfloat16)
-    tile_hbm = pltpu.HBM((nrow, ncol), jnp.bfloat16)
-    tile_scratch = pltpu.VMEM((nrow, ncol), jnp.bfloat16)
     own_lines, psi_all, psi_near = pl.pallas_call(
         functools.partial(own_rows_kernel, scale2, shard),
         out_shape=(
             jax.ShapeDtypeStruct((nrow // LANES // 2, LANES), jnp.float32),
-            jax.ShapeDtypeStruct((ncol, width), jnp.bfloat16),
+            pltpu.HBM((ncol, width), jnp.bfloat16),
             jax.ShapeDtypeStruct((ncol, width), jnp.bfloat16),
         ),
         in_specs=[smem] + [vmem] * (1 + nz),
-        out_specs=(vmem, anywhere, vmem),
+        out_specs=(vmem, hbm, vmem),
         scratch_shapes=[dma],
         compiler_params=params,
         cost_estimate=cost(0.5),
         name="own_rows",
     )(place, own, *goals)
+    psi_all = pltpu.with_memory_space_constraint(psi_all, pltpu.HBM)
     row_stats = pl.pallas_call(
         functools.partial(all_rows_kernel, scale2, shard),
         out_shape=jax.ShapeDtypeStruct((nplane, nrow // LANES, LANES), jnp.float32),
@@ -472,14 +432,11 @@
     )(place, other, own_lines, psi_near)
     row_parts = spread(row_stats, PLANE)
 
-    col_stats, peaks = pl.pallas_call(
+    col_stats = pl.pallas_call(
         functools.partial(cols_kernel, scale2, shard),
-        out_shape=(
-            jax.ShapeDtypeStruct((nz, 3 * ncol // LANES, LANES), jnp.float32),
-            jax.ShapeDtypeStruct((ncol // LANES, LANES), jnp.float32),
-        ),
-        in_specs=[smem] + [vmem] * 2 + [anywhere],
-        out_specs=(vmem, vmem),
+        out_shape=jax.ShapeDtypeStruct((nz, 3 * ncol // LANES, LANES), jnp.float32),
+        in_specs=[smem] + [vmem] * 2 + [hbm],
+        out_specs=vmem,
         scratch_shapes=[psi_scratch, dma],
         compiler_params=params,
         cost_estimate=cost(1),
@@ -489,41 +446,17 @@
     row_others = swap(row_parts)
     col_parts = spread(col_stats, "z")
 
-    probs, exps, tail = pl.pallas_call(
-        functools.partial(probs_kernel, scale, scale2, shard),
-        out_shape=(tile_hbm, tile_hbm, jax.ShapeDtypeStruct((EXTRA, width), jnp.bfloat16)),
-        in_specs=[smem] + [vmem] * 2 + [anywhere] + [vmem] * 3,
-        out_specs=(hbm, hbm, vmem),
-        scratch_shapes=[
-            pltpu.VMEM((nrow // LANES, LANES), jnp.float32),
-            psi_scratch,
-            tile_scratch,
-            tile_scratch,
-            dma,
-            dma((2, nchunk)),
-        ],
-        compiler_params=params,
-        cost_estimate=cost(1),
-        name="probs",
-    )(place, own, other, psi_all, row_parts, row_others, peaks)
-
     half = jax.ShapeDtypeStruct((nplane, shard + EXTRA, width), jnp.bfloat16)
-    gown, gother, weights = pl.pallas_call(
-        functools.partial(weights_kernel, scale, shard),
-        out_shape=(half, half, tile),
-        in_specs=[vmem] * 2 + [anywhere, hbm, hbm],
-        out_specs=(vmem,) * 3,
-        scratch_shapes=[psi_scratch, tile_scratch, tile_scratch, dma, dma((2, nchunk))],
-        compiler_params=params,
-        cost_estimate=cost(1),
+    gown, gother, weights, tail = pl.pallas_call(
+        functools.partial(weights_kernel, scale, scale2, shard),
+        out_shape=(half, half, tile, jax.ShapeDtypeStruct((EXTRA, width), jnp.bfloat16)),
+        in_specs=[smem] + [vmem] * 2 + [hbm] + [vmem] * 3,
+        out_specs=(vmem,) * 4,
+        scratch_shapes=[pltpu.VMEM((nrow // LANES, LANES), jnp.float32), psi_scratch, dma],
+        compiler_params=params,
+        cost_estimate=cost(2),
         name="weights",
-    )(
-        col_parts,
-        peaks,
-        psi_all,
-        pltpu.with_memory_space_constraint(probs, pltpu.HBM),
-        pltpu.with_memory_space_constraint(exps, pltpu.HBM),
-    )
+    )(place, own, other, psi_all, row_parts, row_others, col_parts)
     part = jax.ShapeDtypeStruct((piece + EXTRA, width), jnp.bfloat16)
     gpsi = pl.pallas_call(
         functools.partial(goals_kernel, shard),

time: 107 us -> 108 us (level)
  waiting for transfers between devices: 21.5 us -> 26.9 us
  Pallas kernels: 32.4 us -> 28.3 us
    all_to_all x4, waiting for transfers between devices: 3.2 us -> 7.39 us  [spread(): return lax.all_to_all(array, axes, 0, 0, tiled=True)]
    pallas_call x3 -> x2, Pallas kernels: 17.1 us -> 13.8 us  [the longest x1 7.29 us: shards(): pl.pallas_call(functools.partial(weights_kernel, scale, scale2, shard), o...]
    ppermute x3, waiting for transfers between devices: 0.39 us -> 1.7 us  [swap(): return lax.ppermute(array, 'core', [(0, 1), (1, 0)])]
  transfers between devices with their start and end apart: 21 -> 21, of which waited for: 12 -> 12; matrix products, arithmetic and copies ran while one was open for 0% -> 0% of each run, Pallas kernels for 19% -> 13%
where the time goes in v5:
time: 108 us; the launch traced here: 107 us
  starting transfers between devices  51.4 us (48%)
  Pallas kernels  28.3 us (26%)
  waiting for transfers between devices  26.9 us (25%)
    all_to_all x4, starting transfers between devices, spread(): return lax.all_to_all(array, axes, 0, 0, tiled=True)  25.8 us
    ppermute x12, starting transfers between devices, move(): return lax.ppermute(array, 'z', [(i, (i + shift) % nz) for i in range(nz)])  24.8 us
    ppermute x12, waiting for transfers between devices, move(): return lax.ppermute(array, 'z', [(i, (i + shift) % nz) for i in range(nz)])  14.2 us
    all_to_all x4, waiting for transfers between devices, spread(): return lax.all_to_all(array, axes, 0, 0, tiled=True)  7.39 us
    pallas_call x1, Pallas kernels, shards(): pl.pallas_call(functools.partial(weights_kernel, scale, scale2, shard), o...  7.29 us
    pallas_call x1, Pallas kernels, shards(): pl.pallas_call(functools.partial(cols_kernel, scale2, shard), out_shape=j...  6.51 us
    pallas_call x1, Pallas kernels, shards(): pl.pallas_call(functools.partial(goals_kernel, shard), out_shape=(part,)...  3.7 us
    ppermute x1, waiting for transfers between devices, shards(): near[4] = lax.ppermute(jnp.where(even, near[2], near[6]), 'z', across)  3.63 us
  transfers between devices with their start and end apart: 21, of which 12 were waited for; matrix products, arithmetic and copies ran while one was open for 0% of the time, Pallas kernels for 13%

profile of v5, /device:TPU:8, one launch (start us, length us, event | category | flops | bytes accessed | tf_op | source)
XLA Modules:
  0.0 107.5 jit_solution(7266254558663836631)
XLA Ops:
  0.6 2.0 %pack.1 = bf16[16,72,512]{2,1,0:T(8,128)(2,1)} custom-call(bf16[64,512]{1,0:T(8,128)(2,1)} %phi_in.1, s32[1,64]{1,0:T(1,128)} %bitcast.5), custom_call_target="tpu_custom_call" | custom-call | tf_op jit(solution)/shard_map/pack/pallas_call | solution.py:370
  2.7 0.0 copy-start
  2.7 7.5 %all-to-all-start = ((bf16[16,72,512]{2,1,0:T(8,128)(2,1)}), bf16[16,72,512]{2,1,0:T(8,128)(2,1)S(1)}, u32[]{:S(2)}, u32[]{:S(2)}) async-start(bf16[16,72,512]{2,1,0:T(8,128)(2,1)} %pack.1), calls=%async_computation | async-start | bytes 2359296 | tf_op jit(solution)/shard_map/all_to_all | solution.py:356
  10.2 0.0 copy-done
  10.2 6.4 %collective-permute-start.3 = (bf16[128,512]{1,0:T(8,128)(2,1)S(1)}, bf16[128,512]{1,0:T(8,128)(2,1)S(1)}, u32[]{:S(2)}, u32[]{:S(2)}) collective-permute-start(bf16[128,512]{1,0:T(8,128)(2,1)S(1)} %copy-done), channel_id=1, source_target_pairs={{0,6},{1,7},{2,0},{3,1},{4,2},{5,3},{6,4},{7,5},{8,14},{9,15},{10,... | collective-permute-start | bytes 393224 | tf_op jit(solution)/shard_map/ppermute | solution.py:362
  16.6 0.0 collective-permute-start.1
  16.6 1.0 collective-permute-start
  17.6 2.7 %collective-permute-start.6 = (bf16[128,512]{1,0:T(8,128)(2,1)S(1)}, bf16[128,512]{1,0:T(8,128)(2,1)S(1)}, u32[]{:S(2)}, u32[]{:S(2)}) collective-permute-start(bf16[128,512]{1,0:T(8,128)(2,1)S(1)} %copy-done), channel_id=1, source_target_pairs={{0,7},{1,0},{2,1},{3,2},{4,3},{5,4},{6,5},{7,6},{8,15},{9,8},{10,9... | collective-permute-start | bytes 393224 | tf_op jit(solution)/shard_map/ppermute | solution.py:362
  20.3 2.1 %collective-permute-done.3.refs_6_ = bf16[128,512]{1,0:T(8,128)(2,1)S(1)} collective-permute-done((bf16[128,512]{1,0:T(8,128)(2,1)S(1)}, bf16[128,512]{1,0:T(8,128)(2,1)S(1)}, u32[]{:S(2)}, u32[]{:S(2)}) %collective-permute-start.3) | collective-permute-done | bytes 131104 | tf_op jit(solution)/shard_map/ppermute | solution.py:362
  22.4 2.5 %collective-permute-start.5 = (bf16[128,512]{1,0:T(8,128)(2,1)S(1)}, bf16[128,512]{1,0:T(8,128)(2,1)S(1)}, u32[]{:S(2)}, u32[]{:S(2)}) collective-permute-start(bf16[128,512]{1,0:T(8,128)(2,1)S(1)} %collective-permute-done.3.refs_6_), channel_id=1, source_target_pairs={{0,7},{1,0},{2,1},{3,2},{4,3},{5,4},{6,5},{7,6},{8,15},{9,8},{10,9... | collective-permute-start | bytes 393224 | tf_op jit(solution)/shard_map/ppermute | solution.py:362
  24.9 1.8 %collective-permute-done.1.refs_2_ = bf16[128,512]{1,0:T(8,128)(2,1)S(1)} collective-permute-done((bf16[128,512]{1,0:T(8,128)(2,1)S(1)}, bf16[128,512]{1,0:T(8,128)(2,1)S(1)}, u32[]{:S(2)}, u32[]{:S(2)}) %collective-permute-start.1) | collective-permute-done | bytes 131104 | tf_op jit(solution)/shard_map/ppermute | solution.py:362
  26.7 0.1 collective-permute-start.4
  26.8 2.5 %collective-permute-start.2 = (bf16[128,512]{1,0:T(8,128)(2,1)S(1)}, bf16[128,512]{1,0:T(8,128)(2,1)S(1)}, u32[]{:S(2)}, u32[]{:S(2)}) collective-permute-start(bf16[128,512]{1,0:T(8,128)(2,1)S(1)} %collective-permute-done.1.refs_2_), channel_id=1, source_target_pairs={{0,1},{1,2},{2,3},{3,4},{4,5},{5,6},{6,7},{7,0},{8,9},{9,10},{10,1... | collective-permute-start | bytes 393224 | tf_op jit(solution)/shard_map/ppermute | solution.py:362
  29.3 1.1 %collective-permute-done.refs_1_ = bf16[128,512]{1,0:T(8,128)(2,1)S(1)} collective-permute-done((bf16[128,512]{1,0:T(8,128)(2,1)S(1)}, bf16[128,512]{1,0:T(8,128)(2,1)S(1)}, u32[]{:S(2)}, u32[]{:S(2)}) %collective-permute-start) | collective-permute-done | bytes 131104 | tf_op jit(solution)/shard_map/ppermute | solution.py:362
  30.3 0.0 collective-permute-done.6.refs_7_
  30.4 0.0 collective-permute-done.5.refs_5_
  30.4 3.6 %collective-permute-done.4.refs_4_ = bf16[128,512]{1,0:T(8,128)(2,1)S(1)} collective-permute-done((bf16[128,512]{1,0:T(8,128)(2,1)S(1)}, bf16[128,512]{1,0:T(8,128)(2,1)S(1)}, u32[]{:S(2)}, u32[]{:S(2)}) %collective-permute-start.4) | collective-permute-done | bytes 131104 | tf_op jit(solution)/shard_map/ppermute | solution.py:391
  34.0 0.5 collective-permute-done.2.refs_3_
  34.5 0.0 all-to-all-done.phi_ref.own_ref
  34.5 0.0 collective-permute-start.7
  34.5 0.1 pad_add_fusion.place_ref
  34.6 2.4 %own_rows.1 = (f32[8,128]{1,0:T(8,128)S(1)}, bf16[1024,512]{1,0:T(8,128)(2,1)}, bf16[1024,512]{1,0:T(8,128)(2,1)S(1)}) custom-call(s32[3]{0:T(128)S(1)} %pad_add_fusion.place_ref, bf16[16,72,512]{2,1,0:T(8,128)(2,1)S(1)} %all-to-all-done.phi_ref.own_ref, bf16[128,512]{1,0:T(8,128)(2,1)S(1)} %copy-done, bf16[128,512]{1,0:T(8,128)(2,1)S(1)} %collective-permute-done.refs_1_, ...), custom_call_target="tpu_custom_call" | custom-call | flops 1073741824 | bytes 4194304 | tf_op jit(solution)/shard_map/own_rows/pallas_call | solution.py:409
  37.0 0.4 collective-permute-done.7.phi_ref.other_ref
  37.3 3.0 %all_rows.1 = f32[16,16,128]{2,1,0:T(8,128)} custom-call(s32[3]{0:T(128)S(1)} %pad_add_fusion.place_ref, bf16[16,72,512]{2,1,0:T(8,128)(2,1)S(1)} %collective-permute-done.7.phi_ref.other_ref, f32[8,128]{1,0:T(8,128)S(1)} %get-tuple-element.51.line_ref, bf16[1024,512]{1,0:T(8,128)(2,1)S(1)} %get-tuple-element.52.psi_ref), custom_call_target="tpu_custom_call" | custom-call | flops 1073741824 | bytes 4194304 | tf_op jit(solution)/shard_map/all_rows/pallas_call | solution.py:424
  40.4 7.1 %all-to-all-start.1 = ((f32[16,16,128]{2,1,0:T(8,128)}), f32[16,16,128]{2,1,0:T(8,128)S(1)}, u32[]{:S(2)}, u32[]{:S(2)}) async-start(f32[16,16,128]{2,1,0:T(8,128)} %all_rows.1), calls=%async_computation.1 | async-start | bytes 262144 | tf_op jit(solution)/shard_map/all_to_all | solution.py:356
  47.5 6.5 %cols.1 = f32[8,24,128]{2,1,0:T(8,128)} custom-call(s32[3]{0:T(128)S(1)} %pad_add_fusion.place_ref, bf16[16,72,512]{2,1,0:T(8,128)(2,1)S(1)} %all-to-all-done.phi_ref.own_ref, bf16[16,72,512]{2,1,0:T(8,128)(2,1)S(1)} %collective-permute-done.7.phi_ref.other_ref, bf16[1024,512]{1,0:T(8,128)(2,1)} %get-tuple-element.50.psi_in), custom_call_target="tpu_custom_call" | custom-call | flops 2147483648 | bytes 4194304 | tf_op jit(solution)/shard_map/cols/pallas_call | solution.py:435
  54.0 0.0 all-to-all-done.1.rows_ref
  54.0 3.9 %all-to-all-start.2 = ((f32[8,24,128]{2,1,0:T(8,128)}), f32[8,24,128]{2,1,0:T(8,128)S(1)}, u32[]{:S(2)}, u32[]{:S(2)}) async-start(f32[8,24,128]{2,1,0:T(8,128)} %cols.1), calls=%async_computation.2 | async-start | bytes 196608 | tf_op jit(solution)/shard_map/all_to_all | solution.py:356
  57.9 0.0 collective-permute-start.8
  57.9 1.3 %collective-permute-done.8.others_ref = f32[16,16,128]{2,1,0:T(8,128)S(1)} collective-permute-done((f32[16,16,128]{2,1,0:T(8,128)S(1)}, f32[16,16,128]{2,1,0:T(8,128)S(1)}, u32[]{:S(2)}, u32[]{:S(2)}) %collective-permute-start.8) | collective-permute-done | bytes 131104 | tf_op jit(solution)/shard_map/ppermute | solution.py:359
  59.3 7.4 %all-to-all-done.2.refs_0_ = f32[8,24,128]{2,1,0:T(8,128)S(1)} async-done(((f32[8,24,128]{2,1,0:T(8,128)}), f32[8,24,128]{2,1,0:T(8,128)S(1)}, u32[]{:S(2)}, u32[]{:S(2)}) %all-to-all-start.2) | async-done | bytes 98336 | tf_op jit(solution)/shard_map/all_to_all | solution.py:356
  66.7 7.3 %weights.1 = (bf16[16,72,512]{2,1,0:T(8,128)(2,1)S(1)}, bf16[16,72,512]{2,1,0:T(8,128)(2,1)S(1)}, bf16[2048,1024]{1,0:T(8,128)(2,1)S(1)}, bf16[8,512]{1,0:T(8,128)(2,1)S(1)}) custom-call(s32[3]{0:T(128)S(1)} %pad_add_fusion.place_ref, bf16[16,72,512]{2,1,0:T(8,128)(2,1)S(1)} %all-to-all-done.phi_ref.own_ref, ...), custom_call_target="tpu_custom_call" | custom-call | flops 4294967296 | bytes 4194304 | tf_op jit(solution)/shard_map/weights/pallas_call | solution.py:450
  74.0 0.3 collective-permute-start.9
  74.3 3.7 %goals.1 = (bf16[136,512]{1,0:T(8,128)(2,1)S(1)}, bf16[136,512]{1,0:T(8,128)(2,1)S(1)}, bf16[136,512]{1,0:T(8,128)(2,1)S(1)}, bf16[136,512]{1,0:T(8,128)(2,1)}, ...) custom-call(s32[3]{0:T(128)S(1)} %pad_add_fusion.place_ref, ...), custom_call_target="tpu_custom_call" | custom-call | flops 2147483648 | bytes 4194304 | tf_op jit(solution)/shard_map/goals/pallas_call | solution.py:461
  78.0 0.0 collective-permute-done.9.other_ref
  78.0 1.1 %join.1 = bf16[16,72,512]{2,1,0:T(8,128)(2,1)} custom-call(bf16[16,72,512]{2,1,0:T(8,128)(2,1)S(1)} %get-tuple-element.55.own_ref, bf16[16,72,512]{2,1,0:T(8,128)(2,1)S(1)} %collective-permute-done.9.other_ref), custom_call_target="tpu_custom_call" | custom-call | tf_op jit(solution)/shard_map/join/pallas_call | solution.py:473
  79.1 7.2 %all-to-all-start.3 = ((bf16[16,72,512]{2,1,0:T(8,128)(2,1)}), bf16[16,72,512]{2,1,0:T(8,128)(2,1)S(1)}, u32[]{:S(2)}, u32[]{:S(2)}) async-start(bf16[16,72,512]{2,1,0:T(8,128)(2,1)} %join.1), calls=%async_computation.3 | async-start | bytes 2359296 | tf_op jit(solution)/shard_map/all_to_all | solution.py:356
  86.4 0.6 collective-permute-start.12
  87.0 0.4 collective-permute-start.13
  87.4 2.2 %collective-permute-start.15 = (bf16[136,512]{1,0:T(8,128)(2,1)S(1)}, bf16[136,512]{1,0:T(8,128)(2,1)S(1)}, u32[]{:S(2)}, u32[]{:S(2)}) collective-permute-start(bf16[136,512]{1,0:T(8,128)(2,1)S(1)} %get-tuple-element.75), channel_id=1, source_target_pairs={{0,7},{1,0},{2,1},{3,2},{4,3},{5,4},{6,5},{7,6},{8,15},{9,8},{10,9... | collective-permute-start | bytes 417800 | tf_op jit(solution)/shard_map/ppermute | solution.py:362
  89.6 1.5 %collective-permute-start.10 = (bf16[136,512]{1,0:T(8,128)(2,1)S(1)}, bf16[136,512]{1,0:T(8,128)(2,1)S(1)}, u32[]{:S(2)}, u32[]{:S(2)}) collective-permute-start(bf16[136,512]{1,0:T(8,128)(2,1)S(1)} %get-tuple-element.69), channel_id=1, source_target_pairs={{0,1},{1,2},{2,3},{3,4},{4,5},{5,6},{6,7},{7,0},{8,9},{9,10},{10,1... | collective-permute-start | bytes 417800 | tf_op jit(solution)/shard_map/ppermute | solution.py:362
  91.1 1.8 %collective-permute-start.11 = (bf16[136,512]{1,0:T(8,128)(2,1)S(1)}, bf16[136,512]{1,0:T(8,128)(2,1)S(1)}, u32[]{:S(2)}, u32[]{:S(2)}) collective-permute-start(bf16[136,512]{1,0:T(8,128)(2,1)S(1)} %get-tuple-element.70), channel_id=1, source_target_pairs={{0,7},{1,0},{2,1},{3,2},{4,3},{5,4},{6,5},{7,6},{8,15},{9,8},{10,9... | collective-permute-start | bytes 417800 | tf_op jit(solution)/shard_map/ppermute | solution.py:362
  92.9 4.5 %collective-permute-done.12.refs_1_ = bf16[136,512]{1,0:T(8,128)(2,1)S(1)} collective-permute-done((bf16[136,512]{1,0:T(8,128)(2,1)}, bf16[136,512]{1,0:T(8,128)(2,1)S(1)}, u32[]{:S(2)}, u32[]{:S(2)}) %collective-permute-start.12) | collective-permute-done | bytes 139296 | tf_op jit(solution)/shard_map/ppermute | solution.py:362
  97.3 0.0 collective-permute-done.13.refs_2_
  97.3 0.6 relay.2
  98.0 0.3 collective-permute-start.14
  98.3 0.5 collective-permute-done.15.refs_1_
  98.8 0.6 relay.3
  99.5 3.4 %collective-permute-start.16 = (bf16[136,512]{1,0:T(8,128)(2,1)S(1)}, bf16[136,512]{1,0:T(8,128)(2,1)S(1)}, u32[]{:S(2)}, u32[]{:S(2)}) collective-permute-start(bf16[136,512]{1,0:T(8,128)(2,1)S(1)} %relay.3), channel_id=1, source_target_pairs={{0,6},{1,7},{2,0},{3,1},{4,2},{5,3},{6,4},{7,5},{8,14},{9,15},{10,... | collective-permute-start | bytes 417800 | tf_op jit(solution)/shard_map/ppermute | solution.py:362
  102.9 0.0 collective-permute-done.10.refs_1_
  102.9 0.0 collective-permute-done.11.refs_2_
  102.9 3.2 %collective-permute-done.14.refs_3_ = bf16[136,512]{1,0:T(8,128)(2,1)S(1)} collective-permute-done((bf16[136,512]{1,0:T(8,128)(2,1)S(1)}, bf16[136,512]{1,0:T(8,128)(2,1)S(1)}, u32[]{:S(2)}, u32[]{:S(2)}) %collective-permute-start.14) | collective-permute-done | bytes 139296 | tf_op jit(solution)/shard_map/ppermute | solution.py:362
  106.1 0.5 collective-permute-done.16.refs_4_
  106.6 0.0 all-to-all-done.3.phi_parts_ref
  106.6 0.9 totals.1
  (1 shorter events, 0.0 us)
Async XLA Ops:
  2.7 7.6 %copy-start = (bf16[128,512]{1,0:T(8,128)(2,1)S(1)}, bf16[128,512]{1,0:T(8,128)(2,1)}, u32[]{:S(2)}) copy-start(bf16[128,512]{1,0:T(8,128)(2,1)} %refs_0_) | copy-start | bytes 393220
  2.7 31.8 %all-to-all-start = ((bf16[16,72,512]{2,1,0:T(8,128)(2,1)}), bf16[16,72,512]{2,1,0:T(8,128)(2,1)S(1)}, u32[]{:S(2)}, u32[]{:S(2)}) async-start(bf16[16,72,512]{2,1,0:T(8,128)(2,1)} %pack.1), calls=%async_computation | async-start | bytes 2359296 | tf_op jit(solution)/shard_map/all_to_all | solution.py:356
  10.2 12.2 %collective-permute-start.3 = (bf16[128,512]{1,0:T(8,128)(2,1)S(1)}, bf16[128,512]{1,0:T(8,128)(2,1)S(1)}, u32[]{:S(2)}, u32[]{:S(2)}) collective-permute-start(bf16[128,512]{1,0:T(8,128)(2,1)S(1)} %copy-done), channel_id=1, source_target_pairs={{0,6},{1,7},{2,0},{3,1},{4,2},{5,3},{6,4},{7,5},{8,14},{9,15},{10,... | collective-permute-start | bytes 393224 | tf_op jit(solution)/shard_map/ppermute | solution.py:362
  16.6 10.1 %collective-permute-start.1 = (bf16[128,512]{1,0:T(8,128)(2,1)S(1)}, bf16[128,512]{1,0:T(8,128)(2,1)S(1)}, u32[]{:S(2)}, u32[]{:S(2)}) collective-permute-start(bf16[128,512]{1,0:T(8,128)(2,1)S(1)} %copy-done), channel_id=1, source_target_pairs={{0,2},{1,3},{2,4},{3,5},{4,6},{5,7},{6,0},{7,1},{8,10},{9,11},{10,... | collective-permute-start | bytes 393224 | tf_op jit(solution)/shard_map/ppermute | solution.py:362
  16.6 13.7 %collective-permute-start = (bf16[128,512]{1,0:T(8,128)(2,1)S(1)}, bf16[128,512]{1,0:T(8,128)(2,1)S(1)}, u32[]{:S(2)}, u32[]{:S(2)}) collective-permute-start(bf16[128,512]{1,0:T(8,128)(2,1)S(1)} %copy-done), channel_id=1, source_target_pairs={{0,1},{1,2},{2,3},{3,4},{4,5},{5,6},{6,7},{7,0},{8,9},{9,10},{10,1... | collective-permute-start | bytes 393224 | tf_op jit(solution)/shard_map/ppermute | solution.py:362
  17.6 12.7 %collective-permute-start.6 = (bf16[128,512]{1,0:T(8,128)(2,1)S(1)}, bf16[128,512]{1,0:T(8,128)(2,1)S(1)}, u32[]{:S(2)}, u32[]{:S(2)}) collective-permute-start(bf16[128,512]{1,0:T(8,128)(2,1)S(1)} %copy-done), channel_id=1, source_target_pairs={{0,7},{1,0},{2,1},{3,2},{4,3},{5,4},{6,5},{7,6},{8,15},{9,8},{10,9... | collective-permute-start | bytes 393224 | tf_op jit(solution)/shard_map/ppermute | solution.py:362
  22.4 7.9 %collective-permute-start.5 = (bf16[128,512]{1,0:T(8,128)(2,1)S(1)}, bf16[128,512]{1,0:T(8,128)(2,1)S(1)}, u32[]{:S(2)}, u32[]{:S(2)}) collective-permute-start(bf16[128,512]{1,0:T(8,128)(2,1)S(1)} %collective-permute-done.3.refs_6_), channel_id=1, source_target_pairs={{0,7},{1,0},{2,1},{3,2},{4,3},{5,4},{6,5},{7,6},{8,15},{9,8},{10,9... | collective-permute-start | bytes 393224 | tf_op jit(solution)/shard_map/ppermute | solution.py:362
  26.7 7.3 %collective-permute-start.4 = (bf16[128,512]{1,0:T(8,128)(2,1)S(1)}, bf16[128,512]{1,0:T(8,128)(2,1)S(1)}, u32[]{:S(2)}, u32[]{:S(2)}) collective-permute-start(bf16[128,512]{1,0:T(8,128)(2,1)S(1)} %broadcast_select_fusion), channel_id=1, source_target_pairs={{0,2},{1,7},{2,4},{3,1},{4,6},{5,3},{6,0},{7,5},{8,10},{9,15},{10,... | collective-permute-start | bytes 393224 | tf_op jit(solution)/shard_map/ppermute | solution.py:391
  26.8 7.7 %collective-permute-start.2 = (bf16[128,512]{1,0:T(8,128)(2,1)S(1)}, bf16[128,512]{1,0:T(8,128)(2,1)S(1)}, u32[]{:S(2)}, u32[]{:S(2)}) collective-permute-start(bf16[128,512]{1,0:T(8,128)(2,1)S(1)} %collective-permute-done.1.refs_2_), channel_id=1, source_target_pairs={{0,1},{1,2},{2,3},{3,4},{4,5},{5,6},{6,7},{7,0},{8,9},{9,10},{10,1... | collective-permute-start | bytes 393224 | tf_op jit(solution)/shard_map/ppermute | solution.py:362
  34.5 2.8 %collective-permute-start.7 = (bf16[16,72,512]{2,1,0:T(8,128)(2,1)S(1)}, bf16[16,72,512]{2,1,0:T(8,128)(2,1)S(1)}, u32[]{:S(2)}, u32[]{:S(2)}) collective-permute-start(bf16[16,72,512]{2,1,0:T(8,128)(2,1)S(1)} %all-to-all-done.phi_ref.own_ref), channel_id=1, source_target_pairs={{0,32},{32,0},{1,33},{33,1},{2,34},{34,2},{3,35},{35,3},{4,36},{36... | collective-permute-start | bytes 3538952 | tf_op jit(solution)/shard_map/ppermute | solution.py:359
  40.4 13.7 %all-to-all-start.1 = ((f32[16,16,128]{2,1,0:T(8,128)}), f32[16,16,128]{2,1,0:T(8,128)S(1)}, u32[]{:S(2)}, u32[]{:S(2)}) async-start(f32[16,16,128]{2,1,0:T(8,128)} %all_rows.1), calls=%async_computation.1 | async-start | bytes 262144 | tf_op jit(solution)/shard_map/all_to_all | solution.py:356
  54.0 12.6 %all-to-all-start.2 = ((f32[8,24,128]{2,1,0:T(8,128)}), f32[8,24,128]{2,1,0:T(8,128)S(1)}, u32[]{:S(2)}, u32[]{:S(2)}) async-start(f32[8,24,128]{2,1,0:T(8,128)} %cols.1), calls=%async_computation.2 | async-start | bytes 196608 | tf_op jit(solution)/shard_map/all_to_all | solution.py:356
  57.9 1.3 %collective-permute-start.8 = (f32[16,16,128]{2,1,0:T(8,128)S(1)}, f32[16,16,128]{2,1,0:T(8,128)S(1)}, u32[]{:S(2)}, u32[]{:S(2)}) collective-permute-start(f32[16,16,128]{2,1,0:T(8,128)S(1)} %all-to-all-done.1.rows_ref), channel_id=1, source_target_pairs={{0,32},{32,0},{1,33},{33,1},{2,34},{34,2},{3,35},{35,3},{4,36},{36... | collective-permute-start | bytes 393224 | tf_op jit(solution)/shard_map/ppermute | solution.py:359
  74.0 4.0 %collective-permute-start.9 = (bf16[16,72,512]{2,1,0:T(8,128)(2,1)S(1)}, bf16[16,72,512]{2,1,0:T(8,128)(2,1)S(1)}, u32[]{:S(2)}, u32[]{:S(2)}) collective-permute-start(bf16[16,72,512]{2,1,0:T(8,128)(2,1)S(1)} %get-tuple-element.56), channel_id=1, source_target_pairs={{0,32},{32,0},{1,33},{33,1},{2,34},{34,2},{3,35},{35,3},{4,36},{36... | collective-permute-start | bytes 3538952 | tf_op jit(solution)/shard_map/ppermute | solution.py:359
  79.1 27.5 %all-to-all-start.3 = ((bf16[16,72,512]{2,1,0:T(8,128)(2,1)}), bf16[16,72,512]{2,1,0:T(8,128)(2,1)S(1)}, u32[]{:S(2)}, u32[]{:S(2)}) async-start(bf16[16,72,512]{2,1,0:T(8,128)(2,1)} %join.1), calls=%async_computation.3 | async-start | bytes 2359296 | tf_op jit(solution)/shard_map/all_to_all | solution.py:356
  86.4 11.0 %collective-permute-start.12 = (bf16[136,512]{1,0:T(8,128)(2,1)}, bf16[136,512]{1,0:T(8,128)(2,1)S(1)}, u32[]{:S(2)}, u32[]{:S(2)}) collective-permute-start(bf16[136,512]{1,0:T(8,128)(2,1)} %get-tuple-element.72), channel_id=1, source_target_pairs={{0,1},{1,2},{2,3},{3,4},{4,5},{5,6},{6,7},{7,0},{8,9},{9,10},{10,1... | collective-permute-start | bytes 417800 | tf_op jit(solution)/shard_map/ppermute | solution.py:362
  87.0 10.4 %collective-permute-start.13 = (bf16[136,512]{1,0:T(8,128)(2,1)}, bf16[136,512]{1,0:T(8,128)(2,1)S(1)}, u32[]{:S(2)}, u32[]{:S(2)}) collective-permute-start(bf16[136,512]{1,0:T(8,128)(2,1)} %get-tuple-element.73), channel_id=1, source_target_pairs={{0,2},{1,7},{2,4},{3,1},{4,6},{5,3},{6,0},{7,5},{8,10},{9,15},{10,... | collective-permute-start | bytes 417800 | tf_op jit(solution)/shard_map/ppermute | solution.py:494
  87.4 11.5 %collective-permute-start.15 = (bf16[136,512]{1,0:T(8,128)(2,1)S(1)}, bf16[136,512]{1,0:T(8,128)(2,1)S(1)}, u32[]{:S(2)}, u32[]{:S(2)}) collective-permute-start(bf16[136,512]{1,0:T(8,128)(2,1)S(1)} %get-tuple-element.75), channel_id=1, source_target_pairs={{0,7},{1,0},{2,1},{3,2},{4,3},{5,4},{6,5},{7,6},{8,15},{9,8},{10,9... | collective-permute-start | bytes 417800 | tf_op jit(solution)/shard_map/ppermute | solution.py:362
  89.6 13.3 %collective-permute-start.10 = (bf16[136,512]{1,0:T(8,128)(2,1)S(1)}, bf16[136,512]{1,0:T(8,128)(2,1)S(1)}, u32[]{:S(2)}, u32[]{:S(2)}) collective-permute-start(bf16[136,512]{1,0:T(8,128)(2,1)S(1)} %get-tuple-element.69), channel_id=1, source_target_pairs={{0,1},{1,2},{2,3},{3,4},{4,5},{5,6},{6,7},{7,0},{8,9},{9,10},{10,1... | collective-permute-start | bytes 417800 | tf_op jit(solution)/shard_map/ppermute | solution.py:362
  91.1 11.8 %collective-permute-start.11 = (bf16[136,512]{1,0:T(8,128)(2,1)S(1)}, bf16[136,512]{1,0:T(8,128)(2,1)S(1)}, u32[]{:S(2)}, u32[]{:S(2)}) collective-permute-start(bf16[136,512]{1,0:T(8,128)(2,1)S(1)} %get-tuple-element.70), channel_id=1, source_target_pairs={{0,7},{1,0},{2,1},{3,2},{4,3},{5,4},{6,5},{7,6},{8,15},{9,8},{10,9... | collective-permute-start | bytes 417800 | tf_op jit(solution)/shard_map/ppermute | solution.py:362
  98.0 8.1 %collective-permute-start.14 = (bf16[136,512]{1,0:T(8,128)(2,1)S(1)}, bf16[136,512]{1,0:T(8,128)(2,1)S(1)}, u32[]{:S(2)}, u32[]{:S(2)}) collective-permute-start(bf16[136,512]{1,0:T(8,128)(2,1)S(1)} %relay.2), channel_id=1, source_target_pairs={{0,2},{1,3},{2,4},{3,5},{4,6},{5,7},{6,0},{7,1},{8,10},{9,11},{10,... | collective-permute-start | bytes 417800 | tf_op jit(solution)/shard_map/ppermute | solution.py:362
  99.5 7.1 %collective-permute-start.16 = (bf16[136,512]{1,0:T(8,128)(2,1)S(1)}, bf16[136,512]{1,0:T(8,128)(2,1)S(1)}, u32[]{:S(2)}, u32[]{:S(2)}) collective-permute-start(bf16[136,512]{1,0:T(8,128)(2,1)S(1)} %relay.3), channel_id=1, source_target_pairs={{0,6},{1,7},{2,0},{3,1},{4,2},{5,3},{6,4},{7,5},{8,14},{9,15},{10,... | collective-permute-start | bytes 417800 | tf_op jit(solution)/shard_map/ppermute | solution.py:362

commit v6 on v5

--- a/solution.py
+++ b/solution.py
@@ -55,11 +55,26 @@
         psi_ref[pl.ds(pl.multiple_of(slot * shard, shard), shard), :] = piece[...]
 
 
+def fold_rows(ref, first, count, shard):
+    parts = range((ref.shape[1] - EXTRA) // shard)
+    cut = slice(first, first + count)
+    parts = [ref[cut, t * shard : (t + 1) * shard, :] for t in parts]
+    parts = [part.reshape(count * shard, LANES) for part in parts]
+    return jnp.concatenate(parts, axis=1)
+
+
+def put_rows(ref, first, count, shard, rows):
+    for t in range(rows.shape[1] // LANES):
+        part = rows[:, t * LANES : (t + 1) * LANES].reshape(count, shard, LANES)
+        ref[first : first + count, t * shard : (t + 1) * shard, :] = part
+
+
 def row_places(phi_ref, first, shards, shard):
     out = []
     for k in range(shards):
         block = phi_ref[first + k]
-        code = to_rows(block[shard : shard + 1, :LANES].astype(jnp.float32))
+        last = block.shape[0] - EXTRA
+        code = to_rows(block[last : last + 1, :].astype(jnp.float32))
         out.append(code[:shard] * 256.0 + code[shard : 2 * shard])
     return jnp.concatenate(out, axis=0)
 
@@ -75,19 +90,21 @@
 
 def pack_kernel(phi_in, pos_in, out_ref, block_ref, pos_ref, sems, sem):
     shard, width = phi_in.shape
-    loads = [
-        pltpu.make_async_copy(pos_in, pos_ref, sems.at[0]),
-        pltpu.make_async_copy(phi_in, block_ref.at[:shard], sems.at[1]),
-    ]
+    loads = [pltpu.make_async_copy(pos_in, pos_ref, sems.at[0])]
+    for t in range(width // LANES):
+        part = phi_in.at[:, t * LANES : (t + 1) * LANES]
+        held = block_ref.at[t * shard : (t + 1) * shard]
+        loads.append(pltpu.make_async_copy(part, held, sems.at[1 + t]))
     for load in loads:
         load.start()
     loads[0].wait()
     places = pos_ref[...]
     high = lax.shift_right_logical(places, 8)
     code = jnp.concatenate([high, places - high * 256], axis=1).astype(jnp.float32)
-    code = jnp.concatenate([code, jnp.zeros((1, width - 2 * shard), jnp.float32)], axis=1)
-    block_ref[shard:, :] = jnp.broadcast_to(code, (EXTRA, width)).astype(jnp.bfloat16)
-    loads[1].wait()
+    last = block_ref.shape[0] - EXTRA
+    block_ref[last:, :] = jnp.broadcast_to(code, (EXTRA, LANES)).astype(jnp.bfloat16)
+    for load in loads[1:]:
+        load.wait()
     copies = [
         pltpu.make_async_copy(block_ref, out_ref.at[k], sem.at[k])
         for k in range(out_ref.shape[0])
@@ -118,7 +135,7 @@
     per = CHUNK // shard
     out = []
     for _, _, first, ref in chunks_of((phi_ref,), shard):
-        rows = ref[first : first + per, :shard, :].reshape(CHUNK, -1)
+        rows = fold_rows(ref, first, per, shard)
         logits = nt(rows, psi) * scale2
         peak = jnp.max(logits, axis=1, keepdims=True)
         total = jnp.sum(jnp.exp2(logits - peak), axis=1, keepdims=True)
@@ -168,7 +185,7 @@
     count = jnp.zeros((LANES, LANES), jnp.float32)
     hit_sum = jnp.zeros((1, ncol), jnp.float32)
     for _, _, first, phi_ref in chunks_of((own_ref, other_ref), shard):
-        rows = phi_ref[first : first + per, :shard, :].reshape(CHUNK, -1)
+        rows = fold_rows(phi_ref, first, per, shard)
         logits = nt(rows, psi) * scale2
         new_max = jnp.maximum(col_max, jnp.max(logits, axis=0, keepdims=True))
         part = jnp.sum(jnp.exp2(logits - new_max), axis=0, keepdims=True)
@@ -221,7 +238,7 @@
     row_parts = jnp.concatenate([rows_ref[...], others_ref[...]], axis=0)
     row_peak = jnp.max(row_parts, axis=0)
     row_lse = row_peak + jnp.log2(jnp.sum(jnp.exp2(row_parts - row_peak[None]), axis=0))
-    tail_ref[...] = tail_rows(jnp.sum(row_lse, keepdims=True), width)
+    tail_ref[...] = tail_rows(jnp.sum(row_lse, keepdims=True), LANES)
     shift_ref[...] = row_lse - shift2
 
     col_parts = cols_ref[:, :nline, :]
@@ -230,7 +247,8 @@
     counts = jnp.sum(cols_ref[:, nline : 2 * nline, :], axis=0)
     hits = jnp.sum(cols_ref[:, 2 * nline :, :], axis=0)
     col_total = jnp.sum(counts * col_lse - 2.0 * hits, keepdims=True)
-    tail = jnp.broadcast_to(tail_rows(col_total, width)[None], (plane, EXTRA, width))
+    last = gown_ref.shape[1] - EXTRA
+    tail = jnp.broadcast_to(tail_rows(col_total, LANES)[None], (plane, EXTRA, LANES))
     line = col_lse - jnp.log2(counts) - shift2
     line = jnp.concatenate([line[t : t + 1] for t in range(nline)], axis=1)
 
@@ -238,7 +256,7 @@
     psi = psi_ref[...]
     chunks = chunks_of((own_ref, other_ref), shard)
     for number, half, first, phi_ref in chunks:
-        rows = phi_ref[first : first + per, :shard, :].reshape(CHUNK, width)
+        rows = fold_rows(phi_ref, first, per, shard)
         logits = nt(rows, psi) * scale2
         at = line_of(place_ref, number, half, len(chunks))
         lse = jnp.concatenate(
@@ -254,24 +272,24 @@
         if (first + per) % GROUP == 0:
             end = (number + 1) * CHUNK
             part = nn(w_ref[end - GROUP * shard : end, :], psi).astype(jnp.bfloat16)
-            block = slice(first + per - GROUP, first + per)
-            out_ref[block, :shard, :] = part.reshape(GROUP, shard, width)
-    gown_ref[:, shard:, :] = tail
-    gother_ref[:, shard:, :] = tail
-
-
-def join_kernel(shard, own_ref, other_ref, out, out_ref, sems):
-    npeer, _, width = own_ref.shape
+            put_rows(out_ref, first + per - GROUP, GROUP, shard, part)
+    gown_ref[:, last:, :] = tail
+    gother_ref[:, last:, :] = tail
+
+
+def join_kernel(own_ref, other_ref, out, out_ref, sems):
+    npeer = own_ref.shape[0]
+    last = own_ref.shape[1] - EXTRA
     copies = []
     for k in range(npeer):
         total = own_ref[k].astype(jnp.float32) + other_ref[k].astype(jnp.float32)
-        out_ref[k, :shard, :] = total[:shard].astype(jnp.bfloat16)
+        out_ref[k, :last, :] = total[:last].astype(jnp.bfloat16)
         if k == 0:
             loss = jnp.zeros((1, LANES), jnp.float32)
             for r in range(3):
-                loss = loss + total[shard + r : shard + r + 1, :LANES]
-            tail = tail_rows(loss[:, :1], width)
-        out_ref[k, shard:, :] = tail
+                loss = loss + total[last + r : last + r + 1]
+            tail = tail_rows(loss[:, :1], LANES)
+        out_ref[k, last:, :] = tail
         if k % 4 == 3:
             cut = pl.ds(k - 3, 4)
             copies.append(
@@ -287,9 +305,8 @@
     gpsi_refs = refs[:nz]
     (acc_ref,) = refs[nz:]
     nrow, ncol = w_ref.shape
-    own = own_ref[:, :shard, :].reshape(nrow // 2, -1)
-    other = other_ref[:, :shard, :].reshape(nrow // 2, -1)
-    rows = jnp.concatenate([own, other], axis=0)
+    halves = [fold_rows(ref, 0, ref.shape[0], shard) for ref in (own_ref, other_ref)]
+    rows = jnp.concatenate(halves, axis=0)
     for c in range(ncol // CHUNK):
         cut = slice(c * CHUNK, (c + 1) * CHUNK)
         acc_ref[cut, :] = tn(w_ref[:, cut], rows).astype(jnp.bfloat16)
@@ -297,8 +314,11 @@
     piece = ncol // nz
     for out, shift in zip(gpsi_refs, (0,) + SHIFTS):
         slot = lax.rem(own + shift, nz)
-        out[:piece, :] = acc_ref[pl.ds(pl.multiple_of(slot * piece, piece), piece), :]
-        out[piece:, :] = tail_ref[...]
+        part = acc_ref[pl.ds(pl.multiple_of(slot * piece, piece), piece), :]
+        for t in range(part.shape[1] // LANES):
+            cut = slice(t * LANES, (t + 1) * LANES)
+            out[t * piece : (t + 1) * piece, :] = part[:, cut]
+        out[out.shape[0] - EXTRA :, :] = tail_ref[...]
 
 
 def relay_kernel(parity, place_ref, *refs):
@@ -325,16 +345,20 @@
     total = phi_parts_ref[0].astype(jnp.float32)
     for k in range(1, phi_parts_ref.shape[0]):
         total = total + phi_parts_ref[k].astype(jnp.float32)
-    gphi_ref[...] = total[:shard]
-    loss = total[shard : shard + 1, :LANES]
+    for t in range(gphi_ref.shape[1] // LANES):
+        gphi_ref[:, t * LANES : (t + 1) * LANES] = total[t * shard : (t + 1) * shard]
+    last = total.shape[0] - EXTRA
+    loss = total[last : last + 1]
     for r in range(1, 3):
-        loss = loss + total[shard + r : shard + r + 1, :LANES]
+        loss = loss + total[last + r : last + r + 1]
     total = parts[0][...].astype(jnp.float32)
     for part in parts[1:]:
         total = total + part[...].astype(jnp.float32)
-    gpsi_ref[...] = total[:piece]
+    for t in range(gpsi_ref.shape[1] // LANES):
+        gpsi_ref[:, t * LANES : (t + 1) * LANES] = total[t * piece : (t + 1) * piece]
+    last = total.shape[0] - EXTRA
     for r in range(3):
-        loss = loss + total[piece + r : piece + r + 1, :LANES]
+        loss = loss + total[last + r : last + r + 1]
     loss_ref[...] = loss[:, :1] * (math.log(2.0) / nrow)
 
 
@@ -367,15 +391,17 @@
     params = pltpu.CompilerParams(vmem_limit_bytes=VMEM_LIMIT)
 
     nplane = npeer // 2
+    fold = shard * width // LANES + EXTRA
+    half = jax.ShapeDtypeStruct((nplane, fold, LANES), jnp.bfloat16)
     packed = pl.pallas_call(
         pack_kernel,
-        out_shape=pltpu.HBM((nplane, shard + EXTRA, width), jnp.bfloat16),
+        out_shape=pltpu.HBM(half.shape, half.dtype),
         in_specs=[hbm] * 2,
         out_specs=hbm,
         scratch_shapes=[
-            pltpu.VMEM((shard + EXTRA, width), jnp.bfloat16),
+            pltpu.VMEM(half.shape[1:], half.dtype),
             pltpu.VMEM((1, shard), jnp.int32),
-            pltpu.SemaphoreType.DMA((2,)),
+            pltpu.SemaphoreType.DMA((1 + width // LANES,)),
             pltpu.SemaphoreType.DMA((nplane,)),
         ],
         compiler_params=params,
@@ -446,10 +472,9 @@
     row_others = swap(row_parts)
     col_parts = spread(col_stats, "z")
 
-    half = jax.ShapeDtypeStruct((nplane, shard + EXTRA, width), jnp.bfloat16)
     gown, gother, weights, tail = pl.pallas_call(
         functools.partial(weights_kernel, scale, scale2, shard),
-        out_shape=(half, half, tile, jax.ShapeDtypeStruct((EXTRA, width), jnp.bfloat16)),
+        out_shape=(half, half, tile, jax.ShapeDtypeStruct((EXTRA, LANES), jnp.bfloat16)),
         in_specs=[smem] + [vmem] * 2 + [hbm] + [vmem] * 3,
         out_specs=(vmem,) * 4,
         scratch_shapes=[pltpu.VMEM((nrow // LANES, LANES), jnp.float32), psi_scratch, dma],
@@ -457,7 +482,7 @@
         cost_estimate=cost(2),
         name="weights",
     )(place, own, other, psi_all, row_parts, row_others, col_parts)
-    part = jax.ShapeDtypeStruct((piece + EXTRA, width), jnp.bfloat16)
+    part = jax.ShapeDtypeStruct((piece * width // LANES + EXTRA, LANES), jnp.bfloat16)
     gpsi = pl.pallas_call(
         functools.partial(goals_kernel, shard),
         out_shape=(part,) * nz,
@@ -471,7 +496,7 @@
 
     other_part, *gpsi = lax.optimization_barrier((swap(gother), *gpsi))
     joined = pl.pallas_call(
-        functools.partial(join_kernel, shard),
+        join_kernel,
         out_shape=pltpu.HBM(half.shape, half.dtype),
         in_specs=[vmem] * 2,
         out_specs=hbm,

time: 108 us -> 107 us (level)
  transfers between devices with their start and end apart: 21 -> 21, of which waited for: 12 -> 12; matrix products, arithmetic and copies ran while one was open for 0% -> 0% of each run, Pallas kernels for 13% -> 12%
where the time goes in v6:
time: 107 us; the launch traced here: 106 us
  starting transfers between devices  51.4 us (48%)
  Pallas kernels  27.5 us (26%)
  waiting for transfers between devices  26.3 us (25%)
    all_to_all x4, starting transfers between devices, spread(): return lax.all_to_all(array, axes, 0, 0, tiled=True)  25.8 us
    ppermute x12, starting transfers between devices, move(): return lax.ppermute(array, 'z', [(i, (i + shift) % nz) for i in range(nz)])  24.8 us
    ppermute x12, waiting for transfers between devices, move(): return lax.ppermute(array, 'z', [(i, (i + shift) % nz) for i in range(nz)])  13.7 us
    all_to_all x4, waiting for transfers between devices, spread(): return lax.all_to_all(array, axes, 0, 0, tiled=True)  7.39 us
    pallas_call x1, Pallas kernels, shards(): pl.pallas_call(functools.partial(weights_kernel, scale, scale2, shard), o...  7.31 us
    pallas_call x1, Pallas kernels, shards(): pl.pallas_call(functools.partial(cols_kernel, scale2, shard), out_shape=j...  6.49 us
    ppermute x1, waiting for transfers between devices, shards(): near[4] = lax.ppermute(jnp.where(even, near[2], near[6]), 'z', across)  3.63 us
    pallas_call x1, Pallas kernels, shards(): pl.pallas_call(functools.partial(goals_kernel, shard), out_shape=(part,)...  3.06 us
  transfers between devices with their start and end apart: 21, of which 12 were waited for; matrix products, arithmetic and copies ran while one was open for 0% of the time, Pallas kernels for 12%

profile of v6, /device:TPU:8, one launch (start us, length us, event | category | flops | bytes accessed | tf_op | source)
XLA Modules:
  0.0 106.1 jit_solution(5954457398934660812)
XLA Ops:
  0.6 2.0 %pack.1 = bf16[16,264,128]{2,1,0:T(8,128)(2,1)} custom-call(bf16[64,512]{1,0:T(8,128)(2,1)} %phi_in.1, s32[1,64]{1,0:T(1,128)} %bitcast.5), custom_call_target="tpu_custom_call" | custom-call | tf_op jit(solution)/shard_map/pack/pallas_call | solution.py:396
  2.6 0.0 copy-start
  2.6 7.5 %all-to-all-start = ((bf16[16,264,128]{2,1,0:T(8,128)(2,1)}), bf16[16,264,128]{2,1,0:T(8,128)(2,1)S(1)}, u32[]{:S(2)}, u32[]{:S(2)}) async-start(bf16[16,264,128]{2,1,0:T(8,128)(2,1)} %pack.1), calls=%async_computation | async-start | bytes 2162688 | tf_op jit(solution)/shard_map/all_to_all | solution.py:380
  10.1 0.0 copy-done
  10.2 6.4 %collective-permute-start.3 = (bf16[128,512]{1,0:T(8,128)(2,1)S(1)}, bf16[128,512]{1,0:T(8,128)(2,1)S(1)}, u32[]{:S(2)}, u32[]{:S(2)}) collective-permute-start(bf16[128,512]{1,0:T(8,128)(2,1)S(1)} %copy-done), channel_id=1, source_target_pairs={{0,6},{1,7},{2,0},{3,1},{4,2},{5,3},{6,4},{7,5},{8,14},{9,15},{10,... | collective-permute-start | bytes 393224 | tf_op jit(solution)/shard_map/ppermute | solution.py:386
  16.5 0.0 collective-permute-start.1
  16.5 1.0 collective-permute-start
  17.6 2.7 %collective-permute-start.6 = (bf16[128,512]{1,0:T(8,128)(2,1)S(1)}, bf16[128,512]{1,0:T(8,128)(2,1)S(1)}, u32[]{:S(2)}, u32[]{:S(2)}) collective-permute-start(bf16[128,512]{1,0:T(8,128)(2,1)S(1)} %copy-done), channel_id=1, source_target_pairs={{0,7},{1,0},{2,1},{3,2},{4,3},{5,4},{6,5},{7,6},{8,15},{9,8},{10,9... | collective-permute-start | bytes 393224 | tf_op jit(solution)/shard_map/ppermute | solution.py:386
  20.2 2.1 %collective-permute-done.3.refs_6_ = bf16[128,512]{1,0:T(8,128)(2,1)S(1)} collective-permute-done((bf16[128,512]{1,0:T(8,128)(2,1)S(1)}, bf16[128,512]{1,0:T(8,128)(2,1)S(1)}, u32[]{:S(2)}, u32[]{:S(2)}) %collective-permute-start.3) | collective-permute-done | bytes 131104 | tf_op jit(solution)/shard_map/ppermute | solution.py:386
  22.3 2.5 %collective-permute-start.5 = (bf16[128,512]{1,0:T(8,128)(2,1)S(1)}, bf16[128,512]{1,0:T(8,128)(2,1)S(1)}, u32[]{:S(2)}, u32[]{:S(2)}) collective-permute-start(bf16[128,512]{1,0:T(8,128)(2,1)S(1)} %collective-permute-done.3.refs_6_), channel_id=1, source_target_pairs={{0,7},{1,0},{2,1},{3,2},{4,3},{5,4},{6,5},{7,6},{8,15},{9,8},{10,9... | collective-permute-start | bytes 393224 | tf_op jit(solution)/shard_map/ppermute | solution.py:386
  24.8 1.8 %collective-permute-done.1.refs_2_ = bf16[128,512]{1,0:T(8,128)(2,1)S(1)} collective-permute-done((bf16[128,512]{1,0:T(8,128)(2,1)S(1)}, bf16[128,512]{1,0:T(8,128)(2,1)S(1)}, u32[]{:S(2)}, u32[]{:S(2)}) %collective-permute-start.1) | collective-permute-done | bytes 131104 | tf_op jit(solution)/shard_map/ppermute | solution.py:386
  26.6 0.1 collective-permute-start.4
  26.7 2.5 %collective-permute-start.2 = (bf16[128,512]{1,0:T(8,128)(2,1)S(1)}, bf16[128,512]{1,0:T(8,128)(2,1)S(1)}, u32[]{:S(2)}, u32[]{:S(2)}) collective-permute-start(bf16[128,512]{1,0:T(8,128)(2,1)S(1)} %collective-permute-done.1.refs_2_), channel_id=1, source_target_pairs={{0,1},{1,2},{2,3},{3,4},{4,5},{5,6},{6,7},{7,0},{8,9},{9,10},{10,1... | collective-permute-start | bytes 393224 | tf_op jit(solution)/shard_map/ppermute | solution.py:386
  29.2 1.1 %collective-permute-done.refs_1_ = bf16[128,512]{1,0:T(8,128)(2,1)S(1)} collective-permute-done((bf16[128,512]{1,0:T(8,128)(2,1)S(1)}, bf16[128,512]{1,0:T(8,128)(2,1)S(1)}, u32[]{:S(2)}, u32[]{:S(2)}) %collective-permute-start) | collective-permute-done | bytes 131104 | tf_op jit(solution)/shard_map/ppermute | solution.py:386
  30.3 0.0 collective-permute-done.6.refs_7_
  30.3 0.0 collective-permute-done.5.refs_5_
  30.3 3.6 %collective-permute-done.4.refs_4_ = bf16[128,512]{1,0:T(8,128)(2,1)S(1)} collective-permute-done((bf16[128,512]{1,0:T(8,128)(2,1)S(1)}, bf16[128,512]{1,0:T(8,128)(2,1)S(1)}, u32[]{:S(2)}, u32[]{:S(2)}) %collective-permute-start.4) | collective-permute-done | bytes 131104 | tf_op jit(solution)/shard_map/ppermute | solution.py:417
  33.9 0.5 collective-permute-done.2.refs_3_
  34.4 0.0 all-to-all-done.phi_ref.own_ref
  34.4 0.0 collective-permute-start.7
  34.4 0.1 pad_add_fusion.place_ref
  34.5 2.4 %own_rows.1 = (f32[8,128]{1,0:T(8,128)S(1)}, bf16[1024,512]{1,0:T(8,128)(2,1)}, bf16[1024,512]{1,0:T(8,128)(2,1)S(1)}) custom-call(s32[3]{0:T(128)S(1)} %pad_add_fusion.place_ref, bf16[16,264,128]{2,1,0:T(8,128)(2,1)S(1)} %all-to-all-done.phi_ref.own_ref, bf16[128,512]{1,0:T(8,128)(2,1)S(1)} %copy-done, bf16[128,512]{1,0:T(8,128)(2,1)S(1)} %collective-permute-done.refs_1_, ...), custom_call_target="tpu_custom_call" | custom-call | flops 1073741824 | bytes 4194304 | tf_op jit(solution)/shard_map/own_rows/pallas_call | solution.py:435
  36.9 0.2 collective-permute-done.7.phi_ref.other_ref
  37.1 3.0 %all_rows.1 = f32[16,16,128]{2,1,0:T(8,128)} custom-call(s32[3]{0:T(128)S(1)} %pad_add_fusion.place_ref, bf16[16,264,128]{2,1,0:T(8,128)(2,1)S(1)} %collective-permute-done.7.phi_ref.other_ref, f32[8,128]{1,0:T(8,128)S(1)} %get-tuple-element.51.line_ref, bf16[1024,512]{1,0:T(8,128)(2,1)S(1)} %get-tuple-element.52.psi_ref), custom_call_target="tpu_custom_call" | custom-call | flops 1073741824 | bytes 4194304 | tf_op jit(solution)/shard_map/all_rows/pallas_call | solution.py:450
  40.2 7.1 %all-to-all-start.1 = ((f32[16,16,128]{2,1,0:T(8,128)}), f32[16,16,128]{2,1,0:T(8,128)S(1)}, u32[]{:S(2)}, u32[]{:S(2)}) async-start(f32[16,16,128]{2,1,0:T(8,128)} %all_rows.1), calls=%async_computation.1 | async-start | bytes 262144 | tf_op jit(solution)/shard_map/all_to_all | solution.py:380
  47.3 6.5 %cols.1 = f32[8,24,128]{2,1,0:T(8,128)} custom-call(s32[3]{0:T(128)S(1)} %pad_add_fusion.place_ref, bf16[16,264,128]{2,1,0:T(8,128)(2,1)S(1)} %all-to-all-done.phi_ref.own_ref, bf16[16,264,128]{2,1,0:T(8,128)(2,1)S(1)} %collective-permute-done.7.phi_ref.other_ref, bf16[1024,512]{1,0:T(8,128)(2,1)} %get-tuple-element.50.psi_in), custom_call_target="tpu_custom_call" | custom-call | flops 2147483648 | bytes 4194304 | tf_op jit(solution)/shard_map/cols/pallas_call | solution.py:461
  53.8 0.0 all-to-all-done.1.rows_ref
  53.8 3.9 %all-to-all-start.2 = ((f32[8,24,128]{2,1,0:T(8,128)}), f32[8,24,128]{2,1,0:T(8,128)S(1)}, u32[]{:S(2)}, u32[]{:S(2)}) async-start(f32[8,24,128]{2,1,0:T(8,128)} %cols.1), calls=%async_computation.2 | async-start | bytes 196608 | tf_op jit(solution)/shard_map/all_to_all | solution.py:380
  57.7 0.0 collective-permute-start.8
  57.7 1.3 %collective-permute-done.8.others_ref = f32[16,16,128]{2,1,0:T(8,128)S(1)} collective-permute-done((f32[16,16,128]{2,1,0:T(8,128)S(1)}, f32[16,16,128]{2,1,0:T(8,128)S(1)}, u32[]{:S(2)}, u32[]{:S(2)}) %collective-permute-start.8) | collective-permute-done | bytes 131104 | tf_op jit(solution)/shard_map/ppermute | solution.py:383
  59.0 7.4 %all-to-all-done.2.refs_0_ = f32[8,24,128]{2,1,0:T(8,128)S(1)} async-done(((f32[8,24,128]{2,1,0:T(8,128)}), f32[8,24,128]{2,1,0:T(8,128)S(1)}, u32[]{:S(2)}, u32[]{:S(2)}) %all-to-all-start.2) | async-done | bytes 98336 | tf_op jit(solution)/shard_map/all_to_all | solution.py:380
  66.4 7.3 %weights.1 = (bf16[16,264,128]{2,1,0:T(8,128)(2,1)S(1)}, bf16[16,264,128]{2,1,0:T(8,128)(2,1)S(1)}, bf16[2048,1024]{1,0:T(8,128)(2,1)S(1)}, bf16[8,128]{1,0:T(8,128)(2,1)S(1)}) custom-call(s32[3]{0:T(128)S(1)} %pad_add_fusion.place_ref, bf16[16,264,128]{2,1,0:T(8,128)(2,1)S(1)} %all-to-all-done.phi_ref.own_ref, ...), custom_call_target="tpu_custom_call" | custom-call | flops 4294967296 | bytes 4194304 | tf_op jit(solution)/shard_map/weights/pallas_call | solution.py:475
  73.7 0.3 collective-permute-start.9
  74.0 3.1 %goals.1 = (bf16[520,128]{1,0:T(8,128)(2,1)S(1)}, bf16[520,128]{1,0:T(8,128)(2,1)S(1)}, bf16[520,128]{1,0:T(8,128)(2,1)S(1)}, bf16[520,128]{1,0:T(8,128)(2,1)S(1...) custom-call(s32[3]{0:T(128)S(1)} %pad_add_fusion.place_ref, ...), custom_call_target="tpu_custom_call" | custom-call | flops 2147483648 | bytes 4194304 | tf_op jit(solution)/shard_map/goals/pallas_call | solution.py:486
  77.1 0.0 collective-permute-done.9.other_ref
  77.1 1.1 %join.1 = bf16[16,264,128]{2,1,0:T(8,128)(2,1)} custom-call(bf16[16,264,128]{2,1,0:T(8,128)(2,1)S(1)} %get-tuple-element.55.own_ref, bf16[16,264,128]{2,1,0:T(8,128)(2,1)S(1)} %collective-permute-done.9.other_ref), custom_call_target="tpu_custom_call" | custom-call | tf_op jit(solution)/shard_map/join/pallas_call | solution.py:498
  78.2 7.2 %all-to-all-start.3 = ((bf16[16,264,128]{2,1,0:T(8,128)(2,1)}), bf16[16,264,128]{2,1,0:T(8,128)(2,1)S(1)}, u32[]{:S(2)}, u32[]{:S(2)}) async-start(bf16[16,264,128]{2,1,0:T(8,128)(2,1)} %join.1), calls=%async_computation.3 | async-start | bytes 2162688 | tf_op jit(solution)/shard_map/all_to_all | solution.py:380
  85.5 0.6 collective-permute-start.12
  86.1 0.4 collective-permute-start.13
  86.5 2.2 %collective-permute-start.15 = (bf16[520,128]{1,0:T(8,128)(2,1)S(1)}, bf16[520,128]{1,0:T(8,128)(2,1)S(1)}, u32[]{:S(2)}, u32[]{:S(2)}) collective-permute-start(bf16[520,128]{1,0:T(8,128)(2,1)S(1)} %get-tuple-element.75), channel_id=1, source_target_pairs={{0,7},{1,0},{2,1},{3,2},{4,3},{5,4},{6,5},{7,6},{8,15},{9,8},{10,9... | collective-permute-start | bytes 399368 | tf_op jit(solution)/shard_map/ppermute | solution.py:386
  88.7 1.5 %collective-permute-start.10 = (bf16[520,128]{1,0:T(8,128)(2,1)S(1)}, bf16[520,128]{1,0:T(8,128)(2,1)S(1)}, u32[]{:S(2)}, u32[]{:S(2)}) collective-permute-start(bf16[520,128]{1,0:T(8,128)(2,1)S(1)} %get-tuple-element.69), channel_id=1, source_target_pairs={{0,1},{1,2},{2,3},{3,4},{4,5},{5,6},{6,7},{7,0},{8,9},{9,10},{10,1... | collective-permute-start | bytes 399368 | tf_op jit(solution)/shard_map/ppermute | solution.py:386
  90.2 1.8 %collective-permute-start.11 = (bf16[520,128]{1,0:T(8,128)(2,1)S(1)}, bf16[520,128]{1,0:T(8,128)(2,1)S(1)}, u32[]{:S(2)}, u32[]{:S(2)}) collective-permute-start(bf16[520,128]{1,0:T(8,128)(2,1)S(1)} %get-tuple-element.70), channel_id=1, source_target_pairs={{0,7},{1,0},{2,1},{3,2},{4,3},{5,4},{6,5},{7,6},{8,15},{9,8},{10,9... | collective-permute-start | bytes 399368 | tf_op jit(solution)/shard_map/ppermute | solution.py:386
  92.0 4.0 %collective-permute-done.12.refs_1_ = bf16[520,128]{1,0:T(8,128)(2,1)S(1)} collective-permute-done((bf16[520,128]{1,0:T(8,128)(2,1)S(1)}, bf16[520,128]{1,0:T(8,128)(2,1)S(1)}, u32[]{:S(2)}, u32[]{:S(2)}) %collective-permute-start.12) | collective-permute-done | bytes 133152 | tf_op jit(solution)/shard_map/ppermute | solution.py:386
  96.0 0.0 collective-permute-done.13.refs_2_
  96.0 0.6 relay.2
  96.6 0.3 collective-permute-start.14
  96.9 0.5 collective-permute-done.15.refs_1_
  97.5 0.6 relay.3
  98.1 3.4 %collective-permute-start.16 = (bf16[520,128]{1,0:T(8,128)(2,1)S(1)}, bf16[520,128]{1,0:T(8,128)(2,1)S(1)}, u32[]{:S(2)}, u32[]{:S(2)}) collective-permute-start(bf16[520,128]{1,0:T(8,128)(2,1)S(1)} %relay.3), channel_id=1, source_target_pairs={{0,6},{1,7},{2,0},{3,1},{4,2},{5,3},{6,4},{7,5},{8,14},{9,15},{10,... | collective-permute-start | bytes 399368 | tf_op jit(solution)/shard_map/ppermute | solution.py:386
  101.5 0.0 collective-permute-done.10.refs_1_
  101.5 0.0 collective-permute-done.11.refs_2_
  101.5 3.2 %collective-permute-done.14.refs_3_ = bf16[520,128]{1,0:T(8,128)(2,1)S(1)} collective-permute-done((bf16[520,128]{1,0:T(8,128)(2,1)S(1)}, bf16[520,128]{1,0:T(8,128)(2,1)S(1)}, u32[]{:S(2)}, u32[]{:S(2)}) %collective-permute-start.14) | collective-permute-done | bytes 133152 | tf_op jit(solution)/shard_map/ppermute | solution.py:386
  104.8 0.4 collective-permute-done.16.refs_4_
  105.2 0.0 all-to-all-done.3.phi_parts_ref
  105.2 0.9 totals.1
  (1 shorter events, 0.0 us)
Async XLA Ops:
  2.6 7.6 %copy-start = (bf16[128,512]{1,0:T(8,128)(2,1)S(1)}, bf16[128,512]{1,0:T(8,128)(2,1)}, u32[]{:S(2)}) copy-start(bf16[128,512]{1,0:T(8,128)(2,1)} %refs_0_) | copy-start | bytes 393220
  2.6 31.8 %all-to-all-start = ((bf16[16,264,128]{2,1,0:T(8,128)(2,1)}), bf16[16,264,128]{2,1,0:T(8,128)(2,1)S(1)}, u32[]{:S(2)}, u32[]{:S(2)}) async-start(bf16[16,264,128]{2,1,0:T(8,128)(2,1)} %pack.1), calls=%async_computation | async-start | bytes 2162688 | tf_op jit(solution)/shard_map/all_to_all | solution.py:380
  10.2 12.2 %collective-permute-start.3 = (bf16[128,512]{1,0:T(8,128)(2,1)S(1)}, bf16[128,512]{1,0:T(8,128)(2,1)S(1)}, u32[]{:S(2)}, u32[]{:S(2)}) collective-permute-start(bf16[128,512]{1,0:T(8,128)(2,1)S(1)} %copy-done), channel_id=1, source_target_pairs={{0,6},{1,7},{2,0},{3,1},{4,2},{5,3},{6,4},{7,5},{8,14},{9,15},{10,... | collective-permute-start | bytes 393224 | tf_op jit(solution)/shard_map/ppermute | solution.py:386
  16.5 10.1 %collective-permute-start.1 = (bf16[128,512]{1,0:T(8,128)(2,1)S(1)}, bf16[128,512]{1,0:T(8,128)(2,1)S(1)}, u32[]{:S(2)}, u32[]{:S(2)}) collective-permute-start(bf16[128,512]{1,0:T(8,128)(2,1)S(1)} %copy-done), channel_id=1, source_target_pairs={{0,2},{1,3},{2,4},{3,5},{4,6},{5,7},{6,0},{7,1},{8,10},{9,11},{10,... | collective-permute-start | bytes 393224 | tf_op jit(solution)/shard_map/ppermute | solution.py:386
  16.5 13.7 %collective-permute-start = (bf16[128,512]{1,0:T(8,128)(2,1)S(1)}, bf16[128,512]{1,0:T(8,128)(2,1)S(1)}, u32[]{:S(2)}, u32[]{:S(2)}) collective-permute-start(bf16[128,512]{1,0:T(8,128)(2,1)S(1)} %copy-done), channel_id=1, source_target_pairs={{0,1},{1,2},{2,3},{3,4},{4,5},{5,6},{6,7},{7,0},{8,9},{9,10},{10,1... | collective-permute-start | bytes 393224 | tf_op jit(solution)/shard_map/ppermute | solution.py:386
  17.6 12.7 %collective-permute-start.6 = (bf16[128,512]{1,0:T(8,128)(2,1)S(1)}, bf16[128,512]{1,0:T(8,128)(2,1)S(1)}, u32[]{:S(2)}, u32[]{:S(2)}) collective-permute-start(bf16[128,512]{1,0:T(8,128)(2,1)S(1)} %copy-done), channel_id=1, source_target_pairs={{0,7},{1,0},{2,1},{3,2},{4,3},{5,4},{6,5},{7,6},{8,15},{9,8},{10,9... | collective-permute-start | bytes 393224 | tf_op jit(solution)/shard_map/ppermute | solution.py:386
  22.3 7.9 %collective-permute-start.5 = (bf16[128,512]{1,0:T(8,128)(2,1)S(1)}, bf16[128,512]{1,0:T(8,128)(2,1)S(1)}, u32[]{:S(2)}, u32[]{:S(2)}) collective-permute-start(bf16[128,512]{1,0:T(8,128)(2,1)S(1)} %collective-permute-done.3.refs_6_), channel_id=1, source_target_pairs={{0,7},{1,0},{2,1},{3,2},{4,3},{5,4},{6,5},{7,6},{8,15},{9,8},{10,9... | collective-permute-start | bytes 393224 | tf_op jit(solution)/shard_map/ppermute | solution.py:386
  26.6 7.3 %collective-permute-start.4 = (bf16[128,512]{1,0:T(8,128)(2,1)S(1)}, bf16[128,512]{1,0:T(8,128)(2,1)S(1)}, u32[]{:S(2)}, u32[]{:S(2)}) collective-permute-start(bf16[128,512]{1,0:T(8,128)(2,1)S(1)} %broadcast_select_fusion), channel_id=1, source_target_pairs={{0,2},{1,7},{2,4},{3,1},{4,6},{5,3},{6,0},{7,5},{8,10},{9,15},{10,... | collective-permute-start | bytes 393224 | tf_op jit(solution)/shard_map/ppermute | solution.py:417
  26.7 7.7 %collective-permute-start.2 = (bf16[128,512]{1,0:T(8,128)(2,1)S(1)}, bf16[128,512]{1,0:T(8,128)(2,1)S(1)}, u32[]{:S(2)}, u32[]{:S(2)}) collective-permute-start(bf16[128,512]{1,0:T(8,128)(2,1)S(1)} %collective-permute-done.1.refs_2_), channel_id=1, source_target_pairs={{0,1},{1,2},{2,3},{3,4},{4,5},{5,6},{6,7},{7,0},{8,9},{9,10},{10,1... | collective-permute-start | bytes 393224 | tf_op jit(solution)/shard_map/ppermute | solution.py:386
  34.4 2.7 %collective-permute-start.7 = (bf16[16,264,128]{2,1,0:T(8,128)(2,1)S(1)}, bf16[16,264,128]{2,1,0:T(8,128)(2,1)S(1)}, u32[]{:S(2)}, u32[]{:S(2)}) collective-permute-start(bf16[16,264,128]{2,1,0:T(8,128)(2,1)S(1)} %all-to-all-done.phi_ref.own_ref), channel_id=1, source_target_pairs={{0,32},{32,0},{1,33},{33,1},{2,34},{34,2},{3,35},{35,3},{4,36},{36... | collective-permute-start | bytes 3244040 | tf_op jit(solution)/shard_map/ppermute | solution.py:383
  40.2 13.6 %all-to-all-start.1 = ((f32[16,16,128]{2,1,0:T(8,128)}), f32[16,16,128]{2,1,0:T(8,128)S(1)}, u32[]{:S(2)}, u32[]{:S(2)}) async-start(f32[16,16,128]{2,1,0:T(8,128)} %all_rows.1), calls=%async_computation.1 | async-start | bytes 262144 | tf_op jit(solution)/shard_map/all_to_all | solution.py:380
  53.8 12.6 %all-to-all-start.2 = ((f32[8,24,128]{2,1,0:T(8,128)}), f32[8,24,128]{2,1,0:T(8,128)S(1)}, u32[]{:S(2)}, u32[]{:S(2)}) async-start(f32[8,24,128]{2,1,0:T(8,128)} %cols.1), calls=%async_computation.2 | async-start | bytes 196608 | tf_op jit(solution)/shard_map/all_to_all | solution.py:380
  57.7 1.3 %collective-permute-start.8 = (f32[16,16,128]{2,1,0:T(8,128)S(1)}, f32[16,16,128]{2,1,0:T(8,128)S(1)}, u32[]{:S(2)}, u32[]{:S(2)}) collective-permute-start(f32[16,16,128]{2,1,0:T(8,128)S(1)} %all-to-all-done.1.rows_ref), channel_id=1, source_target_pairs={{0,32},{32,0},{1,33},{33,1},{2,34},{34,2},{3,35},{35,3},{4,36},{36... | collective-permute-start | bytes 393224 | tf_op jit(solution)/shard_map/ppermute | solution.py:383
  73.7 3.4 %collective-permute-start.9 = (bf16[16,264,128]{2,1,0:T(8,128)(2,1)S(1)}, bf16[16,264,128]{2,1,0:T(8,128)(2,1)S(1)}, u32[]{:S(2)}, u32[]{:S(2)}) collective-permute-start(bf16[16,264,128]{2,1,0:T(8,128)(2,1)S(1)} %get-tuple-element.56), channel_id=1, source_target_pairs={{0,32},{32,0},{1,33},{33,1},{2,34},{34,2},{3,35},{35,3},{4,36},{36... | collective-permute-start | bytes 3244040 | tf_op jit(solution)/shard_map/ppermute | solution.py:383
  78.2 26.9 %all-to-all-start.3 = ((bf16[16,264,128]{2,1,0:T(8,128)(2,1)}), bf16[16,264,128]{2,1,0:T(8,128)(2,1)S(1)}, u32[]{:S(2)}, u32[]{:S(2)}) async-start(bf16[16,264,128]{2,1,0:T(8,128)(2,1)} %join.1), calls=%async_computation.3 | async-start | bytes 2162688 | tf_op jit(solution)/shard_map/all_to_all | solution.py:380
  85.5 10.5 %collective-permute-start.12 = (bf16[520,128]{1,0:T(8,128)(2,1)S(1)}, bf16[520,128]{1,0:T(8,128)(2,1)S(1)}, u32[]{:S(2)}, u32[]{:S(2)}) collective-permute-start(bf16[520,128]{1,0:T(8,128)(2,1)S(1)} %get-tuple-element.72), channel_id=1, source_target_pairs={{0,1},{1,2},{2,3},{3,4},{4,5},{5,6},{6,7},{7,0},{8,9},{9,10},{10,1... | collective-permute-start | bytes 399368 | tf_op jit(solution)/shard_map/ppermute | solution.py:386
  86.1 9.9 %collective-permute-start.13 = (bf16[520,128]{1,0:T(8,128)(2,1)S(1)}, bf16[520,128]{1,0:T(8,128)(2,1)S(1)}, u32[]{:S(2)}, u32[]{:S(2)}) collective-permute-start(bf16[520,128]{1,0:T(8,128)(2,1)S(1)} %get-tuple-element.73), channel_id=1, source_target_pairs={{0,2},{1,7},{2,4},{3,1},{4,6},{5,3},{6,0},{7,5},{8,10},{9,15},{10,... | collective-permute-start | bytes 399368 | tf_op jit(solution)/shard_map/ppermute | solution.py:519
  86.5 11.0 %collective-permute-start.15 = (bf16[520,128]{1,0:T(8,128)(2,1)S(1)}, bf16[520,128]{1,0:T(8,128)(2,1)S(1)}, u32[]{:S(2)}, u32[]{:S(2)}) collective-permute-start(bf16[520,128]{1,0:T(8,128)(2,1)S(1)} %get-tuple-element.75), channel_id=1, source_target_pairs={{0,7},{1,0},{2,1},{3,2},{4,3},{5,4},{6,5},{7,6},{8,15},{9,8},{10,9... | collective-permute-start | bytes 399368 | tf_op jit(solution)/shard_map/ppermute | solution.py:386
  88.7 12.8 %collective-permute-start.10 = (bf16[520,128]{1,0:T(8,128)(2,1)S(1)}, bf16[520,128]{1,0:T(8,128)(2,1)S(1)}, u32[]{:S(2)}, u32[]{:S(2)}) collective-permute-start(bf16[520,128]{1,0:T(8,128)(2,1)S(1)} %get-tuple-element.69), channel_id=1, source_target_pairs={{0,1},{1,2},{2,3},{3,4},{4,5},{5,6},{6,7},{7,0},{8,9},{9,10},{10,1... | collective-permute-start | bytes 399368 | tf_op jit(solution)/shard_map/ppermute | solution.py:386
  90.2 11.3 %collective-permute-start.11 = (bf16[520,128]{1,0:T(8,128)(2,1)S(1)}, bf16[520,128]{1,0:T(8,128)(2,1)S(1)}, u32[]{:S(2)}, u32[]{:S(2)}) collective-permute-start(bf16[520,128]{1,0:T(8,128)(2,1)S(1)} %get-tuple-element.70), channel_id=1, source_target_pairs={{0,7},{1,0},{2,1},{3,2},{4,3},{5,4},{6,5},{7,6},{8,15},{9,8},{10,9... | collective-permute-start | bytes 399368 | tf_op jit(solution)/shard_map/ppermute | solution.py:386
  96.6 8.1 %collective-permute-start.14 = (bf16[520,128]{1,0:T(8,128)(2,1)S(1)}, bf16[520,128]{1,0:T(8,128)(2,1)S(1)}, u32[]{:S(2)}, u32[]{:S(2)}) collective-permute-start(bf16[520,128]{1,0:T(8,128)(2,1)S(1)} %relay.2), channel_id=1, source_target_pairs={{0,2},{1,3},{2,4},{3,5},{4,6},{5,7},{6,0},{7,1},{8,10},{9,11},{10,... | collective-permute-start | bytes 399368 | tf_op jit(solution)/shard_map/ppermute | solution.py:386
  98.1 7.1 %collective-permute-start.16 = (bf16[520,128]{1,0:T(8,128)(2,1)S(1)}, bf16[520,128]{1,0:T(8,128)(2,1)S(1)}, u32[]{:S(2)}, u32[]{:S(2)}) collective-permute-start(bf16[520,128]{1,0:T(8,128)(2,1)S(1)} %relay.3), channel_id=1, source_target_pairs={{0,6},{1,7},{2,0},{3,1},{4,2},{5,3},{6,4},{7,5},{8,14},{9,15},{10,... | collective-permute-start | bytes 399368 | tf_op jit(solution)/shard_map/ppermute | solution.py:386

commit v7 on v6

--- a/solution.py
+++ b/solution.py
@@ -518,7 +518,10 @@
 
     over4 = lax.ppermute(gpsi[4], "z", across)
     over3, over5 = move(gpsi[3], 1), move(gpsi[5], 7)
-    psi_parts = [gpsi[0], move(gpsi[1], 1), move(gpsi[7], 7)]
+    over3, over4, over5, up1, down1 = lax.optimization_barrier(
+        (over3, over4, over5, gpsi[1], gpsi[7])
+    )
+    psi_parts = [gpsi[0], move(up1, 1), move(down1, 7)]
     psi_parts.append(move(relay(0, gpsi[2], over3, over4), 2))
     psi_parts.append(move(relay(1, gpsi[6], over5, over4), 6))
 

time: 107 us -> 110 us (1.028)
  waiting for transfers between devices: 26.3 us -> 28.8 us
    ppermute x12, waiting for transfers between devices: 13.7 us -> 16.2 us  [move(): return lax.ppermute(array, 'z', [(i, (i + shift) % nz) for i in range(nz)])]
  transfers between devices with their start and end apart: 21 -> 21, of which waited for: 12 -> 11; matrix products, arithmetic and copies ran while one was open for 0% -> 0% of each run, Pallas kernels for 12% -> 12%
where the time goes in v7:
time: 110 us; the launch traced here: 109 us
  starting transfers between devices  51.9 us (47%)
  waiting for transfers between devices  28.8 us (26%)
  Pallas kernels  27.5 us (25%)
    all_to_all x4, starting transfers between devices, spread(): return lax.all_to_all(array, axes, 0, 0, tiled=True)  25.8 us
    ppermute x12, starting transfers between devices, move(): return lax.ppermute(array, 'z', [(i, (i + shift) % nz) for i in range(nz)])  25.3 us
    ppermute x12, waiting for transfers between devices, move(): return lax.ppermute(array, 'z', [(i, (i + shift) % nz) for i in range(nz)])  16.2 us
    all_to_all x4, waiting for transfers between devices, spread(): return lax.all_to_all(array, axes, 0, 0, tiled=True)  7.39 us
    pallas_call x1, Pallas kernels, shards(): pl.pallas_call(functools.partial(weights_kernel, scale, scale2, shard), o...  7.31 us
    pallas_call x1, Pallas kernels, shards(): pl.pallas_call(functools.partial(cols_kernel, scale2, shard), out_shape=j...  6.49 us
    ppermute x1, waiting for transfers between devices, shards(): near[4] = lax.ppermute(jnp.where(even, near[2], near[6]), 'z', across)  3.63 us
    pallas_call x1, Pallas kernels, shards(): pl.pallas_call(functools.partial(goals_kernel, shard), out_shape=(part,)...  3.06 us
  transfers between devices with their start and end apart: 21, of which 11 were waited for; matrix products, arithmetic and copies ran while one was open for 0% of the time, Pallas kernels for 12%

profile of v7, /device:TPU:8, one launch (start us, length us, event | category | flops | bytes accessed | tf_op | source)
XLA Modules:
  0.0 109.2 jit_solution(15544294037059685652)
XLA Ops:
  0.6 2.0 %pack.1 = bf16[16,264,128]{2,1,0:T(8,128)(2,1)} custom-call(bf16[64,512]{1,0:T(8,128)(2,1)} %phi_in.1, s32[1,64]{1,0:T(1,128)} %bitcast.5), custom_call_target="tpu_custom_call" | custom-call | tf_op jit(solution)/shard_map/pack/pallas_call | solution.py:396
  2.6 0.0 copy-start
  2.6 7.5 %all-to-all-start = ((bf16[16,264,128]{2,1,0:T(8,128)(2,1)}), bf16[16,264,128]{2,1,0:T(8,128)(2,1)S(1)}, u32[]{:S(2)}, u32[]{:S(2)}) async-start(bf16[16,264,128]{2,1,0:T(8,128)(2,1)} %pack.1), calls=%async_computation | async-start | bytes 2162688 | tf_op jit(solution)/shard_map/all_to_all | solution.py:380
  10.1 0.0 copy-done
  10.2 6.4 %collective-permute-start.3 = (bf16[128,512]{1,0:T(8,128)(2,1)S(1)}, bf16[128,512]{1,0:T(8,128)(2,1)S(1)}, u32[]{:S(2)}, u32[]{:S(2)}) collective-permute-start(bf16[128,512]{1,0:T(8,128)(2,1)S(1)} %copy-done), channel_id=1, source_target_pairs={{0,6},{1,7},{2,0},{3,1},{4,2},{5,3},{6,4},{7,5},{8,14},{9,15},{10,... | collective-permute-start | bytes 393224 | tf_op jit(solution)/shard_map/ppermute | solution.py:386
  16.5 0.0 collective-permute-start.1
  16.5 1.0 collective-permute-start
  17.6 2.7 %collective-permute-start.6 = (bf16[128,512]{1,0:T(8,128)(2,1)S(1)}, bf16[128,512]{1,0:T(8,128)(2,1)S(1)}, u32[]{:S(2)}, u32[]{:S(2)}) collective-permute-start(bf16[128,512]{1,0:T(8,128)(2,1)S(1)} %copy-done), channel_id=1, source_target_pairs={{0,7},{1,0},{2,1},{3,2},{4,3},{5,4},{6,5},{7,6},{8,15},{9,8},{10,9... | collective-permute-start | bytes 393224 | tf_op jit(solution)/shard_map/ppermute | solution.py:386
  20.2 2.1 %collective-permute-done.3.refs_6_ = bf16[128,512]{1,0:T(8,128)(2,1)S(1)} collective-permute-done((bf16[128,512]{1,0:T(8,128)(2,1)S(1)}, bf16[128,512]{1,0:T(8,128)(2,1)S(1)}, u32[]{:S(2)}, u32[]{:S(2)}) %collective-permute-start.3) | collective-permute-done | bytes 131104 | tf_op jit(solution)/shard_map/ppermute | solution.py:386
  22.3 2.5 %collective-permute-start.5 = (bf16[128,512]{1,0:T(8,128)(2,1)S(1)}, bf16[128,512]{1,0:T(8,128)(2,1)S(1)}, u32[]{:S(2)}, u32[]{:S(2)}) collective-permute-start(bf16[128,512]{1,0:T(8,128)(2,1)S(1)} %collective-permute-done.3.refs_6_), channel_id=1, source_target_pairs={{0,7},{1,0},{2,1},{3,2},{4,3},{5,4},{6,5},{7,6},{8,15},{9,8},{10,9... | collective-permute-start | bytes 393224 | tf_op jit(solution)/shard_map/ppermute | solution.py:386
  24.8 1.8 %collective-permute-done.1.refs_2_ = bf16[128,512]{1,0:T(8,128)(2,1)S(1)} collective-permute-done((bf16[128,512]{1,0:T(8,128)(2,1)S(1)}, bf16[128,512]{1,0:T(8,128)(2,1)S(1)}, u32[]{:S(2)}, u32[]{:S(2)}) %collective-permute-start.1) | collective-permute-done | bytes 131104 | tf_op jit(solution)/shard_map/ppermute | solution.py:386
  26.6 0.1 collective-permute-start.4
  26.7 2.5 %collective-permute-start.2 = (bf16[128,512]{1,0:T(8,128)(2,1)S(1)}, bf16[128,512]{1,0:T(8,128)(2,1)S(1)}, u32[]{:S(2)}, u32[]{:S(2)}) collective-permute-start(bf16[128,512]{1,0:T(8,128)(2,1)S(1)} %collective-permute-done.1.refs_2_), channel_id=1, source_target_pairs={{0,1},{1,2},{2,3},{3,4},{4,5},{5,6},{6,7},{7,0},{8,9},{9,10},{10,1... | collective-permute-start | bytes 393224 | tf_op jit(solution)/shard_map/ppermute | solution.py:386
  29.2 1.1 collective-permute-done.refs_1_
  30.3 0.0 collective-permute-done.6.refs_7_
  30.3 0.0 collective-permute-done.5.refs_5_
  30.3 3.6 %collective-permute-done.4.refs_4_ = bf16[128,512]{1,0:T(8,128)(2,1)S(1)} collective-permute-done((bf16[128,512]{1,0:T(8,128)(2,1)S(1)}, bf16[128,512]{1,0:T(8,128)(2,1)S(1)}, u32[]{:S(2)}, u32[]{:S(2)}) %collective-permute-start.4) | collective-permute-done | bytes 131104 | tf_op jit(solution)/shard_map/ppermute | solution.py:417
  33.9 0.5 collective-permute-done.2.refs_3_
  34.4 0.0 all-to-all-done.phi_ref.own_ref
  34.4 0.0 collective-permute-start.7
  34.4 0.1 pad_add_fusion.place_ref
  34.5 2.4 %own_rows.1 = (f32[8,128]{1,0:T(8,128)S(1)}, bf16[1024,512]{1,0:T(8,128)(2,1)}, bf16[1024,512]{1,0:T(8,128)(2,1)S(1)}) custom-call(s32[3]{0:T(128)S(1)} %pad_add_fusion.place_ref, bf16[16,264,128]{2,1,0:T(8,128)(2,1)S(1)} %all-to-all-done.phi_ref.own_ref, bf16[128,512]{1,0:T(8,128)(2,1)S(1)} %copy-done, bf16[128,512]{1,0:T(8,128)(2,1)S(1)} %collective-permute-done.refs_1_, ...), custom_call_target="tpu_custom_call" | custom-call | flops 1073741824 | bytes 4194304 | tf_op jit(solution)/shard_map/own_rows/pallas_call | solution.py:435
  36.9 0.2 collective-permute-done.7.phi_ref.other_ref
  37.1 3.0 %all_rows.1 = f32[16,16,128]{2,1,0:T(8,128)} custom-call(s32[3]{0:T(128)S(1)} %pad_add_fusion.place_ref, bf16[16,264,128]{2,1,0:T(8,128)(2,1)S(1)} %collective-permute-done.7.phi_ref.other_ref, f32[8,128]{1,0:T(8,128)S(1)} %get-tuple-element.56.line_ref, bf16[1024,512]{1,0:T(8,128)(2,1)S(1)} %get-tuple-element.57.psi_ref), custom_call_target="tpu_custom_call" | custom-call | flops 1073741824 | bytes 4194304 | tf_op jit(solution)/shard_map/all_rows/pallas_call | solution.py:450
  40.2 7.1 %all-to-all-start.1 = ((f32[16,16,128]{2,1,0:T(8,128)}), f32[16,16,128]{2,1,0:T(8,128)S(1)}, u32[]{:S(2)}, u32[]{:S(2)}) async-start(f32[16,16,128]{2,1,0:T(8,128)} %all_rows.1), calls=%async_computation.1 | async-start | bytes 262144 | tf_op jit(solution)/shard_map/all_to_all | solution.py:380
  47.3 6.5 %cols.1 = f32[8,24,128]{2,1,0:T(8,128)} custom-call(s32[3]{0:T(128)S(1)} %pad_add_fusion.place_ref, bf16[16,264,128]{2,1,0:T(8,128)(2,1)S(1)} %all-to-all-done.phi_ref.own_ref, bf16[16,264,128]{2,1,0:T(8,128)(2,1)S(1)} %collective-permute-done.7.phi_ref.other_ref, bf16[1024,512]{1,0:T(8,128)(2,1)} %get-tuple-element.55.psi_in), custom_call_target="tpu_custom_call" | custom-call | flops 2147483648 | bytes 4194304 | tf_op jit(solution)/shard_map/cols/pallas_call | solution.py:461
  53.8 0.0 all-to-all-done.1.rows_ref
  53.8 3.9 %all-to-all-start.2 = ((f32[8,24,128]{2,1,0:T(8,128)}), f32[8,24,128]{2,1,0:T(8,128)S(1)}, u32[]{:S(2)}, u32[]{:S(2)}) async-start(f32[8,24,128]{2,1,0:T(8,128)} %cols.1), calls=%async_computation.2 | async-start | bytes 196608 | tf_op jit(solution)/shard_map/all_to_all | solution.py:380
  57.7 0.0 collective-permute-start.8
  57.7 1.3 %collective-permute-done.8.others_ref = f32[16,16,128]{2,1,0:T(8,128)S(1)} collective-permute-done((f32[16,16,128]{2,1,0:T(8,128)S(1)}, f32[16,16,128]{2,1,0:T(8,128)S(1)}, u32[]{:S(2)}, u32[]{:S(2)}) %collective-permute-start.8) | collective-permute-done | bytes 131104 | tf_op jit(solution)/shard_map/ppermute | solution.py:383
  59.0 7.4 %all-to-all-done.2.refs_0_ = f32[8,24,128]{2,1,0:T(8,128)S(1)} async-done(((f32[8,24,128]{2,1,0:T(8,128)}), f32[8,24,128]{2,1,0:T(8,128)S(1)}, u32[]{:S(2)}, u32[]{:S(2)}) %all-to-all-start.2) | async-done | bytes 98336 | tf_op jit(solution)/shard_map/all_to_all | solution.py:380
  66.4 7.3 %weights.1 = (bf16[16,264,128]{2,1,0:T(8,128)(2,1)S(1)}, bf16[16,264,128]{2,1,0:T(8,128)(2,1)S(1)}, bf16[2048,1024]{1,0:T(8,128)(2,1)S(1)}, bf16[8,128]{1,0:T(8,128)(2,1)S(1)}) custom-call(s32[3]{0:T(128)S(1)} %pad_add_fusion.place_ref, bf16[16,264,128]{2,1,0:T(8,128)(2,1)S(1)} %all-to-all-done.phi_ref.own_ref, ...), custom_call_target="tpu_custom_call" | custom-call | flops 4294967296 | bytes 4194304 | tf_op jit(solution)/shard_map/weights/pallas_call | solution.py:475
  73.7 0.3 collective-permute-start.9
  74.0 3.1 %goals.1 = (bf16[520,128]{1,0:T(8,128)(2,1)S(1)}, bf16[520,128]{1,0:T(8,128)(2,1)S(1)}, bf16[520,128]{1,0:T(8,128)(2,1)S(1)}, bf16[520,128]{1,0:T(8,128)(2,1)S(1...) custom-call(s32[3]{0:T(128)S(1)} %pad_add_fusion.place_ref, ...), custom_call_target="tpu_custom_call" | custom-call | flops 2147483648 | bytes 4194304 | tf_op jit(solution)/shard_map/goals/pallas_call | solution.py:486
  77.1 0.0 collective-permute-done.9.other_ref
  77.1 1.1 %join.1 = bf16[16,264,128]{2,1,0:T(8,128)(2,1)} custom-call(bf16[16,264,128]{2,1,0:T(8,128)(2,1)S(1)} %get-tuple-element.60.own_ref, bf16[16,264,128]{2,1,0:T(8,128)(2,1)S(1)} %collective-permute-done.9.other_ref), custom_call_target="tpu_custom_call" | custom-call | tf_op jit(solution)/shard_map/join/pallas_call | solution.py:498
  78.2 7.2 %all-to-all-start.3 = ((bf16[16,264,128]{2,1,0:T(8,128)(2,1)}), bf16[16,264,128]{2,1,0:T(8,128)(2,1)S(1)}, u32[]{:S(2)}, u32[]{:S(2)}) async-start(bf16[16,264,128]{2,1,0:T(8,128)(2,1)} %join.1), calls=%async_computation.3 | async-start | bytes 2162688 | tf_op jit(solution)/shard_map/all_to_all | solution.py:380
  85.5 0.6 collective-permute-start.10
  86.1 0.4 collective-permute-start.11
  86.5 2.2 %collective-permute-start.12 = (bf16[520,128]{1,0:T(8,128)(2,1)S(1)}, bf16[520,128]{1,0:T(8,128)(2,1)S(1)}, u32[]{:S(2)}, u32[]{:S(2)}) collective-permute-start(bf16[520,128]{1,0:T(8,128)(2,1)S(1)} %get-tuple-element.76), channel_id=1, source_target_pairs={{0,7},{1,0},{2,1},{3,2},{4,3},{5,4},{6,5},{7,6},{8,15},{9,8},{10,9... | collective-permute-start | bytes 399368 | tf_op jit(solution)/shard_map/ppermute | solution.py:386
  88.7 6.2 %collective-permute-done.10.refs_1_ = bf16[520,128]{1,0:T(8,128)(2,1)S(1)} collective-permute-done((bf16[520,128]{1,0:T(8,128)(2,1)S(1)}, bf16[520,128]{1,0:T(8,128)(2,1)S(1)}, u32[]{:S(2)}, u32[]{:S(2)}) %collective-permute-start.10) | collective-permute-done | bytes 133152 | tf_op jit(solution)/shard_map/ppermute | solution.py:386
  94.9 0.0 collective-permute-done.11.refs_2_
  94.9 1.2 %collective-permute-done.12.refs_1_ = bf16[520,128]{1,0:T(8,128)(2,1)S(1)} collective-permute-done((bf16[520,128]{1,0:T(8,128)(2,1)S(1)}, bf16[520,128]{1,0:T(8,128)(2,1)S(1)}, u32[]{:S(2)}, u32[]{:S(2)}) %collective-permute-start.12) | collective-permute-done | bytes 133152 | tf_op jit(solution)/shard_map/ppermute | solution.py:386
  96.2 0.0 collective-permute-start.13
  96.2 3.2 %collective-permute-start.14 = (bf16[520,128]{1,0:T(8,128)(2,1)S(1)}, bf16[520,128]{1,0:T(8,128)(2,1)S(1)}, u32[]{:S(2)}, u32[]{:S(2)}) collective-permute-start(bf16[520,128]{1,0:T(8,128)(2,1)S(1)} %get-tuple-element.80), channel_id=1, source_target_pairs={{0,7},{1,0},{2,1},{3,2},{4,3},{5,4},{6,5},{7,6},{8,15},{9,8},{10,9... | collective-permute-start | bytes 399368 | tf_op jit(solution)/shard_map/ppermute | solution.py:386
  99.4 0.6 relay.2
  100.0 0.1 collective-permute-start.15
  100.1 0.6 relay.3
  100.8 4.2 %collective-permute-start.16 = (bf16[520,128]{1,0:T(8,128)(2,1)S(1)}, bf16[520,128]{1,0:T(8,128)(2,1)S(1)}, u32[]{:S(2)}, u32[]{:S(2)}) collective-permute-start(bf16[520,128]{1,0:T(8,128)(2,1)S(1)} %relay.3), channel_id=1, source_target_pairs={{0,6},{1,7},{2,0},{3,1},{4,2},{5,3},{6,4},{7,5},{8,14},{9,15},{10,... | collective-permute-start | bytes 399368 | tf_op jit(solution)/shard_map/ppermute | solution.py:386
  105.0 0.0 collective-permute-done.13.refs_1_
  105.0 0.0 collective-permute-done.14.refs_2_
  105.0 3.3 %collective-permute-done.15.refs_3_ = bf16[520,128]{1,0:T(8,128)(2,1)S(1)} collective-permute-done((bf16[520,128]{1,0:T(8,128)(2,1)S(1)}, bf16[520,128]{1,0:T(8,128)(2,1)S(1)}, u32[]{:S(2)}, u32[]{:S(2)}) %collective-permute-start.15) | collective-permute-done | bytes 133152 | tf_op jit(solution)/shard_map/ppermute | solution.py:386
  108.3 0.0 collective-permute-done.16.refs_4_
  108.3 0.0 all-to-all-done.3.phi_parts_ref
  108.3 0.9 totals.1
  (1 shorter events, 0.0 us)
Async XLA Ops:
  2.6 7.6 %copy-start = (bf16[128,512]{1,0:T(8,128)(2,1)S(1)}, bf16[128,512]{1,0:T(8,128)(2,1)}, u32[]{:S(2)}) copy-start(bf16[128,512]{1,0:T(8,128)(2,1)} %refs_0_) | copy-start | bytes 393220
  2.6 31.8 %all-to-all-start = ((bf16[16,264,128]{2,1,0:T(8,128)(2,1)}), bf16[16,264,128]{2,1,0:T(8,128)(2,1)S(1)}, u32[]{:S(2)}, u32[]{:S(2)}) async-start(bf16[16,264,128]{2,1,0:T(8,128)(2,1)} %pack.1), calls=%async_computation | async-start | bytes 2162688 | tf_op jit(solution)/shard_map/all_to_all | solution.py:380
  10.2 12.2 %collective-permute-start.3 = (bf16[128,512]{1,0:T(8,128)(2,1)S(1)}, bf16[128,512]{1,0:T(8,128)(2,1)S(1)}, u32[]{:S(2)}, u32[]{:S(2)}) collective-permute-start(bf16[128,512]{1,0:T(8,128)(2,1)S(1)} %copy-done), channel_id=1, source_target_pairs={{0,6},{1,7},{2,0},{3,1},{4,2},{5,3},{6,4},{7,5},{8,14},{9,15},{10,... | collective-permute-start | bytes 393224 | tf_op jit(solution)/shard_map/ppermute | solution.py:386
  16.5 10.1 %collective-permute-start.1 = (bf16[128,512]{1,0:T(8,128)(2,1)S(1)}, bf16[128,512]{1,0:T(8,128)(2,1)S(1)}, u32[]{:S(2)}, u32[]{:S(2)}) collective-permute-start(bf16[128,512]{1,0:T(8,128)(2,1)S(1)} %copy-done), channel_id=1, source_target_pairs={{0,2},{1,3},{2,4},{3,5},{4,6},{5,7},{6,0},{7,1},{8,10},{9,11},{10,... | collective-permute-start | bytes 393224 | tf_op jit(solution)/shard_map/ppermute | solution.py:386
  16.5 13.7 %collective-permute-start = (bf16[128,512]{1,0:T(8,128)(2,1)S(1)}, bf16[128,512]{1,0:T(8,128)(2,1)S(1)}, u32[]{:S(2)}, u32[]{:S(2)}) collective-permute-start(bf16[128,512]{1,0:T(8,128)(2,1)S(1)} %copy-done), channel_id=1, source_target_pairs={{0,1},{1,2},{2,3},{3,4},{4,5},{5,6},{6,7},{7,0},{8,9},{9,10},{10,1... | collective-permute-start | bytes 393224 | tf_op jit(solution)/shard_map/ppermute | solution.py:386
  17.6 12.7 %collective-permute-start.6 = (bf16[128,512]{1,0:T(8,128)(2,1)S(1)}, bf16[128,512]{1,0:T(8,128)(2,1)S(1)}, u32[]{:S(2)}, u32[]{:S(2)}) collective-permute-start(bf16[128,512]{1,0:T(8,128)(2,1)S(1)} %copy-done), channel_id=1, source_target_pairs={{0,7},{1,0},{2,1},{3,2},{4,3},{5,4},{6,5},{7,6},{8,15},{9,8},{10,9... | collective-permute-start | bytes 393224 | tf_op jit(solution)/shard_map/ppermute | solution.py:386
  22.3 7.9 %collective-permute-start.5 = (bf16[128,512]{1,0:T(8,128)(2,1)S(1)}, bf16[128,512]{1,0:T(8,128)(2,1)S(1)}, u32[]{:S(2)}, u32[]{:S(2)}) collective-permute-start(bf16[128,512]{1,0:T(8,128)(2,1)S(1)} %collective-permute-done.3.refs_6_), channel_id=1, source_target_pairs={{0,7},{1,0},{2,1},{3,2},{4,3},{5,4},{6,5},{7,6},{8,15},{9,8},{10,9... | collective-permute-start | bytes 393224 | tf_op jit(solution)/shard_map/ppermute | solution.py:386
  26.6 7.3 %collective-permute-start.4 = (bf16[128,512]{1,0:T(8,128)(2,1)S(1)}, bf16[128,512]{1,0:T(8,128)(2,1)S(1)}, u32[]{:S(2)}, u32[]{:S(2)}) collective-permute-start(bf16[128,512]{1,0:T(8,128)(2,1)S(1)} %broadcast_select_fusion), channel_id=1, source_target_pairs={{0,2},{1,7},{2,4},{3,1},{4,6},{5,3},{6,0},{7,5},{8,10},{9,15},{10,... | collective-permute-start | bytes 393224 | tf_op jit(solution)/shard_map/ppermute | solution.py:417
  26.7 7.7 %collective-permute-start.2 = (bf16[128,512]{1,0:T(8,128)(2,1)S(1)}, bf16[128,512]{1,0:T(8,128)(2,1)S(1)}, u32[]{:S(2)}, u32[]{:S(2)}) collective-permute-start(bf16[128,512]{1,0:T(8,128)(2,1)S(1)} %collective-permute-done.1.refs_2_), channel_id=1, source_target_pairs={{0,1},{1,2},{2,3},{3,4},{4,5},{5,6},{6,7},{7,0},{8,9},{9,10},{10,1... | collective-permute-start | bytes 393224 | tf_op jit(solution)/shard_map/ppermute | solution.py:386
  34.4 2.7 %collective-permute-start.7 = (bf16[16,264,128]{2,1,0:T(8,128)(2,1)S(1)}, bf16[16,264,128]{2,1,0:T(8,128)(2,1)S(1)}, u32[]{:S(2)}, u32[]{:S(2)}) collective-permute-start(bf16[16,264,128]{2,1,0:T(8,128)(2,1)S(1)} %all-to-all-done.phi_ref.own_ref), channel_id=1, source_target_pairs={{0,32},{32,0},{1,33},{33,1},{2,34},{34,2},{3,35},{35,3},{4,36},{36... | collective-permute-start | bytes 3244040 | tf_op jit(solution)/shard_map/ppermute | solution.py:383
  40.2 13.6 %all-to-all-start.1 = ((f32[16,16,128]{2,1,0:T(8,128)}), f32[16,16,128]{2,1,0:T(8,128)S(1)}, u32[]{:S(2)}, u32[]{:S(2)}) async-start(f32[16,16,128]{2,1,0:T(8,128)} %all_rows.1), calls=%async_computation.1 | async-start | bytes 262144 | tf_op jit(solution)/shard_map/all_to_all | solution.py:380
  53.8 12.6 %all-to-all-start.2 = ((f32[8,24,128]{2,1,0:T(8,128)}), f32[8,24,128]{2,1,0:T(8,128)S(1)}, u32[]{:S(2)}, u32[]{:S(2)}) async-start(f32[8,24,128]{2,1,0:T(8,128)} %cols.1), calls=%async_computation.2 | async-start | bytes 196608 | tf_op jit(solution)/shard_map/all_to_all | solution.py:380
  57.7 1.3 %collective-permute-start.8 = (f32[16,16,128]{2,1,0:T(8,128)S(1)}, f32[16,16,128]{2,1,0:T(8,128)S(1)}, u32[]{:S(2)}, u32[]{:S(2)}) collective-permute-start(f32[16,16,128]{2,1,0:T(8,128)S(1)} %all-to-all-done.1.rows_ref), channel_id=1, source_target_pairs={{0,32},{32,0},{1,33},{33,1},{2,34},{34,2},{3,35},{35,3},{4,36},{36... | collective-permute-start | bytes 393224 | tf_op jit(solution)/shard_map/ppermute | solution.py:383
  73.7 3.4 %collective-permute-start.9 = (bf16[16,264,128]{2,1,0:T(8,128)(2,1)S(1)}, bf16[16,264,128]{2,1,0:T(8,128)(2,1)S(1)}, u32[]{:S(2)}, u32[]{:S(2)}) collective-permute-start(bf16[16,264,128]{2,1,0:T(8,128)(2,1)S(1)} %get-tuple-element.61), channel_id=1, source_target_pairs={{0,32},{32,0},{1,33},{33,1},{2,34},{34,2},{3,35},{35,3},{4,36},{36... | collective-permute-start | bytes 3244040 | tf_op jit(solution)/shard_map/ppermute | solution.py:383
  78.2 30.0 %all-to-all-start.3 = ((bf16[16,264,128]{2,1,0:T(8,128)(2,1)}), bf16[16,264,128]{2,1,0:T(8,128)(2,1)S(1)}, u32[]{:S(2)}, u32[]{:S(2)}) async-start(bf16[16,264,128]{2,1,0:T(8,128)(2,1)} %join.1), calls=%async_computation.3 | async-start | bytes 2162688 | tf_op jit(solution)/shard_map/all_to_all | solution.py:380
  85.5 9.4 %collective-permute-start.10 = (bf16[520,128]{1,0:T(8,128)(2,1)S(1)}, bf16[520,128]{1,0:T(8,128)(2,1)S(1)}, u32[]{:S(2)}, u32[]{:S(2)}) collective-permute-start(bf16[520,128]{1,0:T(8,128)(2,1)S(1)} %get-tuple-element.74), channel_id=1, source_target_pairs={{0,1},{1,2},{2,3},{3,4},{4,5},{5,6},{6,7},{7,0},{8,9},{9,10},{10,1... | collective-permute-start | bytes 399368 | tf_op jit(solution)/shard_map/ppermute | solution.py:386
  86.1 8.9 %collective-permute-start.11 = (bf16[520,128]{1,0:T(8,128)(2,1)S(1)}, bf16[520,128]{1,0:T(8,128)(2,1)S(1)}, u32[]{:S(2)}, u32[]{:S(2)}) collective-permute-start(bf16[520,128]{1,0:T(8,128)(2,1)S(1)} %get-tuple-element.75), channel_id=1, source_target_pairs={{0,2},{1,7},{2,4},{3,1},{4,6},{5,3},{6,0},{7,5},{8,10},{9,15},{10,... | collective-permute-start | bytes 399368 | tf_op jit(solution)/shard_map/ppermute | solution.py:519
  86.5 9.7 %collective-permute-start.12 = (bf16[520,128]{1,0:T(8,128)(2,1)S(1)}, bf16[520,128]{1,0:T(8,128)(2,1)S(1)}, u32[]{:S(2)}, u32[]{:S(2)}) collective-permute-start(bf16[520,128]{1,0:T(8,128)(2,1)S(1)} %get-tuple-element.76), channel_id=1, source_target_pairs={{0,7},{1,0},{2,1},{3,2},{4,3},{5,4},{6,5},{7,6},{8,15},{9,8},{10,9... | collective-permute-start | bytes 399368 | tf_op jit(solution)/shard_map/ppermute | solution.py:386
  96.2 8.8 %collective-permute-start.13 = (bf16[520,128]{1,0:T(8,128)(2,1)S(1)}, bf16[520,128]{1,0:T(8,128)(2,1)S(1)}, u32[]{:S(2)}, u32[]{:S(2)}) collective-permute-start(bf16[520,128]{1,0:T(8,128)(2,1)S(1)} %get-tuple-element.79), channel_id=1, source_target_pairs={{0,1},{1,2},{2,3},{3,4},{4,5},{5,6},{6,7},{7,0},{8,9},{9,10},{10,1... | collective-permute-start | bytes 399368 | tf_op jit(solution)/shard_map/ppermute | solution.py:386
  96.2 8.8 %collective-permute-start.14 = (bf16[520,128]{1,0:T(8,128)(2,1)S(1)}, bf16[520,128]{1,0:T(8,128)(2,1)S(1)}, u32[]{:S(2)}, u32[]{:S(2)}) collective-permute-start(bf16[520,128]{1,0:T(8,128)(2,1)S(1)} %get-tuple-element.80), channel_id=1, source_target_pairs={{0,7},{1,0},{2,1},{3,2},{4,3},{5,4},{6,5},{7,6},{8,15},{9,8},{10,9... | collective-permute-start | bytes 399368 | tf_op jit(solution)/shard_map/ppermute | solution.py:386
  100.0 8.2 %collective-permute-start.15 = (bf16[520,128]{1,0:T(8,128)(2,1)S(1)}, bf16[520,128]{1,0:T(8,128)(2,1)S(1)}, u32[]{:S(2)}, u32[]{:S(2)}) collective-permute-start(bf16[520,128]{1,0:T(8,128)(2,1)S(1)} %relay.2), channel_id=1, source_target_pairs={{0,2},{1,3},{2,4},{3,5},{4,6},{5,7},{6,0},{7,1},{8,10},{9,11},{10,... | collective-permute-start | bytes 399368 | tf_op jit(solution)/shard_map/ppermute | solution.py:386
  100.8 7.5 %collective-permute-start.16 = (bf16[520,128]{1,0:T(8,128)(2,1)S(1)}, bf16[520,128]{1,0:T(8,128)(2,1)S(1)}, u32[]{:S(2)}, u32[]{:S(2)}) collective-permute-start(bf16[520,128]{1,0:T(8,128)(2,1)S(1)} %relay.3), channel_id=1, source_target_pairs={{0,6},{1,7},{2,0},{3,1},{4,2},{5,3},{6,4},{7,5},{8,14},{9,15},{10,... | collective-permute-start | bytes 399368 | tf_op jit(solution)/shard_map/ppermute | solution.py:386
